TPU v7x, 128 devices: a whole 4x4x4 slice. The times are simulated.
128 devices in a mesh: row: 8 (over x, core), col: 16 (over z, y).
Axes of the slice: x: 4, y: 4, z: 4, core: 2. Of those that a mesh axis runs over, the one named last changes fastest.
Arguments:
- panel_block: float32 [18432, 128], P(('row', 'col')), may hold values from -160 to 160
- trailing: float32 [18432, 18432], P('row', 'col'), may hold values from -4 to 4
Outputs:
- upper_factor: float32 [128, 128], replicated
- updated: float32 [18432, 18432], P('row', 'col')
All inputs are finite; a program needn't handle non-finite values.
Results may differ from a plain program's by a relative error of at most 0.00011.
Values sent between devices are 32-bit elements; how exact they have to be, the bound alone decides.
No kernel may reach another device: no remote copies, remote signals or barrier semaphores. Data moves between devices by JAX's collectives and lax.ppermute only.
A program may use at most 128 MiB of HBM per device.

v0:
```python
import jax
import jax.numpy as jnp
from jax import lax
from jax.sharding import PartitionSpec as P

precise = lax.Precision.HIGHEST


def product(left_side, right_side):
    return jnp.dot(left_side, right_side, precision=precise, preferred_element_type=jnp.float32)


def transpose_inverse(square):
    normal_matrix = product(square.T, square)
    lower_chol = jnp.linalg.cholesky(normal_matrix)
    factor_t = jax.scipy.linalg.cho_solve((lower_chol, True), square.T)
    return factor_t.T


def shards(panel_block, trailing):
    shard_rows, panel_width = panel_block.shape
    rows_here, cols_here = trailing.shape
    col_count = lax.axis_size("col")
    row_index = lax.axis_index("row")
    col_index = lax.axis_index("col")
    first_row = (row_index * col_count + col_index) * shard_rows
    global_rows = first_row + lax.iota(jnp.int32, shard_rows)[:, None]
    top_mask = (global_rows == lax.iota(jnp.int32, panel_width)[None, :]).astype(jnp.float32)
    gram_block, top_rows = lax.psum(
        (product(panel_block.T, panel_block), product(top_mask.T, panel_block)), ("row", "col")
    )
    upper_factor = jnp.linalg.cholesky(gram_block).T
    basis_rows = jax.scipy.linalg.solve_triangular(upper_factor.T, panel_block.T, lower=True).T
    shifted = basis_rows + top_mask
    top_shifted = jax.scipy.linalg.solve_triangular(
        upper_factor.T, top_rows.T, lower=True
    ).T + jnp.eye(panel_width, dtype=jnp.float32)
    factor = transpose_inverse(top_shifted)
    every_rows = lax.all_gather(shifted, ("row", "col"), axis=0, tiled=True)
    x_rows = lax.dynamic_slice_in_dim(every_rows, row_index * rows_here, rows_here, 0)
    x_cols = lax.dynamic_slice_in_dim(every_rows, col_index * cols_here, cols_here, 0)
    image_rows = lax.psum(product(trailing, x_cols), "col")
    inner_block = lax.psum(product(x_rows.T, image_rows), "row")
    core_block = product(product(factor.T, inner_block), factor)
    w_rows = product(image_rows, factor) - 0.5 * product(x_rows, core_block)
    w_every = lax.all_gather(w_rows, "row", axis=0, tiled=True)
    w_cols = lax.dynamic_slice_in_dim(w_every, col_index * cols_here, cols_here, 0)
    left_side = jnp.concatenate([x_rows, w_rows], axis=1)
    right_side = jnp.concatenate([w_cols, x_cols], axis=1)
    updated = trailing - product(left_side, right_side.T)
    return (upper_factor, updated)


def solution(mesh):
    return jax.shard_map(
        shards,
        mesh=mesh,
        in_specs=(P(("row", "col"), None), P("row", "col")),
        out_specs=(P(), P("row", "col")),
        check_vma=False,
    )
```

profile of v0, /device:TPU:1, one launch (start us, length us, event | category | flops | bytes accessed | tf_op | source)
XLA Modules:
  0.0 494.2 jit_solution(5422940148727398810)
XLA Ops:
  7.2 0.0 copy-start
  7.2 0.0 all-reduce.9.cloned.1.call-start
  7.2 0.8 copy-done
  8.1 1.1 fusion.27
  9.1 1.0 convolution_bitcast_fusion.2
  10.1 0.0 all-reduce.9.cloned.1.call-update
  10.2 0.0 all-gather.3.cloned.1.call-start
  10.2 146.9 %all-reduce.9.cloned.1.call-done = (f32[128,128]{0,1:T(8,128)}, f32[128,128]{0,1:T(8,128)}) async-done(((f32[128,128]{0,1:T(8,128)}, f32[128,128]{0,1:T(8,128)}), (f32[128,128]{0,1:T(8,128)}, f32[128,128]{0,1:T(8,128)})) %all-reduce.9.cloned.1.call-update) | async-done | bytes 131088 | tf_op jit(solution)/shard_map/psum | solution.py:29
  157.1 0.9 copy.5
  158.0 0.9 fusion.18
  158.9 11.7 %cholesky.44 = f32[128,128]{1,0:T(8,128)S(1)} custom-call(f32[128,128]{1,0:T(8,128)S(1)} %fusion.18), custom_call_target="Cholesky" | custom-call | tf_op jit(solution)/shard_map/jit(cholesky)/cholesky | solution.py:32
  170.6 0.6 compare_reduce_fusion.1
  171.3 0.7 fusion.20
  171.9 9.8 %custom-call.13 = f32[1,128,128]{1,2,0:T(8,128)S(1)} custom-call(f32[1,128,128]{2,1,0:T(8,128)S(1)} %get-tuple-element.8), custom_call_target="InvertDiagBlocksLowerTriangular" | custom-call | tf_op jit(solution)/shard_map/jit(_solve_triangular)/triangular_solve | solution.py:33
  181.7 0.8 fusion.7
  182.6 0.0 all-gather.3.cloned.1.call-update
  182.6 0.2 all-reduce.5.cloned.1.call-start
  182.9 1.1 fusion.15
  184.0 0.3 fusion.14
  184.3 0.1 copy.6
  184.4 11.7 %cholesky.55 = f32[128,128]{1,0:T(8,128)S(1)} custom-call(f32[128,128]{1,0:T(8,128)S(1)} %fusion.13), custom_call_target="Cholesky" | custom-call | tf_op jit(solution)/shard_map/jit(cholesky)/cholesky | solution.py:15
  196.1 55.7 %all-gather.3.cloned.1.call-done = f32[18432,128]{1,0:T(8,128)} async-done(((f32[144,128]{1,0:T(8,128)}), f32[18432,128]{1,0:T(8,128)}) %all-gather.3.cloned.1.call-update) | async-done | bytes 9437200 | tf_op jit(solution)/shard_map/all_gather | solution.py:39
  251.8 1.1 constant_dynamic-slice_fusion.1
  252.9 16.4 %convolution_bitcast_fusion = f32[2304,128]{0,1:T(8,128)} fusion(f32[1152,128]{1,0:T(8,128)S(1)} %constant_dynamic-slice_fusion.1, f32[2304,1152]{1,0:T(8,128)} %param.6), kind=kOutput, calls=%fused_computation.3 | convolution fusion | flops 4076863488 | bytes 12386304 | tf_op jit(solution)/shard_map/dot_general | solution.py:10
  269.3 0.0 all-reduce.5.cloned.1.call-update
  269.3 0.0 all-reduce.7.cloned.1.call-start
  269.4 0.6 compare_reduce_fusion
  270.1 0.7 fusion.8
  270.7 9.8 %custom-call.14 = f32[1,128,128]{1,2,0:T(8,128)S(1)} custom-call(f32[1,128,128]{2,1,0:T(8,128)S(1)} %fusion.8), custom_call_target="InvertDiagBlocksLowerTriangular" | custom-call | tf_op jit(solution)/shard_map/jit(_cho_solve)/triangular_solve | solution.py:16
  280.6 0.3 fusion.9
  280.8 0.2 fusion.11
  281.1 1.4 constant_dynamic-slice_fusion.2
  282.4 69.9 %all-reduce.5.cloned.1.call-done = f32[2304,128]{0,1:T(8,128)} async-done(((f32[2304,128]{0,1:T(8,128)}), f32[2304,128]{0,1:T(8,128)}) %all-reduce.5.cloned.1.call-update) | async-done | bytes 1179664 | tf_op jit(solution)/shard_map/psum | solution.py:42
  352.3 4.0 fusion.29
  356.3 0.0 all-reduce.7.cloned.1.call-update
  356.3 0.3 all-gather.5.cloned.1.call-start
  356.6 3.3 fusion.28
  359.9 53.6 %all-reduce.7.cloned.1.call-done = f32[128,128]{1,0:T(8,128)} async-done(((f32[128,128]{1,0:T(8,128)}), f32[128,128]{1,0:T(8,128)}) %all-reduce.7.cloned.1.call-update) | async-done | bytes 65552 | tf_op jit(solution)/shard_map/psum | solution.py:43
  413.5 1.0 fusion.30
  414.6 0.3 fusion.31
  414.8 2.1 fusion
  417.0 0.0 copy-start.1
  417.0 0.0 all-gather.5.cloned.1.call-update
  417.0 0.7 copy.9
  417.7 55.0 %all-gather.5.cloned.1.call-done = f32[18432,128]{1,0:T(8,128)} async-done(((f32[2304,128]{1,0:T(8,128)}), f32[18432,128]{1,0:T(8,128)}) %all-gather.5.cloned.1.call-update) | async-done | bytes 9437200 | tf_op jit(solution)/shard_map/all_gather | solution.py:46
  472.8 1.1 constant_dynamic-slice_fusion
  473.9 0.0 copy-done.1
  473.9 13.8 %convolution_subtract_fusion = f32[2304,1152]{1,0:T(8,128)} fusion(f32[2304,1152]{1,0:T(8,128)} %param.6, f32[2304,128]{1,0:T(8,128)S(1)} %copy-done.1, f32[2304,128]{1,0:T(8,128)S(1)} %constant_dynamic-slice_fusion.2, f32[1152,128]{1,0:T(8,128)S(1)} %constant_dynamic-slice_fusion.1, f32[1152,128]{1,0:T(8,128)S(1)} %constant_dynamic-slice_fusion), kind=kOutput, calls=%fused_computation | convolution fusion | flops 8157265920 | bytes 24772608 | tf_op jit(solution)/shard_map/dot_general | solution.py:10
  (4 shorter events, 0.1 us)
Async XLA Ops:
  7.2 0.9 copy-start
  7.2 149.9 %all-reduce.9.cloned.1.call-start = ((), (), s32[]{:S(2)}) async-start(), calls=%async_computation.4 | async-start | bytes 262144 | tf_op jit(solution)/shard_map/psum | solution.py:29
  10.2 241.6 %all-gather.3.cloned.1.call-start = ((), (), s32[]{:S(2)}) async-start(), calls=%async_computation | async-start | bytes 9510912 | tf_op jit(solution)/shard_map/all_gather | solution.py:39
  182.6 169.7 %all-reduce.5.cloned.1.call-start = ((), (), s32[]{:S(2)}) async-start(), calls=%async_computation.1 | async-start | bytes 2359296 | tf_op jit(solution)/shard_map/psum | solution.py:42
  269.3 144.2 %all-reduce.7.cloned.1.call-start = ((), (), s32[]{:S(2)}) async-start(), calls=%async_computation.2 | async-start | bytes 131072 | tf_op jit(solution)/shard_map/psum | solution.py:43
  356.3 116.5 %all-gather.5.cloned.1.call-start = ((), (), s32[]{:S(2)}) async-start(), calls=%async_computation.3 | async-start | bytes 10616832 | tf_op jit(solution)/shard_map/all_gather | solution.py:46
  417.0 56.9 %copy-start.1 = (f32[2304,128]{1,0:T(8,128)S(1)}, f32[2304,128]{1,0:T(8,128)}, u32[]{:S(2)}) copy-start(f32[2304,128]{1,0:T(8,128)} %fusion) | copy-start | bytes 3538948
Sparse Core Ops, SparseCore 0:
  13.5 143.5 all-reduce.8
  182.7 68.9 all-gather.2
  269.5 82.7 all-reduce.4
  356.4 57.0 all-reduce.6
  417.1 55.6 all-gather.4
where the time goes:
time: 495 us; the launch traced here: 494 us
  waiting for transfers between devices  381 us (77%)
  other arithmetic  46.6 us (9%)
  matrix products  45.8 us (9%)
  between operations  13.9 us (3%)
  local copies, waits for them, and re-layouts  6.13 us (1%)
    psum x1, waiting for transfers between devices, shards(): lax.psum((product(panel_block.T, panel_block), product(top_mask.T, panel_...  147 us
    psum x1, waiting for transfers between devices, shards(): image_rows = lax.psum(product(trailing, x_cols), 'col')  69.9 us
    all_gather x1, waiting for transfers between devices, shards(): every_rows = lax.all_gather(shifted, ('row', 'col'), axis=0, tiled=True)  55.7 us
    all_gather x1, waiting for transfers between devices, shards(): w_every = lax.all_gather(w_rows, 'row', axis=0, tiled=True)  55 us
    psum x1, waiting for transfers between devices, shards(): inner_block = lax.psum(product(x_rows.T, image_rows), 'row')  53.6 us
    dot_general x10, matrix products, product(): jnp.dot(left_side, right_side, precision=precise, preferred_element_type=...  43.3 us
    another operation x3, other arithmetic, shards(): upper_factor = jnp.linalg.cholesky(gram_block).T  12.4 us
    another operation x3, other arithmetic, transpose_inverse(): lower_chol = jnp.linalg.cholesky(normal_matrix)  12.4 us
  transfers between devices with their start and end apart: 5, of which 5 were waited for; matrix products, arithmetic and copies ran while one was open for 6% of the time, Pallas kernels for 0%

commit v1 on v0

v1 whole, which is shorter than its diff:
```python
import jax
import jax.numpy as jnp
from jax import lax
from jax.experimental import pallas as pl
from jax.experimental.pallas import tpu as pltpu
from jax.sharding import PartitionSpec as P

F32 = jnp.float32
BF16 = jnp.bfloat16
AXES = ("row", "col")
PIECE = 144
WIDTH = 128
ROWS = 16 * PIECE
COLS = 8 * PIECE
TALL = 256
STEPS = ROWS // TALL
VMEM = pl.BlockSpec(memory_space=pltpu.VMEM)
SMEM = pl.BlockSpec(memory_space=pltpu.SMEM)


def pairs(where):
    result = []
    for x in range(4):
        for core in range(2):
            for z in range(4):
                for y in range(4):
                    tx, tcore, tz, ty = where(x, core, z, y)
                    source = (2 * x + core) * 16 + 4 * z + y
                    target = (2 * tx + tcore) * 16 + 4 * tz + ty
                    result.append((source, target))
    return result


def send(value, where):
    return lax.ppermute(value, AXES, pairs(where))


def along_x(k):
    return lambda x, core, z, y: ((x + k) % 4, core, z, y)


def along_z(k):
    return lambda x, core, z, y: (x, core, (z + k) % 4, y)


def along_y(k):
    return lambda x, core, z, y: (x, core, z, (y + k) % 4)


def other_core(x, core, z, y):
    return (x, 1 - core, z, y)


def planes(k):
    return lambda x, core, z, y: (z, core, (x + k) % 4, y)


def to_col_owner(x, core, z, y):
    q = (2 * x + core) * 16 + 4 * z + y
    row, col = q % 8, q // 8
    return (row // 2, row % 2, col // 4, col % 4)


def ring(value, direction):
    return [send(value, direction(k)) for k in (1, 3, 2)]


def halves(value):
    high = value.astype(BF16)
    return high, (value - high.astype(F32)).astype(BF16)


def dot16(left, right, dims):
    return lax.dot_general(left, right, (dims, ((), ())), preferred_element_type=F32)


def split_dot(left, right, dims):
    left_high, left_low = halves(left)
    right_high, right_low = halves(right)
    return (
        dot16(left_low, right_high, dims)
        + dot16(left_high, right_low, dims)
        + dot16(left_high, right_high, dims)
    )


def full_dot(left, right, dims=((1,), (0,))):
    return lax.dot_general(
        left, right, (dims, ((), ())), precision=lax.Precision.HIGHEST, preferred_element_type=F32
    )


def lane(value, index):
    return jnp.take_along_axis(value, jnp.full(value.shape, index, jnp.int32), axis=1)


def rows_of_panel(place, first, near, far, opposite, target):
    z, y = place[2], place[3]
    for kz, block in enumerate((first, near, far, opposite)):
        kz = (0, 1, 3, 2)[kz]
        for ky, slot in ((0, 0), (1, 1), (3, 2), (2, 3)):
            index = ((z - kz) % 4) * 4 + (y - ky) % 4
            start = pl.multiple_of(index * PIECE, 16)
            target[pl.ds(start, PIECE), :] = block[slot * PIECE : (slot + 1) * PIECE, :]


def cols_of_panel(place, own, swapped, target):
    x, core = place[0], place[1]
    for half, block in ((core, own), (1 - core, swapped)):
        for kx, slot in ((0, 0), (1, 1), (3, 2), (2, 3)):
            index = ((x - kx) % 4) * 2 + half
            start = pl.multiple_of(index * PIECE, 16)
            target[pl.ds(start, PIECE), :] = block[slot * PIECE : (slot + 1) * PIECE, :]


def image_kernel(place, trailing, p0, p1, p3, p2, sent, kept, panel_rows, total, corner):
    step = pl.program_id(0)

    @pl.when(step == 0)
    def _():
        rows_of_panel(place, p0, p1, p3, p2, panel_rows)
        total[...] = jnp.zeros_like(total)
        first = jnp.where((place[0] == 0) & (place[1] == 0), 1.0, 0.0)
        corner[...] = trailing[:WIDTH, :].T * first
        gram = full_dot(panel_rows[...], panel_rows[...], ((0,), (0,)))
        top = panel_rows[:WIDTH, :] * first
        for out in (sent, kept):
            out[8 * PIECE : 8 * PIECE + WIDTH, :] = gram
            out[8 * PIECE + WIDTH :, :] = top

    block_high, block_low = halves(trailing[...])
    start = pl.multiple_of(step * TALL, TALL)
    turned_high, turned_low = halves(panel_rows[pl.ds(start, TALL), :].T)
    both = jnp.concatenate([turned_high, turned_low], axis=0)
    wide = dot16(both, block_high, ((1,), (0,)))
    total[...] += wide[:WIDTH] + wide[WIDTH:] + dot16(turned_high, block_low, ((1,), (0,)))

    @pl.when(step == STEPS - 1)
    def _():
        image = total[...].T
        for out, half in ((kept, place[1]), (sent, 1 - place[1])):
            for value in range(2):

                @pl.when(half == value)
                def _(out=out, value=value):
                    for x in range(4):
                        index = (2 * x + value) * PIECE
                        out[x * PIECE : (x + 1) * PIECE, :] = image[index : index + PIECE, :]
                        out[(4 + x) * PIECE : (5 + x) * PIECE, :] = corner[index : index + PIECE, :]


def deal_kernel(place, kept, received, m0, m1, m3, m2):
    x = place[0]
    small = kept[8 * PIECE :, :] + received[8 * PIECE :, :]
    for k, out in ((0, m0), (1, m1), (3, m3), (2, m2)):
        index = (x + k) % 4
        for part in range(2):
            start = pl.multiple_of((4 * part + index) * PIECE, 16)
            rows = pl.ds(start, PIECE)
            out[part * PIECE : (part + 1) * PIECE, :] = kept[rows, :] + received[rows, :]
        out[2 * PIECE :, :] = small


def cholesky_rows(work, factor):
    lanes = lax.broadcasted_iota(jnp.int32, (1, WIDTH), 1)
    subs = lax.broadcasted_iota(jnp.int32, (8, 1), 0)

    def body(t, carry):
        first = pl.multiple_of(8 * t, 8)
        whole = work[...]
        block = work[pl.ds(first, 8), :]
        columns = [lane(whole, first + b) for b in range(8)]
        pivots = [lane(block, first + b) for b in range(8)]
        for i in range(8):
            row, pivot = block[i : i + 1], pivots[i][i : i + 1]
            inverse = 1.0 / pivot
            scaled = row * lax.rsqrt(pivot)
            factor[pl.ds(first + i, 1), :] = jnp.where(lanes >= first + i, scaled, 0.0)
            column, here = pivots[i], subs == i
            row = row * inverse
            block = jnp.where(here, row, block - column * row)
            for b in range(i + 1, 8):
                entry = pivots[b][i : i + 1] * inverse
                pivots[b] = jnp.where(here, entry, pivots[b] - column * entry)
        for i in range(8):
            whole = whole - columns[i] * block[i : i + 1]
        work[...] = whole
        return carry

    lax.fori_loop(0, WIDTH // 8, body, 0)


def factor_kernel(place, own, r1, r3, r2, upper, normal, image, work):
    total = (own[...] + r2[...]) + (r1[...] + r3[...])
    gram = total[2 * PIECE : 2 * PIECE + WIDTH, :]
    work[...] = gram
    cholesky_rows(work, upper)
    factor = upper[...]
    normal[...] = gram + full_dot(total[2 * PIECE + WIDTH :, :], factor, ((0,), (0,)))
    image[...] = total[:PIECE, :] + full_dot(total[PIECE : 2 * PIECE, :], factor)


def inverse_kernel(source, out):
    out[...] = source[...]
    lanes = lax.broadcasted_iota(jnp.int32, (1, WIDTH), 1)
    subs = lax.broadcasted_iota(jnp.int32, (8, 1), 0)

    def body(t, carry):
        first = pl.multiple_of(8 * t, 8)
        whole = out[...]
        block = out[pl.ds(first, 8), :]
        columns = [lane(whole, first + b) for b in range(8)]
        pivots = [lane(block, first + b) for b in range(8)]
        for i in range(8):
            row, column, here = block[i : i + 1], pivots[i], subs == i
            inverse = 1.0 / column[i : i + 1]
            is_lane = lanes == first + i
            row = jnp.where(is_lane, inverse, row * inverse)
            block = jnp.where(here, row, jnp.where(is_lane, 0.0, block) - column * row)
            for b in range(8):
                if b != i:
                    entry = pivots[b][i : i + 1] * inverse
                    pivots[b] = jnp.where(here, entry, pivots[b] - column * entry)
            pivots[i] = jnp.where(here, inverse, -column * inverse)
        whole = jnp.where((lanes >= first) & (lanes < first + 8), 0.0, whole)
        for i in range(8):
            whole = whole - columns[i] * block[i : i + 1]
        out[...] = whole
        out[pl.ds(first, 8), :] = block
        return carry

    lax.fori_loop(0, WIDTH // 8, body, 0)


def pick_kernel(place, b0, b1, b3, b2, out):
    core, y = place[1], place[3]
    for part in range(2):
        wanted = (y - (2 * (1 - core) + part)) % 4
        for k, block in ((0, b0), (1, b1), (3, b3), (2, b2)):

            @pl.when(wanted == k)
            def _(block=block, part=part):
                out[part * 4 * PIECE : (part + 1) * 4 * PIECE, :] = block[...]


def gather_kernel(place, p0, p1, p3, p2, upper, b0, b1, b3, b2, swapped, panel_rows, image_rows, inner):
    x, core, z, y = place[0], place[1], place[2], place[3]
    rows_of_panel(place, p0, p1, p3, p2, panel_rows)
    first = jnp.where((x == 0) & (core == 0), 1.0, 0.0)
    panel_rows[:WIDTH, :] += upper[...] * first

    def put(block, offset, part, half):
        for kz, slot in ((0, 0), (1, 1), (3, 2), (2, 3)):
            index = 8 * part + 2 * ((z - kz) % 4) + half
            start = pl.multiple_of(index * PIECE, 16)
            piece = offset + slot * PIECE
            image_rows[pl.ds(start, PIECE), :] = block[piece : piece + PIECE, :]

    for part in range(2):
        wanted = (y - (2 * core + part)) % 4
        for k, block in ((0, b0), (1, b1), (3, b3), (2, b2)):

            @pl.when(wanted == k)
            def _(block=block, part=part):
                put(block, 0, part, core)

        put(swapped, part * 4 * PIECE, part, 1 - core)
    inner[...] = split_dot(panel_rows[...], image_rows[...], ((0,), (0,)))


def update_kernel(
    place, trailing, panel_rows, image_rows, pc_own, pc_swap, ic_own, ic_swap, upper, inverse,
    k0, k1, k3, k2, out, mixer, right_high, right_low, panel_cols, image_cols,
):
    step = pl.program_id(0)

    @pl.when(step == 0)
    def _():
        inner = (k0[...] + k2[...]) + (k1[...] + k3[...])
        core_block = full_dot(full_dot(inverse[...], inner, ((0,), (0,))), inverse[...])
        mixer[:WIDTH, :] = inverse[...]
        mixer[WIDTH:, :] = -0.5 * core_block
        cols_of_panel(place, pc_own, pc_swap, panel_cols)
        cols_of_panel(place, ic_own, ic_swap, image_cols)
        first = jnp.where((place[2] == 0) & (place[3] == 0), 1.0, 0.0)
        panel_cols[:WIDTH, :] += upper[...] * first
        shifted = panel_cols[...]
        both = jnp.concatenate([image_cols[...], shifted], axis=1)
        w_cols = split_dot(both, mixer[...], ((1,), (0,)))
        right_high[...], right_low[...] = halves(jnp.concatenate([w_cols, shifted], axis=1))

    shifted = panel_rows[...]
    both = jnp.concatenate([image_rows[...], shifted], axis=1)
    w_rows = split_dot(both, mixer[...], ((1,), (0,)))
    left_high, left_low = halves(jnp.concatenate([shifted, w_rows], axis=1))
    dims = ((1,), (1,))
    change = dot16(left_low, right_high[...], dims) + dot16(left_high, right_low[...], dims)
    out[...] = trailing[...] - (change + dot16(left_high, right_high[...], dims))


def shape(rows, columns=WIDTH):
    return jax.ShapeDtypeStruct((rows, columns), F32)


def params(mib):
    return pltpu.CompilerParams(vmem_limit_bytes=mib * 1024 * 1024)


def shards(panel, trailing):
    row, col = lax.axis_index("row"), lax.axis_index("col")
    place = jnp.stack([row // 2, row % 2, col // 4, col % 4]).astype(jnp.int32)

    with jax.named_scope("panel_y"):
        in_y = jnp.concatenate([panel] + ring(panel, along_y), axis=0)
    with jax.named_scope("panel_z"):
        in_z = [in_y] + ring(in_y, along_z)
    with jax.named_scope("panel_columns"):
        piece = send(panel, to_col_owner)
        panel_own = jnp.concatenate([piece] + ring(piece, along_x), axis=0)
        panel_swap = send(panel_own, other_core)

    count = 8 * PIECE + 2 * WIDTH
    with jax.named_scope("image"):
        sent, kept = pl.pallas_call(
            image_kernel,
            grid=(STEPS,),
            in_specs=[SMEM, pl.BlockSpec((TALL, COLS), lambda i: (i, 0))] + [VMEM] * 4,
            out_specs=[VMEM] * 2,
            out_shape=[shape(count)] * 2,
            scratch_shapes=[pltpu.VMEM((ROWS, WIDTH), F32), pltpu.VMEM((WIDTH, COLS), F32), pltpu.VMEM((COLS, WIDTH), F32)],
            compiler_params=params(24),
            cost_estimate=pl.CostEstimate(flops=6 * ROWS * COLS * WIDTH, bytes_accessed=4 * ROWS * COLS, transcendentals=0),
        )(place, trailing, *in_z)
    with jax.named_scope("image_core"):
        received = send(sent, other_core)
    with jax.named_scope("deal"):
        m0, m1, m3, m2 = pl.pallas_call(
            deal_kernel,
            in_specs=[SMEM] + [VMEM] * 2,
            out_specs=[VMEM] * 4,
            out_shape=[shape(2 * PIECE + 2 * WIDTH)] * 4,
            compiler_params=params(8),
        )(place, kept, received)
    with jax.named_scope("image_x"):
        r1, r3, r2 = (send(m, along_x(k)) for m, k in ((m1, 1), (m3, 3), (m2, 2)))
    with jax.named_scope("factor"):
        upper, normal, image = pl.pallas_call(
            factor_kernel,
            in_specs=[SMEM] + [VMEM] * 4,
            out_specs=[VMEM] * 3,
            out_shape=[shape(WIDTH), shape(WIDTH), shape(PIECE)],
            scratch_shapes=[pltpu.VMEM((WIDTH, WIDTH), F32)],
            compiler_params=params(8),
        )(place, m0, r1, r3, r2)

    with jax.named_scope("image_planes"):
        in_plane = jnp.concatenate([send(image, planes(k)) for k in (0, 1, 3, 2)], axis=0)
    with jax.named_scope("image_y"):
        blocks = [in_plane] + ring(in_plane, along_y)
    with jax.named_scope("inverse"):
        inverse = pl.pallas_call(
            inverse_kernel,
            in_specs=[VMEM],
            out_specs=VMEM,
            out_shape=shape(WIDTH),
            compiler_params=params(4),
            cost_estimate=pl.CostEstimate(flops=2000000000, bytes_accessed=131072, transcendentals=0),
        )(normal)
    with jax.named_scope("image_columns"):
        image_own = jnp.concatenate([image] + ring(image, along_x), axis=0)
        image_swap = send(image_own, other_core)
    with jax.named_scope("pick"):
        chosen = pl.pallas_call(
            pick_kernel,
            in_specs=[SMEM] + [VMEM] * 4,
            out_specs=VMEM,
            out_shape=shape(8 * PIECE),
            compiler_params=params(8),
        )(place, *blocks)
    with jax.named_scope("image_swap"):
        swapped = send(chosen, other_core)
    with jax.named_scope("gather"):
        panel_rows, image_rows, inner = pl.pallas_call(
            gather_kernel,
            in_specs=[SMEM] + [VMEM] * 10,
            out_specs=[VMEM] * 3,
            out_shape=[shape(ROWS), shape(ROWS), shape(WIDTH)],
            compiler_params=params(16),
        )(place, *in_z, upper, *blocks, swapped)
    with jax.named_scope("inner"):
        inner = inner + send(inner, other_core)
        k1, k3, k2 = ring(inner, along_x)

    tall = pl.BlockSpec((TALL, WIDTH), lambda i: (i, 0))
    block = pl.BlockSpec((TALL, COLS), lambda i: (i, 0))
    with jax.named_scope("update"):
        updated = pl.pallas_call(
            update_kernel,
            grid=(STEPS,),
            in_specs=[SMEM, block, tall, tall] + [VMEM] * 10,
            out_specs=block,
            out_shape=shape(ROWS, COLS),
            scratch_shapes=[
                pltpu.VMEM((2 * WIDTH, WIDTH), F32),
                pltpu.VMEM((COLS, 2 * WIDTH), BF16),
                pltpu.VMEM((COLS, 2 * WIDTH), BF16),
                pltpu.VMEM((COLS, WIDTH), F32),
                pltpu.VMEM((COLS, WIDTH), F32),
            ],
            compiler_params=params(32),
            cost_estimate=pl.CostEstimate(flops=12 * ROWS * COLS * WIDTH, bytes_accessed=8 * ROWS * COLS, transcendentals=0),
        )(
            place, trailing, panel_rows, image_rows, panel_own, panel_swap, image_own, image_swap, upper, inverse,
            inner, k1, k3, k2,
        )
    return upper, updated


def solution(mesh):
    return jax.shard_map(
        shards,
        mesh=mesh,
        in_specs=(P(("row", "col"), None), P("row", "col")),
        out_specs=(P(), P("row", "col")),
        check_vma=False,
    )
```

time: 495 us -> 136 us (0.27)
  waiting for transfers between devices: 381 us -> 58.5 us
  other arithmetic: 46.6 us -> 0.09 us
  matrix products: 45.8 us -> 0 us
  starting transfers between devices: 0.65 us -> 38.4 us
  Pallas kernels: 0 us -> 31.9 us
  between operations: 13.9 us -> 0.94 us
    psum x3 -> x0, waiting for transfers between devices: 270 us -> none  [the longest x1 147 us: shards(): lax.psum((product(panel_block.T, panel_block), product(top_mask.T, panel_...]
    all_gather x2 -> x0, waiting for transfers between devices: 111 us -> none  [the longest x1 55.7 us: shards(): every_rows = lax.all_gather(shifted, ('row', 'col'), axis=0, tiled=True)]
    ppermute x0 -> x31, waiting for transfers between devices: none -> 58.5 us  [send(): return lax.ppermute(value, AXES, pairs(where))]
    another operation x10 -> x1, other arithmetic: 45.7 us -> 0.08 us  [shards(): place = jnp.stack([row // 2, row % 2, col // 4, col % 4]).astype(jnp.int32)]
    dot_general x10 -> x0, matrix products: 43.3 us -> none  [product(): jnp.dot(left_side, right_side, precision=precise, preferred_element_type=...]
    ppermute x0 -> x31, starting transfers between devices: none -> 38.4 us  [send(): return lax.ppermute(value, AXES, pairs(where))]
    pallas_call x0 -> x7, Pallas kernels: none -> 31.9 us  [the longest x1 11.4 us: shards(): pl.pallas_call(update_kernel, grid=(STEPS,), in_specs=[SMEM, block, tall,...]
  transfers between devices with their start and end apart: 5 -> 31, of which waited for: 5 -> 13; matrix products, arithmetic and copies ran while one was open for 6% -> 1% of each run, Pallas kernels for 0% -> 9%
where the time goes in v1:
time: 136 us
  waiting for transfers between devices  58.5 us (43%)
  starting transfers between devices  38.4 us (28%)
  Pallas kernels  31.9 us (23%)
  local copies, waits for them, and re-layouts  5.9 us (4%)
    ppermute x31, waiting for transfers between devices, send(): return lax.ppermute(value, AXES, pairs(where))  58.5 us
    ppermute x31, starting transfers between devices, send(): return lax.ppermute(value, AXES, pairs(where))  38.4 us
    pallas_call x1, Pallas kernels, shards(): pl.pallas_call(update_kernel, grid=(STEPS,), in_specs=[SMEM, block, tall,...  11.4 us
    pallas_call x1, Pallas kernels, shards(): pl.pallas_call(image_kernel, grid=(STEPS,), in_specs=[SMEM, pl.BlockSpec(...  7.04 us
    unnamed x26, local copies, waits for them, and re-layouts  5.87 us
    pallas_call x1, Pallas kernels, shards(): pl.pallas_call(factor_kernel, in_specs=[SMEM] + [VMEM] * 4, out_specs=[VM...  5.83 us
    pallas_call x1, Pallas kernels, shards(): pl.pallas_call(inverse_kernel, in_specs=[VMEM], out_specs=VMEM, out_shape...  4.67 us
  transfers between devices with their start and end apart: 31, of which 13 were waited for; matrix products, arithmetic and copies ran while one was open for 1% of the time, Pallas kernels for 9%

profile of v1, /device:TPU:1, one launch (start us, length us, event | category | flops | bytes accessed | tf_op | source)
XLA Modules:
  0.0 135.7 jit_solution(14929670505431309227)
XLA Ops:
  0.6 3.8 %collective-permute-start.2 = (f32[144,128]{1,0:T(8,128)}, f32[144,128]{1,0:T(8,128)S(1)}, u32[]{:S(2)}, u32[]{:S(2)}) collective-permute-start(f32[144,128]{1,0:T(8,128)} %param.2), channel_id=1, source_target_pairs={{0,2},{1,3},{2,0},{3,1},{4,6},{5,7},{6,4},{7,5},{8,10},{9,11},{10,... | collective-permute-start | bytes 221192 | tf_op jit(solution)/shard_map/panel_y/ppermute | solution.py:35
  4.5 0.8 collective-permute-start.1
  5.2 0.7 collective-permute-start
  5.9 0.9 constant_dynamic-update-slice_fusion.3
  6.9 3.0 %collective-permute-done = f32[144,128]{1,0:T(8,128)S(1)} collective-permute-done((f32[144,128]{1,0:T(8,128)}, f32[144,128]{1,0:T(8,128)S(1)}, u32[]{:S(2)}, u32[]{:S(2)}) %collective-permute-start) | collective-permute-done | bytes 73760 | tf_op jit(solution)/shard_map/panel_y/ppermute | solution.py:35
  9.9 3.7 %collective-permute-start.5 = (f32[576,128]{1,0:T(8,128)S(1)}, f32[576,128]{1,0:T(8,128)S(1)}, u32[]{:S(2)}, u32[]{:S(2)}) collective-permute-start(f32[576,128]{1,0:T(8,128)S(1)} %constant_dynamic-update-slice_fusion.p0), channel_id=1, source_target_pairs={{0,8},{1,9},{2,10},{3,11},{4,12},{5,13},{6,14},{7,15},{8,0},{9,1},... | collective-permute-start | bytes 884744 | tf_op jit(solution)/shard_map/panel_z/ppermute | solution.py:35
  13.6 0.4 collective-permute-start.4
  14.0 1.0 collective-permute-start.3
  15.1 3.4 %collective-permute-done.5.p2 = f32[576,128]{1,0:T(8,128)S(1)} collective-permute-done((f32[576,128]{1,0:T(8,128)S(1)}, f32[576,128]{1,0:T(8,128)S(1)}, u32[]{:S(2)}, u32[]{:S(2)}) %collective-permute-start.5) | collective-permute-done | bytes 294944 | tf_op jit(solution)/shard_map/panel_z/ppermute | solution.py:35
  18.5 8.5 %collective-permute-done.4.p3 = f32[576,128]{1,0:T(8,128)S(1)} collective-permute-done((f32[576,128]{1,0:T(8,128)S(1)}, f32[576,128]{1,0:T(8,128)S(1)}, u32[]{:S(2)}, u32[]{:S(2)}) %collective-permute-start.4) | collective-permute-done | bytes 294944 | tf_op jit(solution)/shard_map/panel_z/ppermute | solution.py:35
  27.1 4.0 %copy-done = f32[2304,1152]{1,0:T(8,128)S(1)} copy-done((f32[2304,1152]{1,0:T(8,128)S(1)}, f32[2304,1152]{1,0:T(8,128)}, u32[]{:S(2)}) %copy-start) | copy-done | bytes 10616856
  31.1 7.0 %image.1 = (f32[1408,128]{1,0:T(8,128)S(1)}, f32[1408,128]{1,0:T(8,128)S(1)}) custom-call(s32[4]{0:T(128)S(1)} %pad_add_fusion.place, f32[2304,1152]{1,0:T(8,128)S(1)} %copy-done, f32[576,128]{1,0:T(8,128)S(1)} %constant_dynamic-update-slice_fusion.p0, f32[576,128]{1,0:T(8,128)S(1)} %collective-permute-done.3.p1, f32[576,128]{1,0:T(8,128)S(1)} %collective-permute-done.4.p3, ...), custom_call_target="tpu_custom_call" | custom-call | flops 2038431744 | bytes 10616832 | tf_op jit(solution)/shard_map/image/pallas_call | solution.py:324
  38.1 1.6 %collective-permute-start.6 = (f32[1408,128]{1,0:T(8,128)S(1)}, f32[1408,128]{1,0:T(8,128)S(1)}, u32[]{:S(2)}, u32[]{:S(2)}) collective-permute-start(f32[1408,128]{1,0:T(8,128)S(1)} %get-tuple-element.15), channel_id=1, source_target_pairs={{0,16},{1,17},{2,18},{3,19},{4,20},{5,21},{6,22},{7,23},{8,24},{9,... | collective-permute-start | bytes 2162696 | tf_op jit(solution)/shard_map/image_core/ppermute | solution.py:35
  39.8 1.8 %collective-permute-done.6.received = f32[1408,128]{1,0:T(8,128)S(1)} collective-permute-done((f32[1408,128]{1,0:T(8,128)S(1)}, f32[1408,128]{1,0:T(8,128)S(1)}, u32[]{:S(2)}, u32[]{:S(2)}) %collective-permute-start.6) | collective-permute-done | bytes 720928 | tf_op jit(solution)/shard_map/image_core/ppermute | solution.py:35
  41.6 0.6 deal.1
  42.2 1.3 collective-permute-start.7
  43.5 1.5 %collective-permute-start.8 = (f32[544,128]{1,0:T(8,128)S(1)}, f32[544,128]{1,0:T(8,128)S(1)}, u32[]{:S(2)}, u32[]{:S(2)}) collective-permute-start(f32[544,128]{1,0:T(8,128)S(1)} %get-tuple-element.18), channel_id=1, source_target_pairs={{0,96},{1,97},{2,98},{3,99},{4,100},{5,101},{6,102},{7,103},{8,104... | collective-permute-start | bytes 835592 | tf_op jit(solution)/shard_map/image_x/ppermute | solution.py:35
  45.0 1.5 %collective-permute-start.9 = (f32[544,128]{1,0:T(8,128)S(1)}, f32[544,128]{1,0:T(8,128)S(1)}, u32[]{:S(2)}, u32[]{:S(2)}) collective-permute-start(f32[544,128]{1,0:T(8,128)S(1)} %get-tuple-element.19), channel_id=1, source_target_pairs={{0,64},{1,65},{2,66},{3,67},{4,68},{5,69},{6,70},{7,71},{8,72},{9,... | collective-permute-start | bytes 835592 | tf_op jit(solution)/shard_map/image_x/ppermute | solution.py:35
  46.5 4.4 %collective-permute-start.18 = (f32[144,128]{1,0:T(8,128)S(1)}, f32[144,128]{1,0:T(8,128)S(1)}, u32[]{:S(2)}, u32[]{:S(2)}) collective-permute-start(f32[144,128]{1,0:T(8,128)S(1)} %copy-done.3), channel_id=1, source_target_pairs={{0,0},{1,16},{2,32},{3,48},{4,64},{5,80},{6,96},{7,112},{8,1},{9,1... | collective-permute-start | bytes 221192 | tf_op jit(solution)/shard_map/panel_columns/ppermute | solution.py:35
  50.9 0.5 collective-permute-done.7.r1
  51.4 7.0 %collective-permute-done.9.r2 = f32[544,128]{1,0:T(8,128)S(1)} collective-permute-done((f32[544,128]{1,0:T(8,128)S(1)}, f32[544,128]{1,0:T(8,128)S(1)}, u32[]{:S(2)}, u32[]{:S(2)}) %collective-permute-start.9) | collective-permute-done | bytes 278560 | tf_op jit(solution)/shard_map/image_x/ppermute | solution.py:35
  58.4 5.8 %factor.1 = (f32[128,128]{1,0:T(8,128)}, f32[128,128]{1,0:T(8,128)S(1)}, f32[144,128]{1,0:T(8,128)S(1)}) custom-call(s32[4]{0:T(128)S(1)} %pad_add_fusion.place, f32[544,128]{1,0:T(8,128)S(1)} %get-tuple-element.16.own, f32[544,128]{1,0:T(8,128)S(1)} %collective-permute-done.7.r1, f32[544,128]{1,0:T(8,128)S(1)} %collective-permute-done.8.r3, ...), custom_call_target="tpu_custom_call" | custom-call | tf_op jit(solution)/shard_map/factor/pallas_call | solution.py:347
  64.2 0.8 collective-permute-start.10
  65.0 6.2 %collective-permute-start.21 = (f32[144,128]{1,0:T(8,128)S(1)}, f32[144,128]{1,0:T(8,128)S(1)}, u32[]{:S(2)}, u32[]{:S(2)}) collective-permute-start(f32[144,128]{1,0:T(8,128)S(1)} %collective-permute-done.18), channel_id=1, source_target_pairs={{0,64},{1,65},{2,66},{3,67},{4,68},{5,69},{6,70},{7,71},{8,72},{9,... | collective-permute-start | bytes 221192 | tf_op jit(solution)/shard_map/panel_columns/ppermute | solution.py:35
  71.2 0.4 collective-permute-start.19
  71.6 0.7 collective-permute-start.12
  72.3 2.1 %collective-permute-start.11 = (f32[144,128]{1,0:T(8,128)S(1)}, f32[144,128]{1,0:T(8,128)S(1)}, u32[]{:S(2)}, u32[]{:S(2)}) collective-permute-start(f32[144,128]{1,0:T(8,128)S(1)} %get-tuple-element.21), channel_id=1, source_target_pairs={{0,4},{1,5},{2,6},{3,7},{4,36},{5,37},{6,38},{7,39},{8,68},{9,69},... | collective-permute-start | bytes 221192 | tf_op jit(solution)/shard_map/image_planes/ppermute | solution.py:35
  74.3 13.3 %collective-permute-done.11 = f32[144,128]{1,0:T(8,128)S(1)} collective-permute-done((f32[144,128]{1,0:T(8,128)S(1)}, f32[144,128]{1,0:T(8,128)S(1)}, u32[]{:S(2)}, u32[]{:S(2)}) %collective-permute-start.11) | collective-permute-done | bytes 73760 | tf_op jit(solution)/shard_map/image_planes/ppermute | solution.py:35
  87.7 0.3 collective-permute-start.16
  88.0 2.4 %collective-permute-start.15 = (f32[576,128]{1,0:T(8,128)S(1)}, f32[576,128]{1,0:T(8,128)S(1)}, u32[]{:S(2)}, u32[]{:S(2)}) collective-permute-start(f32[576,128]{1,0:T(8,128)S(1)} %constant_dynamic-update-slice_fusion.4.b0), channel_id=1, source_target_pairs={{0,3},{1,0},{2,1},{3,2},{4,7},{5,4},{6,5},{7,6},{8,11},{9,8},{10,9... | collective-permute-start | bytes 884744 | tf_op jit(solution)/shard_map/image_y/ppermute | solution.py:35
  90.5 3.5 %collective-permute-done.20 = f32[144,128]{1,0:T(8,128)S(1)} collective-permute-done((f32[144,128]{1,0:T(8,128)S(1)}, f32[144,128]{1,0:T(8,128)S(1)}, u32[]{:S(2)}, u32[]{:S(2)}) %collective-permute-start.20) | collective-permute-done | bytes 73760 | tf_op jit(solution)/shard_map/panel_columns/ppermute | solution.py:35
  94.0 3.2 %collective-permute-done.16.b2 = f32[576,128]{1,0:T(8,128)S(1)} collective-permute-done((f32[576,128]{1,0:T(8,128)S(1)}, f32[576,128]{1,0:T(8,128)S(1)}, u32[]{:S(2)}, u32[]{:S(2)}) %collective-permute-start.16) | collective-permute-done | bytes 294944 | tf_op jit(solution)/shard_map/image_y/ppermute | solution.py:35
  97.2 3.6 %collective-permute-done.15.b3 = f32[576,128]{1,0:T(8,128)S(1)} collective-permute-done((f32[576,128]{1,0:T(8,128)S(1)}, f32[576,128]{1,0:T(8,128)S(1)}, u32[]{:S(2)}, u32[]{:S(2)}) %collective-permute-start.15) | collective-permute-done | bytes 294944 | tf_op jit(solution)/shard_map/image_y/ppermute | solution.py:35
  100.8 3.7 %collective-permute-done.14.b1 = f32[576,128]{1,0:T(8,128)S(1)} collective-permute-done((f32[576,128]{1,0:T(8,128)S(1)}, f32[576,128]{1,0:T(8,128)S(1)}, u32[]{:S(2)}, u32[]{:S(2)}) %collective-permute-start.14) | collective-permute-done | bytes 294944 | tf_op jit(solution)/shard_map/image_y/ppermute | solution.py:35
  104.5 0.6 pick.1
  105.2 0.6 collective-permute-start.17
  105.7 0.1 collective-permute-start.22
  106.0 1.5 %collective-permute-start.23 = (f32[144,128]{1,0:T(8,128)S(1)}, f32[144,128]{1,0:T(8,128)S(1)}, u32[]{:S(2)}, u32[]{:S(2)}) collective-permute-start(f32[144,128]{1,0:T(8,128)S(1)} %get-tuple-element.21), channel_id=1, source_target_pairs={{0,32},{1,33},{2,34},{3,35},{4,36},{5,37},{6,38},{7,39},{8,40},{9,... | collective-permute-start | bytes 221192 | tf_op jit(solution)/shard_map/image_columns/ppermute | solution.py:35
  107.5 5.7 %collective-permute-done.23 = f32[144,128]{1,0:T(8,128)S(1)} collective-permute-done((f32[144,128]{1,0:T(8,128)S(1)}, f32[144,128]{1,0:T(8,128)S(1)}, u32[]{:S(2)}, u32[]{:S(2)}) %collective-permute-start.23) | collective-permute-done | bytes 73760 | tf_op jit(solution)/shard_map/image_columns/ppermute | solution.py:35
  113.2 0.6 collective-permute-start.26
  113.8 0.8 copy-done.1
  114.7 1.6 %gather.1 = (f32[2304,128]{1,0:T(8,128)S(1)}, f32[2304,128]{1,0:T(8,128)S(1)}, f32[128,128]{1,0:T(8,128)S(1)}) custom-call(s32[4]{0:T(128)S(1)} %pad_add_fusion.place, f32[576,128]{1,0:T(8,128)S(1)} %constant_dynamic-update-slice_fusion.p0, f32[576,128]{1,0:T(8,128)S(1)} %collective-permute-done.3.p1, f32[576,128]{1,0:T(8,128)S(1)} %collective-permute-done.4.p3, ...), custom_call_target="tpu_custom_call" | custom-call | tf_op jit(solution)/shard_map/gather/pallas_call | solution.py:383
  116.4 1.2 collective-permute-done.27
  117.7 0.3 collective-permute-start.30
  118.0 0.9 collective-permute-start.29
  118.9 0.6 collective-permute-start.28
  119.5 4.7 %inverse.1 = f32[128,128]{1,0:T(8,128)S(1)} custom-call(f32[128,128]{1,0:T(8,128)S(1)} %get-tuple-element.24.source), custom_call_target="tpu_custom_call" | custom-call | flops 2000000000 | bytes 131072 | tf_op jit(solution)/shard_map/inverse/pallas_call | solution.py:361
  124.2 11.4 %update.1 = f32[2304,1152]{1,0:T(8,128)} custom-call(s32[4]{0:T(128)S(1)} %pad_add_fusion.place, f32[2304,1152]{1,0:T(8,128)S(1)} %bitcast.5, f32[2304,128]{1,0:T(8,128)S(1)} %get-tuple-element.22.panel_rows, f32[2304,128]{1,0:T(8,128)S(1)} %get-tuple-element.23.image_rows, f32[576,128]{1,0:T(8,128)S(1)} %constant_dynamic-update-slice_fusion.8.pc_own, ...), custom_call_target="tpu_custom_call" | custom-call | flops 4076863488 | bytes 21233664 | tf_op jit(solution)/shard_map/update/pallas_call | solution.py:397
  (54 shorter events, 0.6 us)
Async XLA Ops:
  0.6 45.9 %copy-start.3 = (f32[144,128]{1,0:T(8,128)S(1)}, f32[144,128]{1,0:T(8,128)}, u32[]{:S(2)}) copy-start(f32[144,128]{1,0:T(8,128)} %param.2) | copy-start | bytes 221188
  0.6 9.3 %collective-permute-start.2 = (f32[144,128]{1,0:T(8,128)}, f32[144,128]{1,0:T(8,128)S(1)}, u32[]{:S(2)}, u32[]{:S(2)}) collective-permute-start(f32[144,128]{1,0:T(8,128)} %param.2), channel_id=1, source_target_pairs={{0,2},{1,3},{2,0},{3,1},{4,6},{5,7},{6,4},{7,5},{8,10},{9,11},{10,... | collective-permute-start | bytes 221192 | tf_op jit(solution)/shard_map/panel_y/ppermute | solution.py:35
  4.5 5.4 %collective-permute-start.1 = (f32[144,128]{1,0:T(8,128)}, f32[144,128]{1,0:T(8,128)S(1)}, u32[]{:S(2)}, u32[]{:S(2)}) collective-permute-start(f32[144,128]{1,0:T(8,128)} %param.2), channel_id=1, source_target_pairs={{0,3},{1,0},{2,1},{3,2},{4,7},{5,4},{6,5},{7,6},{8,11},{9,8},{10,9... | collective-permute-start | bytes 221192 | tf_op jit(solution)/shard_map/panel_y/ppermute | solution.py:35
  5.2 4.6 %collective-permute-start = (f32[144,128]{1,0:T(8,128)}, f32[144,128]{1,0:T(8,128)S(1)}, u32[]{:S(2)}, u32[]{:S(2)}) collective-permute-start(f32[144,128]{1,0:T(8,128)} %param.2), channel_id=1, source_target_pairs={{0,1},{1,2},{2,3},{3,0},{4,5},{5,6},{6,7},{7,4},{8,9},{9,10},{10,1... | collective-permute-start | bytes 221192 | tf_op jit(solution)/shard_map/panel_y/ppermute | solution.py:35
  9.9 8.6 %collective-permute-start.5 = (f32[576,128]{1,0:T(8,128)S(1)}, f32[576,128]{1,0:T(8,128)S(1)}, u32[]{:S(2)}, u32[]{:S(2)}) collective-permute-start(f32[576,128]{1,0:T(8,128)S(1)} %constant_dynamic-update-slice_fusion.p0), channel_id=1, source_target_pairs={{0,8},{1,9},{2,10},{3,11},{4,12},{5,13},{6,14},{7,15},{8,0},{9,1},... | collective-permute-start | bytes 884744 | tf_op jit(solution)/shard_map/panel_z/ppermute | solution.py:35
  13.6 13.5 %collective-permute-start.4 = (f32[576,128]{1,0:T(8,128)S(1)}, f32[576,128]{1,0:T(8,128)S(1)}, u32[]{:S(2)}, u32[]{:S(2)}) collective-permute-start(f32[576,128]{1,0:T(8,128)S(1)} %constant_dynamic-update-slice_fusion.p0), channel_id=1, source_target_pairs={{0,12},{1,13},{2,14},{3,15},{4,0},{5,1},{6,2},{7,3},{8,4},{9,5},{1... | collective-permute-start | bytes 884744 | tf_op jit(solution)/shard_map/panel_z/ppermute | solution.py:35
  14.0 13.0 %collective-permute-start.3 = (f32[576,128]{1,0:T(8,128)S(1)}, f32[576,128]{1,0:T(8,128)S(1)}, u32[]{:S(2)}, u32[]{:S(2)}) collective-permute-start(f32[576,128]{1,0:T(8,128)S(1)} %constant_dynamic-update-slice_fusion.p0), channel_id=1, source_target_pairs={{0,4},{1,5},{2,6},{3,7},{4,8},{5,9},{6,10},{7,11},{8,12},{9,13},{1... | collective-permute-start | bytes 884744 | tf_op jit(solution)/shard_map/panel_z/ppermute | solution.py:35
  27.1 4.0 %copy-start = (f32[2304,1152]{1,0:T(8,128)S(1)}, f32[2304,1152]{1,0:T(8,128)}, u32[]{:S(2)}) copy-start(f32[2304,1152]{1,0:T(8,128)} %trailing.3) | copy-start | bytes 31850500
  31.1 93.1 %slice-start = ((s8[10616832]{0:T(1024)(128)(4,1)}), s8[4194304]{0:T(1024)(128)(4,1)S(1)}, s32[]{:S(2)}) async-start(s8[10616832]{0:T(1024)(128)(4,1)} %bitcast.4), calls=%async_computation | async-start | bytes 8388608
  31.1 93.1 %slice-start.1 = ((s8[10616832]{0:T(1024)(128)(4,1)}), s8[4194304]{0:T(1024)(128)(4,1)S(1)}, s32[]{:S(2)}) async-start(s8[10616832]{0:T(1024)(128)(4,1)} %bitcast.4), calls=%async_computation.1 | async-start | bytes 8388608
  38.1 3.5 %collective-permute-start.6 = (f32[1408,128]{1,0:T(8,128)S(1)}, f32[1408,128]{1,0:T(8,128)S(1)}, u32[]{:S(2)}, u32[]{:S(2)}) collective-permute-start(f32[1408,128]{1,0:T(8,128)S(1)} %get-tuple-element.15), channel_id=1, source_target_pairs={{0,16},{1,17},{2,18},{3,19},{4,20},{5,21},{6,22},{7,23},{8,24},{9,... | collective-permute-start | bytes 2162696 | tf_op jit(solution)/shard_map/image_core/ppermute | solution.py:35
  42.2 9.2 %collective-permute-start.7 = (f32[544,128]{1,0:T(8,128)S(1)}, f32[544,128]{1,0:T(8,128)S(1)}, u32[]{:S(2)}, u32[]{:S(2)}) collective-permute-start(f32[544,128]{1,0:T(8,128)S(1)} %get-tuple-element.17), channel_id=1, source_target_pairs={{0,32},{1,33},{2,34},{3,35},{4,36},{5,37},{6,38},{7,39},{8,40},{9,... | collective-permute-start | bytes 835592 | tf_op jit(solution)/shard_map/image_x/ppermute | solution.py:35
  43.5 7.9 %collective-permute-start.8 = (f32[544,128]{1,0:T(8,128)S(1)}, f32[544,128]{1,0:T(8,128)S(1)}, u32[]{:S(2)}, u32[]{:S(2)}) collective-permute-start(f32[544,128]{1,0:T(8,128)S(1)} %get-tuple-element.18), channel_id=1, source_target_pairs={{0,96},{1,97},{2,98},{3,99},{4,100},{5,101},{6,102},{7,103},{8,104... | collective-permute-start | bytes 835592 | tf_op jit(solution)/shard_map/image_x/ppermute | solution.py:35
  45.0 13.4 %collective-permute-start.9 = (f32[544,128]{1,0:T(8,128)S(1)}, f32[544,128]{1,0:T(8,128)S(1)}, u32[]{:S(2)}, u32[]{:S(2)}) collective-permute-start(f32[544,128]{1,0:T(8,128)S(1)} %get-tuple-element.19), channel_id=1, source_target_pairs={{0,64},{1,65},{2,66},{3,67},{4,68},{5,69},{6,70},{7,71},{8,72},{9,... | collective-permute-start | bytes 835592 | tf_op jit(solution)/shard_map/image_x/ppermute | solution.py:35
  46.5 18.5 %collective-permute-start.18 = (f32[144,128]{1,0:T(8,128)S(1)}, f32[144,128]{1,0:T(8,128)S(1)}, u32[]{:S(2)}, u32[]{:S(2)}) collective-permute-start(f32[144,128]{1,0:T(8,128)S(1)} %copy-done.3), channel_id=1, source_target_pairs={{0,0},{1,16},{2,32},{3,48},{4,64},{5,80},{6,96},{7,112},{8,1},{9,1... | collective-permute-start | bytes 221192 | tf_op jit(solution)/shard_map/panel_columns/ppermute | solution.py:35
  64.2 60.0 %copy-start.2 = (f32[128,128]{1,0:T(8,128)S(1)}, f32[128,128]{1,0:T(8,128)}, u32[]{:S(2)}) copy-start(f32[128,128]{1,0:T(8,128)} %get-tuple-element.12.upper) | copy-start | bytes 196612
  64.2 8.1 %collective-permute-start.10 = (f32[144,128]{1,0:T(8,128)S(1)}, f32[144,128]{1,0:T(8,128)S(1)}, u32[]{:S(2)}, u32[]{:S(2)}) collective-permute-start(f32[144,128]{1,0:T(8,128)S(1)} %get-tuple-element.21), channel_id=1, source_target_pairs={{0,0},{1,1},{2,2},{3,3},{4,32},{5,33},{6,34},{7,35},{8,64},{9,65},... | collective-permute-start | bytes 221192 | tf_op jit(solution)/shard_map/image_planes/ppermute | solution.py:35
  65.0 40.7 %collective-permute-start.21 = (f32[144,128]{1,0:T(8,128)S(1)}, f32[144,128]{1,0:T(8,128)S(1)}, u32[]{:S(2)}, u32[]{:S(2)}) collective-permute-start(f32[144,128]{1,0:T(8,128)S(1)} %collective-permute-done.18), channel_id=1, source_target_pairs={{0,64},{1,65},{2,66},{3,67},{4,68},{5,69},{6,70},{7,71},{8,72},{9,... | collective-permute-start | bytes 221192 | tf_op jit(solution)/shard_map/panel_columns/ppermute | solution.py:35
  71.2 19.2 %collective-permute-start.19 = (f32[144,128]{1,0:T(8,128)S(1)}, f32[144,128]{1,0:T(8,128)S(1)}, u32[]{:S(2)}, u32[]{:S(2)}) collective-permute-start(f32[144,128]{1,0:T(8,128)S(1)} %collective-permute-done.18), channel_id=1, source_target_pairs={{0,32},{1,33},{2,34},{3,35},{4,36},{5,37},{6,38},{7,39},{8,40},{9,... | collective-permute-start | bytes 221192 | tf_op jit(solution)/shard_map/panel_columns/ppermute | solution.py:35
  71.6 16.1 %collective-permute-start.13 = (f32[144,128]{1,0:T(8,128)S(1)}, f32[144,128]{1,0:T(8,128)S(1)}, u32[]{:S(2)}, u32[]{:S(2)}) collective-permute-start(f32[144,128]{1,0:T(8,128)S(1)} %get-tuple-element.21), channel_id=1, source_target_pairs={{0,8},{1,9},{2,10},{3,11},{4,40},{5,41},{6,42},{7,43},{8,72},{9,73... | collective-permute-start | bytes 221192 | tf_op jit(solution)/shard_map/image_planes/ppermute | solution.py:35
  71.6 16.1 %collective-permute-start.12 = (f32[144,128]{1,0:T(8,128)S(1)}, f32[144,128]{1,0:T(8,128)S(1)}, u32[]{:S(2)}, u32[]{:S(2)}) collective-permute-start(f32[144,128]{1,0:T(8,128)S(1)} %get-tuple-element.21), channel_id=1, source_target_pairs={{0,12},{1,13},{2,14},{3,15},{4,44},{5,45},{6,46},{7,47},{8,76},{9,... | collective-permute-start | bytes 221192 | tf_op jit(solution)/shard_map/image_planes/ppermute | solution.py:35
  72.3 15.4 %collective-permute-start.11 = (f32[144,128]{1,0:T(8,128)S(1)}, f32[144,128]{1,0:T(8,128)S(1)}, u32[]{:S(2)}, u32[]{:S(2)}) collective-permute-start(f32[144,128]{1,0:T(8,128)S(1)} %get-tuple-element.21), channel_id=1, source_target_pairs={{0,4},{1,5},{2,6},{3,7},{4,36},{5,37},{6,38},{7,39},{8,68},{9,69},... | collective-permute-start | bytes 221192 | tf_op jit(solution)/shard_map/image_planes/ppermute | solution.py:35
  87.7 9.5 %collective-permute-start.16 = (f32[576,128]{1,0:T(8,128)S(1)}, f32[576,128]{1,0:T(8,128)S(1)}, u32[]{:S(2)}, u32[]{:S(2)}) collective-permute-start(f32[576,128]{1,0:T(8,128)S(1)} %constant_dynamic-update-slice_fusion.4.b0), channel_id=1, source_target_pairs={{0,2},{1,3},{2,0},{3,1},{4,6},{5,7},{6,4},{7,5},{8,10},{9,11},{10,... | collective-permute-start | bytes 884744 | tf_op jit(solution)/shard_map/image_y/ppermute | solution.py:35
  88.0 12.8 %collective-permute-start.15 = (f32[576,128]{1,0:T(8,128)S(1)}, f32[576,128]{1,0:T(8,128)S(1)}, u32[]{:S(2)}, u32[]{:S(2)}) collective-permute-start(f32[576,128]{1,0:T(8,128)S(1)} %constant_dynamic-update-slice_fusion.4.b0), channel_id=1, source_target_pairs={{0,3},{1,0},{2,1},{3,2},{4,7},{5,4},{6,5},{7,6},{8,11},{9,8},{10,9... | collective-permute-start | bytes 884744 | tf_op jit(solution)/shard_map/image_y/ppermute | solution.py:35
  90.4 14.1 %collective-permute-start.14 = (f32[576,128]{1,0:T(8,128)S(1)}, f32[576,128]{1,0:T(8,128)S(1)}, u32[]{:S(2)}, u32[]{:S(2)}) collective-permute-start(f32[576,128]{1,0:T(8,128)S(1)} %constant_dynamic-update-slice_fusion.4.b0), channel_id=1, source_target_pairs={{0,1},{1,2},{2,3},{3,0},{4,5},{5,6},{6,7},{7,4},{8,9},{9,10},{10,1... | collective-permute-start | bytes 884744 | tf_op jit(solution)/shard_map/image_y/ppermute | solution.py:35
  90.4 3.6 %collective-permute-start.20 = (f32[144,128]{1,0:T(8,128)S(1)}, f32[144,128]{1,0:T(8,128)S(1)}, u32[]{:S(2)}, u32[]{:S(2)}) collective-permute-start(f32[144,128]{1,0:T(8,128)S(1)} %collective-permute-done.18), channel_id=1, source_target_pairs={{0,96},{1,97},{2,98},{3,99},{4,100},{5,101},{6,102},{7,103},{8,104... | collective-permute-start | bytes 221192 | tf_op jit(solution)/shard_map/panel_columns/ppermute | solution.py:35
  105.2 8.7 %collective-permute-start.17 = (f32[1152,128]{1,0:T(8,128)S(1)}, f32[1152,128]{1,0:T(8,128)S(1)}, u32[]{:S(2)}, u32[]{:S(2)}) collective-permute-start(f32[1152,128]{1,0:T(8,128)S(1)} %pick.1), channel_id=1, source_target_pairs={{0,16},{1,17},{2,18},{3,19},{4,20},{5,21},{6,22},{7,23},{8,24},{9,... | collective-permute-start | bytes 1769480 | tf_op jit(solution)/shard_map/image_swap/ppermute | solution.py:35
  105.7 18.4 %collective-permute-start.22 = (f32[576,128]{1,0:T(8,128)S(1)}, f32[576,128]{1,0:T(8,128)S(1)}, u32[]{:S(2)}, u32[]{:S(2)}) collective-permute-start(f32[576,128]{1,0:T(8,128)S(1)} %constant_dynamic-update-slice_fusion.8.pc_own), channel_id=1, source_target_pairs={{0,16},{1,17},{2,18},{3,19},{4,20},{5,21},{6,22},{7,23},{8,24},{9,... | collective-permute-start | bytes 884744 | tf_op jit(solution)/shard_map/panel_columns/ppermute | solution.py:35
  105.9 7.3 %collective-permute-start.25 = (f32[144,128]{1,0:T(8,128)S(1)}, f32[144,128]{1,0:T(8,128)S(1)}, u32[]{:S(2)}, u32[]{:S(2)}) collective-permute-start(f32[144,128]{1,0:T(8,128)S(1)} %get-tuple-element.21), channel_id=1, source_target_pairs={{0,64},{1,65},{2,66},{3,67},{4,68},{5,69},{6,70},{7,71},{8,72},{9,... | collective-permute-start | bytes 221192 | tf_op jit(solution)/shard_map/image_columns/ppermute | solution.py:35
  105.9 7.2 %collective-permute-start.24 = (f32[144,128]{1,0:T(8,128)S(1)}, f32[144,128]{1,0:T(8,128)S(1)}, u32[]{:S(2)}, u32[]{:S(2)}) collective-permute-start(f32[144,128]{1,0:T(8,128)S(1)} %get-tuple-element.21), channel_id=1, source_target_pairs={{0,96},{1,97},{2,98},{3,99},{4,100},{5,101},{6,102},{7,103},{8,104... | collective-permute-start | bytes 221192 | tf_op jit(solution)/shard_map/image_columns/ppermute | solution.py:35
  106.0 7.1 %collective-permute-start.23 = (f32[144,128]{1,0:T(8,128)S(1)}, f32[144,128]{1,0:T(8,128)S(1)}, u32[]{:S(2)}, u32[]{:S(2)}) collective-permute-start(f32[144,128]{1,0:T(8,128)S(1)} %get-tuple-element.21), channel_id=1, source_target_pairs={{0,32},{1,33},{2,34},{3,35},{4,36},{5,37},{6,38},{7,39},{8,40},{9,... | collective-permute-start | bytes 221192 | tf_op jit(solution)/shard_map/image_columns/ppermute | solution.py:35
  113.2 11.0 %collective-permute-start.26 = (f32[576,128]{1,0:T(8,128)S(1)}, f32[576,128]{1,0:T(8,128)S(1)}, u32[]{:S(2)}, u32[]{:S(2)}) collective-permute-start(f32[576,128]{1,0:T(8,128)S(1)} %constant_dynamic-update-slice_fusion.12.ic_own), channel_id=1, source_target_pairs={{0,16},{1,17},{2,18},{3,19},{4,20},{5,21},{6,22},{7,23},{8,24},{9,... | collective-permute-start | bytes 884744 | tf_op jit(solution)/shard_map/image_columns/ppermute | solution.py:35
  113.8 0.8 copy-start.1
  114.7 9.6 %slice-start.2 = ((s8[10616832]{0:T(1024)(128)(4,1)}), s8[2228224]{0:T(1024)(128)(4,1)S(1)}, s32[]{:S(2)}) async-start(s8[10616832]{0:T(1024)(128)(4,1)} %bitcast.4), calls=%async_computation.2 | async-start | bytes 4456448
  116.3 1.3 collective-permute-start.27
  117.7 6.5 %collective-permute-start.30 = (f32[128,128]{1,0:T(8,128)S(1)}, f32[128,128]{1,0:T(8,128)S(1)}, u32[]{:S(2)}, u32[]{:S(2)}) collective-permute-start(f32[128,128]{1,0:T(8,128)S(1)} %add.14.k0), channel_id=1, source_target_pairs={{0,64},{1,65},{2,66},{3,67},{4,68},{5,69},{6,70},{7,71},{8,72},{9,... | collective-permute-start | bytes 196616 | tf_op jit(solution)/shard_map/inner/ppermute | solution.py:35
  118.0 6.2 %collective-permute-start.29 = (f32[128,128]{1,0:T(8,128)S(1)}, f32[128,128]{1,0:T(8,128)S(1)}, u32[]{:S(2)}, u32[]{:S(2)}) collective-permute-start(f32[128,128]{1,0:T(8,128)S(1)} %add.14.k0), channel_id=1, source_target_pairs={{0,96},{1,97},{2,98},{3,99},{4,100},{5,101},{6,102},{7,103},{8,104... | collective-permute-start | bytes 196616 | tf_op jit(solution)/shard_map/inner/ppermute | solution.py:35
  118.9 5.3 %collective-permute-start.28 = (f32[128,128]{1,0:T(8,128)S(1)}, f32[128,128]{1,0:T(8,128)S(1)}, u32[]{:S(2)}, u32[]{:S(2)}) collective-permute-start(f32[128,128]{1,0:T(8,128)S(1)} %add.14.k0), channel_id=1, source_target_pairs={{0,32},{1,33},{2,34},{3,35},{4,36},{5,37},{6,38},{7,39},{8,40},{9,... | collective-permute-start | bytes 196616 | tf_op jit(solution)/shard_map/inner/ppermute | solution.py:35

commit v2 on v1

v2 whole, which is shorter than its diff:
```python
import jax
import jax.numpy as jnp
from jax import lax
from jax.experimental import pallas as pl
from jax.experimental.pallas import tpu as pltpu
from jax.sharding import PartitionSpec as P

F32 = jnp.float32
BF16 = jnp.bfloat16
AXES = ("row", "col")
PIECE = 144
WIDTH = 128
ROWS = 16 * PIECE
COLS = 8 * PIECE
TALL = 256
STEPS = ROWS // TALL
VMEM = pl.BlockSpec(memory_space=pltpu.VMEM)
SMEM = pl.BlockSpec(memory_space=pltpu.SMEM)


def pairs(where):
    result = []
    for x in range(4):
        for core in range(2):
            for z in range(4):
                for y in range(4):
                    tx, tcore, tz, ty = where(x, core, z, y)
                    source = (2 * x + core) * 16 + 4 * z + y
                    target = (2 * tx + tcore) * 16 + 4 * tz + ty
                    result.append((source, target))
    return result


def send(value, where):
    return lax.ppermute(value, AXES, pairs(where))


def along_x(k):
    return lambda x, core, z, y: ((x + k) % 4, core, z, y)


def along_z(k):
    return lambda x, core, z, y: (x, core, (z + k) % 4, y)


def along_y(k):
    return lambda x, core, z, y: (x, core, z, (y + k) % 4)


def other_core(x, core, z, y):
    return (x, 1 - core, z, y)


def planes(k):
    return lambda x, core, z, y: (z, core, (x + k) % 4, y)


def ring(value, direction):
    return [send(value, direction(k)) for k in (1, 3, 2)]


def halves(value):
    high = value.astype(BF16)
    return high, (value - high.astype(F32)).astype(BF16)


def dot16(left, right, dims):
    return lax.dot_general(left, right, (dims, ((), ())), preferred_element_type=F32)


def split_dot(left, right, dims):
    left_high, left_low = halves(left)
    right_high, right_low = halves(right)
    return (
        dot16(left_low, right_high, dims)
        + dot16(left_high, right_low, dims)
        + dot16(left_high, right_high, dims)
    )


def full_dot(left, right, dims=((1,), (0,))):
    return lax.dot_general(
        left, right, (dims, ((), ())), precision=lax.Precision.HIGHEST, preferred_element_type=F32
    )


def lane(value, index):
    return jnp.take_along_axis(value, jnp.full(value.shape, index, jnp.int32), axis=1)


ALONG = (0, 1, 3, 2)


def around(core):
    return (0, 1 + 2 * core, 3 - 2 * core, 2)


def put_in_order(at, steps, pieces, out, rows, first=0):
    for k, piece in zip(steps, pieces):
        start = pl.multiple_of(first + ((at - k + 4) % 4) * rows, 16)
        out[pl.ds(start, rows), :] = piece[...]


def join_y_kernel(place, p0, p1, p3, p2, out):
    put_in_order(place[3], ALONG, (p0, p1, p3, p2), out, PIECE)


def join_z_kernel(place, p0, p1, p3, p2, out):
    put_in_order(place[2], ALONG, (p0, p1, p3, p2), out, PIECE)


def hand_kernel(place, across, out):
    out[...] = across[pl.ds(pl.multiple_of((1 - place[1]) * PIECE, 16), PIECE), :]


def tag_kernel(place, image, across, handed, out):
    out[:PIECE, :] = image[...]

    @pl.when(place[3] // 2 == place[1])
    def _():
        out[PIECE:, :] = across[pl.ds(pl.multiple_of(place[1] * PIECE, 16), PIECE), :]

    @pl.when(place[3] // 2 != place[1])
    def _():
        out[PIECE:, :] = handed[...]


def split_kernel(trailing, after, whole, high, low, sems):
    copies = []
    for i in range(STEPS):
        rows = pl.ds(i * TALL, TALL)
        copies.append(pltpu.make_async_copy(trailing.at[rows, :], whole.at[rows, :], sems.at[i]))
        copies[-1].start()
    for i in range(STEPS):
        copies[i].wait()
        rows = slice(i * TALL, (i + 1) * TALL)
        high[rows, :], low[rows, :] = halves(whole[rows, :])


def turned_image(place, k, block, high, low):
    rows = pl.ds(pl.multiple_of(((place[2] - k + 4) % 4) * 4 * PIECE, 16), 4 * PIECE)
    turned_high, turned_low = halves(block[...].T)
    wide = dot16(jnp.concatenate([turned_high, turned_low], axis=0), high[rows, :], ((1,), (0,)))
    return wide[:WIDTH] + wide[WIDTH:] + dot16(turned_high, low[rows, :], ((1,), (0,)))


def near_kernel(place, high, low, own, front, back, image, gram, gram_near):
    total = jnp.zeros((WIDTH, COLS), F32)
    for k, block in zip(around(place[1]), (own, front, back)):
        total += turned_image(place, k, block, high, low)
    image[...] = total
    gram[...] = full_dot(own[...], own[...], ((0,), (0,)))
    gram_near[...] = full_dot(front[...], front[...], ((0,), (0,))) + full_dot(back[...], back[...], ((0,), (0,)))


def far_gram_kernel(place, own, below, above, far, gram, gram_near, out):
    x, core, z = place[0], place[1], place[2]
    out[:WIDTH, :] = (gram[...] + full_dot(far[...], far[...], ((0,), (0,)))) + gram_near[...]
    out[WIDTH:, :] = jnp.zeros((WIDTH, WIDTH), F32)
    for k, block in zip(around(core), (own, below, above, far)):

        @pl.when((x == 0) & (core == 0) & (z == k))
        def _(block=block):
            out[WIDTH:, :] = block[:WIDTH, :]


def image_kernel(place, whole, high, low, near, own, front, back, far, sent, kept, across):
    image = (near[...] + turned_image(place, 2, far, high, low)).T
    block, half = 2 * (place[3] % 2) + place[2] // 2, place[2] % 2
    for k, piece in zip(around(place[1]), (own, front, back, far)):

        @pl.when((place[2] - k + 4) % 4 == block)
        def _(piece=piece):
            across[...] = piece[pl.ds(pl.multiple_of(half * 2 * PIECE, 16), 2 * PIECE), :]

    corner = whole[:WIDTH, :].T * jnp.where((place[0] == 0) & (place[1] == 0), 1.0, 0.0)
    for out, half in ((kept, place[1]), (sent, 1 - place[1])):
        for value in range(2):

            @pl.when(half == value)
            def _(out=out, value=value):
                for x in range(4):
                    index = (2 * x + value) * PIECE
                    out[x * PIECE : (x + 1) * PIECE, :] = image[index : index + PIECE, :]
                    out[(4 + x) * PIECE : (5 + x) * PIECE, :] = corner[index : index + PIECE, :]


def factor_kernel(g0, g1, g3, g2, upper, upper_here, normal, work):
    total = (g0[...] + g2[...]) + (g1[...] + g3[...])
    work[...] = total[:WIDTH, :]
    cholesky_rows(work, upper_here)
    factor = upper_here[...]
    upper[...] = factor
    normal[...] = total[:WIDTH, :] + full_dot(total[WIDTH:, :], factor, ((0,), (0,)))


def deal_kernel(place, kept, received, upper, m0, m1, m3, m2, image):
    half = kept[...] + received[...]
    image[...] = half[: 4 * PIECE, :] + split_dot(half[4 * PIECE :, :], upper[...], ((1,), (0,)))
    for k, out in ((0, m0), (1, m1), (3, m3), (2, m2)):
        start = pl.multiple_of(((place[0] + k) % 4) * PIECE, 16)
        out[...] = image[pl.ds(start, PIECE), :]


def sum_kernel(own, r1, r3, r2, image):
    image[...] = (own[...] + r2[...]) + (r1[...] + r3[...])


def untag_kernel(place, p0, p1, p3, p2, out):
    pieces = (p0, p1, p3, p2)
    put_in_order(place[0], ALONG, [p.at[:PIECE, :] for p in pieces], out, PIECE)
    put_in_order(place[0], ALONG, [p.at[PIECE:, :] for p in pieces], out, PIECE, 4 * PIECE)


def cholesky_rows(work, factor):
    lanes = lax.broadcasted_iota(jnp.int32, (1, WIDTH), 1)
    subs = lax.broadcasted_iota(jnp.int32, (8, 1), 0)

    def body(t, carry):
        first = pl.multiple_of(8 * t, 8)
        whole = work[...]
        block = work[pl.ds(first, 8), :]
        columns = [lane(whole, first + b) for b in range(8)]
        pivots = [lane(block, first + b) for b in range(8)]
        for i in range(8):
            row, pivot = block[i : i + 1], pivots[i][i : i + 1]
            inverse = 1.0 / pivot
            scaled = row * lax.rsqrt(pivot)
            factor[pl.ds(first + i, 1), :] = jnp.where(lanes >= first + i, scaled, 0.0)
            column, here = pivots[i], subs == i
            row = row * inverse
            block = jnp.where(here, row, block - column * row)
            for b in range(i + 1, 8):
                entry = pivots[b][i : i + 1] * inverse
                pivots[b] = jnp.where(here, entry, pivots[b] - column * entry)
        for i in range(8):
            whole = whole - columns[i] * block[i : i + 1]
        work[...] = whole
        return carry

    lax.fori_loop(0, WIDTH // 8, body, 0)


def inverse_kernel(source, out):
    out[...] = source[...]
    lanes = lax.broadcasted_iota(jnp.int32, (1, WIDTH), 1)
    subs = lax.broadcasted_iota(jnp.int32, (8, 1), 0)

    def body(t, carry):
        first = pl.multiple_of(8 * t, 8)
        whole = out[...]
        block = out[pl.ds(first, 8), :]
        columns = [lane(whole, first + b) for b in range(8)]
        pivots = [lane(block, first + b) for b in range(8)]
        for i in range(8):
            row, column, here = block[i : i + 1], pivots[i], subs == i
            inverse = 1.0 / column[i : i + 1]
            is_lane = lanes == first + i
            row = jnp.where(is_lane, inverse, row * inverse)
            block = jnp.where(here, row, jnp.where(is_lane, 0.0, block) - column * row)
            for b in range(8):
                if b != i:
                    entry = pivots[b][i : i + 1] * inverse
                    pivots[b] = jnp.where(here, entry, pivots[b] - column * entry)
            pivots[i] = jnp.where(here, inverse, -column * inverse)
        whole = jnp.where((lanes >= first) & (lanes < first + 8), 0.0, whole)
        for i in range(8):
            whole = whole - columns[i] * block[i : i + 1]
        out[...] = whole
        out[pl.ds(first, 8), :] = block
        return carry

    lax.fori_loop(0, WIDTH // 8, body, 0)


def pick_kernel(place, b0, b1, b3, b2, out):
    core, y = place[1], place[3]
    for part in range(2):
        wanted = (y - (2 * (1 - core) + part) + 4) % 4
        for k, block in zip(around(core), (b0, b1, b3, b2)):

            @pl.when(wanted == k)
            def _(block=block, part=part):
                out[part * 4 * PIECE : (part + 1) * 4 * PIECE, :] = block[...]


def gather_kernel(place, p0, p1, p3, p2, upper, b0, b1, b3, b2, swapped, shifted, image_rows, inner):
    x, core, z, y = place[0], place[1], place[2], place[3]
    first = jnp.where((x == 0) & (core == 0), 1.0, 0.0)
    put_in_order(z, around(core), (p0, p1, p3, p2), shifted, 4 * PIECE)
    shifted[:WIDTH, :] += upper[...] * first

    def put(block, offset, part, half):
        for other in range(4):
            start = pl.multiple_of((8 * part + 2 * other + half) * PIECE, 16)
            piece = offset + other * PIECE
            image_rows[pl.ds(start, PIECE), :] = block[piece : piece + PIECE, :]

    for part in range(2):
        wanted = (y - (2 * core + part) + 4) % 4
        for k, block in zip(around(core), (b0, b1, b3, b2)):

            @pl.when(wanted == k)
            def _(block=block, part=part):
                put(block, 0, part, core)

        put(swapped, part * 4 * PIECE, part, 1 - core)
    inner[...] = split_dot(shifted[...], image_rows[...], ((0,), (0,)))


def cols_of(place, own, swapped, target, part):
    for half, block in ((place[1], own), (1 - place[1], swapped)):
        for x in range(4):
            start = pl.multiple_of((2 * x + half) * PIECE, 16)
            piece = (4 * part + x) * PIECE
            target[pl.ds(start, PIECE), :] = block[piece : piece + PIECE, :]


def wide_dot(left, right):
    left_high, left_low = halves(left)
    right_high, right_low = halves(right)
    width = right.shape[1]
    both = dot16(left_high, jnp.concatenate([right_high, right_low], axis=1), ((1,), (0,)))
    return both[:, :width] + both[:, width:] + dot16(left_low, right_high, ((1,), (0,)))


def first_update_kernel(
    place, whole, shifted_rows, image_rows, own, swapped, upper, inverse,
    result, turned, panel_cols, image_cols, right_high, right_low, w_rows,
):
    cols_of(place, own, swapped, image_cols, 0)
    cols_of(place, own, swapped, panel_cols, 1)
    first = jnp.where((place[2] == 0) & (place[3] == 0), 1.0, 0.0)
    panel_cols[:WIDTH, :] += upper[...] * first
    turned[...] = panel_cols[...].T
    w_cols = wide_dot(image_cols[...], inverse[...])
    right_high[:WIDTH, :], right_low[:WIDTH, :] = halves(w_cols.T)
    right_high[WIDTH:, :], right_low[WIDTH:, :] = halves(turned[...])
    w_rows[...] = wide_dot(image_rows[...], inverse[...])
    dims = ((1,), (0,))
    for i in range(ROWS // WIDTH):
        rows = slice(i * WIDTH, (i + 1) * WIDTH)
        left_high, left_low = halves(jnp.concatenate([shifted_rows[rows, :], w_rows[rows, :]], axis=1))
        change = dot16(left_low, right_high[...], dims) + dot16(left_high, right_low[...], dims)
        result[rows, :] = whole[rows, :] - (change + dot16(left_high, right_high[...], dims))


def last_update_kernel(base, shifted_rows, turned, inverse, k0, k1, k3, k2, out, right, right_low, result, sems):
    inner = (k0[...] + k2[...]) + (k1[...] + k3[...])
    dims = ((1,), (0,))
    core_block = split_dot(split_dot(inverse[...], inner, ((0,), (0,))), inverse[...], dims)
    high, low = halves(split_dot(core_block, turned[...], dims))
    right[:WIDTH, :] = high
    right[WIDTH:, :] = high
    right_low[...] = low
    copies = []
    for i in range(ROWS // WIDTH):
        rows = slice(i * WIDTH, (i + 1) * WIDTH)
        left_high, left_low = halves(shifted_rows[rows, :])
        change = dot16(jnp.concatenate([left_high, left_low], axis=1), right[...], dims)
        result[rows, :] = base[rows, :] + (change + dot16(left_high, right_low[...], dims))
        rows = pl.ds(i * WIDTH, WIDTH)
        copies.append(pltpu.make_async_copy(result.at[rows, :], out.at[rows, :], sems.at[i]))
        copies[-1].start()
    for copy in copies:
        copy.wait()


def shape(rows, columns=WIDTH):
    return jax.ShapeDtypeStruct((rows, columns), F32)


def params(mib):
    return pltpu.CompilerParams(vmem_limit_bytes=mib * 1024 * 1024)


def local(kernel, out_shape, mib, scratch=(), flops=0):
    cost = pl.CostEstimate(flops=flops, bytes_accessed=0, transcendentals=0) if flops else None

    def run(*operands):
        specs = [SMEM if value.dtype == jnp.int32 else VMEM for value in operands]
        outs = [VMEM] * len(out_shape) if isinstance(out_shape, list) else VMEM
        return pl.pallas_call(
            kernel, in_specs=specs, out_specs=outs, out_shape=out_shape, scratch_shapes=list(scratch),
            compiler_params=params(mib), cost_estimate=cost,
        )(*operands)

    return run


def turn(axis, first):
    def where(x, core, z, y):
        return axis(first if core == 0 else 4 - first)(x, core, z, y)

    return where


def after(values, *earlier):
    return lax.optimization_barrier((values, earlier))[0]


def shards(panel, trailing):
    row, col = lax.axis_index("row"), lax.axis_index("col")
    place = jnp.stack([row // 2, row % 2, col // 4, col % 4]).astype(jnp.int32)
    anywhere = pl.BlockSpec(memory_space=pl.ANY)
    tile = shape(WIDTH)
    tile16 = jax.ShapeDtypeStruct((ROWS, COLS), BF16)

    with jax.named_scope("panel_y"):
        in_y = local(join_y_kernel, shape(4 * PIECE), 4)(place, panel, *ring(panel, along_y))
    with jax.named_scope("panel_z"):
        below, above = send(in_y, turn(along_z, 1)), send(in_y, turn(along_z, 3))
    with jax.named_scope("split"):
        whole, high, low = pl.pallas_call(
            split_kernel,
            in_specs=[anywhere, VMEM],
            out_specs=[VMEM] * 3,
            out_shape=[shape(ROWS, COLS), tile16, tile16],
            scratch_shapes=[pltpu.SemaphoreType.DMA((STEPS,))],
            compiler_params=params(24),
            cost_estimate=pl.CostEstimate(flops=0, bytes_accessed=4 * ROWS * COLS, transcendentals=0),
        )(trailing, in_y)
    below, above = after((below, above), whole)
    with jax.named_scope("panel_far"):
        far = send(below, turn(along_z, 1))
    with jax.named_scope("near"):
        near, gram, gram_near = local(near_kernel, [shape(WIDTH, COLS), tile, tile], 16, flops=5 * ROWS * COLS * WIDTH)(
            place, high, low, in_y, below, above
        )
    far = after(far, gram)
    in_z = [in_y, below, above, far]

    with jax.named_scope("gram"):
        gram = local(far_gram_kernel, shape(2 * WIDTH), 4)(place, *in_z, gram, gram_near)
    with jax.named_scope("gram_sum"):
        gram = gram + send(gram, other_core)
        grams = [gram] + ring(gram, along_x)
    with jax.named_scope("image"):
        sent, kept, across = local(
            image_kernel, [shape(8 * PIECE)] * 2 + [shape(2 * PIECE)], 24, flops=2 * ROWS * COLS * WIDTH
        )(place, whole, high, low, near, *after(in_z, gram))
    grams = after(grams, kept)
    with jax.named_scope("image_core"):
        received = send(after(sent, grams), other_core)
    with jax.named_scope("panel_across"):
        across = send(after(across, grams), planes(0))
    with jax.named_scope("factor"):
        upper, upper_here, normal = local(factor_kernel, [tile] * 3, 4, [pltpu.VMEM((WIDTH, WIDTH), F32)], 2000000000)(
            *grams
        )
    with jax.named_scope("deal"):
        m0, m1, m3, m2 = local(deal_kernel, [shape(PIECE)] * 4, 8, [pltpu.VMEM((4 * PIECE, WIDTH), F32)])(
            place, kept, received, upper_here
        )
    with jax.named_scope("image_x"):
        r1, r3, r2 = (send(m, along_x(k)) for m, k in ((m1, 1), (m3, 3), (m2, 2)))
    with jax.named_scope("panel_across"):
        handed = send(local(hand_kernel, shape(PIECE), 4)(place, after(across, m0)), other_core)
    r1, r3, r2, handed = after((r1, r3, r2, handed))
    with jax.named_scope("image_x"):
        image = local(sum_kernel, shape(PIECE), 4)(m0, r1, r3, r2)

    with jax.named_scope("image_planes"):
        planes_in = [send(image, planes(k)) for k in (0, 1, 3, 2)]
        in_plane = local(join_z_kernel, shape(4 * PIECE), 4)(place, *planes_in)
    with jax.named_scope("image_y"):
        below, above = send(in_plane, turn(along_y, 1)), send(in_plane, turn(along_y, 3))
    with jax.named_scope("image_columns"):
        tagged = local(tag_kernel, shape(2 * PIECE), 4)(place, image, across, after(handed, in_plane))
    with jax.named_scope("inverse"):
        inverse = local(inverse_kernel, tile, 4, flops=2000000000)(after(normal, in_plane))
    below, tagged = after((below, tagged), inverse)
    with jax.named_scope("image_far"):
        opposite = send(below, turn(along_y, 1))
    with jax.named_scope("image_columns"):
        sides = ring(after(tagged, below), along_x)
    blocks = [in_plane, below, above, opposite]
    with jax.named_scope("pick"):
        chosen = local(pick_kernel, shape(8 * PIECE), 8)(place, *blocks)
    with jax.named_scope("image_swap"):
        swapped = send(chosen, other_core)
    with jax.named_scope("image_columns"):
        own = local(untag_kernel, shape(8 * PIECE), 8)(place, tagged, *after(sides, chosen))
        other = send(own, other_core)
    with jax.named_scope("gather"):
        shifted, image_rows, inner = local(gather_kernel, [shape(ROWS), shape(ROWS), tile], 16)(
            place, *in_z, upper_here, *blocks, swapped
        )
    with jax.named_scope("inner"):
        inner = inner + send(inner, other_core)
        k1, k3, k2 = ring(inner, along_x)

    with jax.named_scope("first_update"):
        base, turned = local(
            first_update_kernel,
            [shape(ROWS, COLS), shape(WIDTH, COLS)],
            24,
            [
                pltpu.VMEM((COLS, WIDTH), F32),
                pltpu.VMEM((COLS, WIDTH), F32),
                pltpu.VMEM((2 * WIDTH, COLS), BF16),
                pltpu.VMEM((2 * WIDTH, COLS), BF16),
                pltpu.VMEM((ROWS, WIDTH), F32),
            ],
            12 * ROWS * COLS * WIDTH,
        )(place, whole, shifted, image_rows, own, other, upper_here, after(inverse, inner))
    k1, k3, k2 = after((k1, k3, k2), base)
    with jax.named_scope("last_update"):
        updated = pl.pallas_call(
            last_update_kernel,
            in_specs=[VMEM] * 8,
            out_specs=anywhere,
            out_shape=shape(ROWS, COLS),
            scratch_shapes=[
                pltpu.VMEM((2 * WIDTH, COLS), BF16),
                pltpu.VMEM((WIDTH, COLS), BF16),
                pltpu.VMEM((ROWS, COLS), F32),
                pltpu.SemaphoreType.DMA((ROWS // WIDTH,)),
            ],
            compiler_params=params(20),
            cost_estimate=pl.CostEstimate(flops=8 * ROWS * COLS * WIDTH, bytes_accessed=4 * ROWS * COLS, transcendentals=0),
        )(base, shifted, turned, inverse, inner, k1, k3, k2)
    return upper, updated


def solution(mesh):
    return jax.shard_map(
        shards,
        mesh=mesh,
        in_specs=(P(("row", "col"), None), P("row", "col")),
        out_specs=(P(), P("row", "col")),
        check_vma=False,
    )
```

time: 136 us -> 124 us (0.912)
  waiting for transfers between devices: 58.5 us -> 22.3 us
  starting transfers between devices: 38.4 us -> 61 us
  Pallas kernels: 31.9 us -> 38.6 us
  local copies, waits for them, and re-layouts: 5.9 us -> 0.88 us
    ppermute x31 -> x32, waiting for transfers between devices: 58.5 us -> 22.3 us  [send(): return lax.ppermute(value, AXES, pairs(where))]
    ppermute x31 -> x32, starting transfers between devices: 38.4 us -> 61 us  [send(): return lax.ppermute(value, AXES, pairs(where))]
    pallas_call x7 -> x17, Pallas kernels: 31.9 us -> 38.6 us  [the longest x15 29.1 us: run(): pl.pallas_call(kernel, in_specs=specs, out_specs=outs, out_shape=out_shap...]
    unnamed x26 -> x2, local copies, waits for them, and re-layouts: 5.87 us -> 0.88 us
  transfers between devices with their start and end apart: 31 -> 32, of which waited for: 13 -> 13; matrix products, arithmetic and copies ran while one was open for 1% -> 0% of each run, Pallas kernels for 9% -> 25%
where the time goes in v2:
time: 124 us
  starting transfers between devices  61 us (49%)
  Pallas kernels  38.6 us (31%)
  waiting for transfers between devices  22.3 us (18%)
    ppermute x32, starting transfers between devices, send(): return lax.ppermute(value, AXES, pairs(where))  61 us
    pallas_call x15, Pallas kernels, run(): pl.pallas_call(kernel, in_specs=specs, out_specs=outs, out_shape=out_shap...  29.1 us
    ppermute x32, waiting for transfers between devices, send(): return lax.ppermute(value, AXES, pairs(where))  22.3 us
    pallas_call x1, Pallas kernels, shards(): pl.pallas_call(last_update_kernel, in_specs=[VMEM] * 8, out_specs=anywher...  5.21 us
    pallas_call x1, Pallas kernels, shards(): pl.pallas_call(split_kernel, in_specs=[anywhere, VMEM], out_specs=[VMEM]...  4.3 us
  transfers between devices with their start and end apart: 32, of which 13 were waited for; matrix products, arithmetic and copies ran while one was open for 0% of the time, Pallas kernels for 25%

profile of v2, /device:TPU:1, one launch (start us, length us, event | category | flops | bytes accessed | tf_op | source)
XLA Modules:
  0.0 123.9 jit_solution(3045834417378845694)
XLA Ops:
  0.6 3.6 %collective-permute-start.1 = (f32[144,128]{1,0:T(8,128)}, f32[144,128]{1,0:T(8,128)S(1)}, u32[]{:S(2)}, u32[]{:S(2)}) collective-permute-start(f32[144,128]{1,0:T(8,128)} %p0.1), channel_id=1, source_target_pairs={{0,3},{1,0},{2,1},{3,2},{4,7},{5,4},{6,5},{7,6},{8,11},{9,8},{10,9... | collective-permute-start | bytes 221192 | tf_op jit(solution)/shard_map/panel_y/ppermute | solution.py:35
  4.3 1.6 %collective-permute-start.2 = (f32[144,128]{1,0:T(8,128)}, f32[144,128]{1,0:T(8,128)S(1)}, u32[]{:S(2)}, u32[]{:S(2)}) collective-permute-start(f32[144,128]{1,0:T(8,128)} %p0.1), channel_id=1, source_target_pairs={{0,2},{1,3},{2,0},{3,1},{4,6},{5,7},{6,4},{7,5},{8,10},{9,11},{10,... | collective-permute-start | bytes 221192 | tf_op jit(solution)/shard_map/panel_y/ppermute | solution.py:35
  6.0 3.5 %collective-permute-done.p1 = f32[144,128]{1,0:T(8,128)S(1)} collective-permute-done((f32[144,128]{1,0:T(8,128)}, f32[144,128]{1,0:T(8,128)S(1)}, u32[]{:S(2)}, u32[]{:S(2)}) %collective-permute-start) | collective-permute-done | bytes 73760 | tf_op jit(solution)/shard_map/panel_y/ppermute | solution.py:35
  9.9 0.9 copy-done
  11.3 1.7 %collective-permute-start.4 = (f32[576,128]{1,0:T(8,128)S(1)}, f32[576,128]{1,0:T(8,128)S(1)}, u32[]{:S(2)}, u32[]{:S(2)}) collective-permute-start(f32[576,128]{1,0:T(8,128)S(1)} %panel_y.1.after.own.p0), channel_id=1, source_target_pairs={{0,12},{1,13},{2,14},{3,15},{4,0},{5,1},{6,2},{7,3},{8,4},{9,5},{1... | collective-permute-start | bytes 884744 | tf_op jit(solution)/shard_map/panel_z/ppermute | solution.py:35
  13.1 2.2 %collective-permute-start.3 = (f32[576,128]{1,0:T(8,128)S(1)}, f32[576,128]{1,0:T(8,128)S(1)}, u32[]{:S(2)}, u32[]{:S(2)}) collective-permute-start(f32[576,128]{1,0:T(8,128)S(1)} %panel_y.1.after.own.p0), channel_id=1, source_target_pairs={{0,4},{1,5},{2,6},{3,7},{4,8},{5,9},{6,10},{7,11},{8,12},{9,13},{1... | collective-permute-start | bytes 884744 | tf_op jit(solution)/shard_map/panel_z/ppermute | solution.py:35
  15.3 4.3 %split.1 = (f32[2304,1152]{1,0:T(8,128)S(1)}, bf16[2304,1152]{1,0:T(8,128)(2,1)S(1)}, bf16[2304,1152]{1,0:T(8,128)(2,1)S(1)}) custom-call(f32[2304,1152]{1,0:T(8,128)} %trailing.1, f32[576,128]{1,0:T(8,128)S(1)} %panel_y.1.after.own.p0), custom_call_target="tpu_custom_call" | custom-call | bytes 10616832 | tf_op jit(solution)/shard_map/split/pallas_call | solution.py:414
  19.6 2.0 %collective-permute-done.3.front.below.p1 = f32[576,128]{1,0:T(8,128)S(1)} collective-permute-done((f32[576,128]{1,0:T(8,128)S(1)}, f32[576,128]{1,0:T(8,128)S(1)}, u32[]{:S(2)}, u32[]{:S(2)}) %collective-permute-start.3) | collective-permute-done | bytes 294944 | tf_op jit(solution)/shard_map/panel_z/ppermute | solution.py:35
  21.6 1.4 %collective-permute-start.5 = (f32[576,128]{1,0:T(8,128)S(1)}, f32[576,128]{1,0:T(8,128)S(1)}, u32[]{:S(2)}, u32[]{:S(2)}) collective-permute-start(f32[576,128]{1,0:T(8,128)S(1)} %collective-permute-done.3.front.below.p1), channel_id=1, source_target_pairs={{0,4},{1,5},{2,6},{3,7},{4,8},{5,9},{6,10},{7,11},{8,12},{9,13},{1... | collective-permute-start | bytes 884744 | tf_op jit(solution)/shard_map/panel_far/ppermute | solution.py:35
  23.0 3.9 %near.1 = (f32[128,1152]{1,0:T(8,128)S(1)}, f32[128,128]{1,0:T(8,128)S(1)}, f32[128,128]{1,0:T(8,128)S(1)}) custom-call(s32[4]{0:T(128)S(1)} %pad_add_fusion.place, bf16[2304,1152]{1,0:T(8,128)(2,1)S(1)} %get-tuple-element.56.high, bf16[2304,1152]{1,0:T(8,128)(2,1)S(1)} %get-tuple-element.57.low, f32[576,128]{1,0:T(8,128)S(1)} %panel_y.1.after.own.p0, ...), custom_call_target="tpu_custom_call" | custom-call | flops 1698693120 | tf_op jit(solution)/shard_map/near/pallas_call | solution.py:383
  27.1 1.0 gram.1
  28.2 6.4 %collective-permute-start.6 = (f32[256,128]{1,0:T(8,128)S(1)}, f32[256,128]{1,0:T(8,128)S(1)}, u32[]{:S(2)}, u32[]{:S(2)}) collective-permute-start(f32[256,128]{1,0:T(8,128)S(1)} %gram.1), channel_id=1, source_target_pairs={{0,16},{1,17},{2,18},{3,19},{4,20},{5,21},{6,22},{7,23},{8,24},{9,... | collective-permute-start | bytes 393224 | tf_op jit(solution)/shard_map/gram_sum/ppermute | solution.py:35
  34.5 1.0 collective-permute-done.6
  35.5 2.8 %collective-permute-start.9 = (f32[256,128]{1,0:T(8,128)S(1)}, f32[256,128]{1,0:T(8,128)S(1)}, u32[]{:S(2)}, u32[]{:S(2)}) collective-permute-start(f32[256,128]{1,0:T(8,128)S(1)} %add.17.g0), channel_id=1, source_target_pairs={{0,64},{1,65},{2,66},{3,67},{4,68},{5,69},{6,70},{7,71},{8,72},{9,... | collective-permute-start | bytes 393224 | tf_op jit(solution)/shard_map/gram_sum/ppermute | solution.py:35
  38.4 0.9 collective-permute-start.8
  39.2 0.6 collective-permute-start.7
  39.8 1.9 %image.1 = (f32[1152,128]{1,0:T(8,128)S(1)}, f32[1152,128]{1,0:T(8,128)S(1)}, f32[288,128]{1,0:T(8,128)S(1)}) custom-call(s32[4]{0:T(128)S(1)} %pad_add_fusion.place, f32[2304,1152]{1,0:T(8,128)S(1)} %get-tuple-element.53.whole, bf16[2304,1152]{1,0:T(8,128)(2,1)S(1)} %get-tuple-element.56.high, bf16[2304,1152]{1,0:T(8,128)(2,1)S(1)} %get-tuple-element.57.low, ...), custom_call_target="tpu_custom_call" | custom-call | flops 679477248 | tf_op jit(solution)/shard_map/image/pallas_call | solution.py:383
  41.8 2.9 %collective-permute-done.8.g3 = f32[256,128]{1,0:T(8,128)S(1)} collective-permute-done((f32[256,128]{1,0:T(8,128)S(1)}, f32[256,128]{1,0:T(8,128)S(1)}, u32[]{:S(2)}, u32[]{:S(2)}) %collective-permute-start.8) | collective-permute-done | bytes 131104 | tf_op jit(solution)/shard_map/gram_sum/ppermute | solution.py:35
  44.8 1.7 %collective-permute-start.10 = (f32[1152,128]{1,0:T(8,128)S(1)}, f32[1152,128]{1,0:T(8,128)S(1)}, u32[]{:S(2)}, u32[]{:S(2)}) collective-permute-start(f32[1152,128]{1,0:T(8,128)S(1)} %get-tuple-element.74), channel_id=1, source_target_pairs={{0,16},{1,17},{2,18},{3,19},{4,20},{5,21},{6,22},{7,23},{8,24},{9,... | collective-permute-start | bytes 1769480 | tf_op jit(solution)/shard_map/image_core/ppermute | solution.py:35
  46.5 0.7 collective-permute-start.14
  47.1 5.3 %factor.1 = (f32[128,128]{1,0:T(8,128)}, f32[128,128]{1,0:T(8,128)S(1)}, f32[128,128]{1,0:T(8,128)S(1)}) custom-call(f32[256,128]{1,0:T(8,128)S(1)} %add.17.g0, f32[256,128]{1,0:T(8,128)S(1)} %collective-permute-done.7.g1, f32[256,128]{1,0:T(8,128)S(1)} %collective-permute-done.8.g3, f32[256,128]{1,0:T(8,128)S(1)} %collective-permute-done.9.g2), custom_call_target="tpu_custom_call" | custom-call | flops 2000000000 | tf_op jit(solution)/shard_map/factor/pallas_call | solution.py:383
  52.4 0.8 deal.1
  53.9 6.0 %collective-permute-start.11 = (f32[144,128]{1,0:T(8,128)S(1)}, f32[144,128]{1,0:T(8,128)S(1)}, u32[]{:S(2)}, u32[]{:S(2)}) collective-permute-start(f32[144,128]{1,0:T(8,128)S(1)} %get-tuple-element.76), channel_id=1, source_target_pairs={{0,32},{1,33},{2,34},{3,35},{4,36},{5,37},{6,38},{7,39},{8,40},{9,... | collective-permute-start | bytes 221192 | tf_op jit(solution)/shard_map/image_x/ppermute | solution.py:35
  59.9 2.2 %collective-permute-start.12 = (f32[144,128]{1,0:T(8,128)S(1)}, f32[144,128]{1,0:T(8,128)S(1)}, u32[]{:S(2)}, u32[]{:S(2)}) collective-permute-start(f32[144,128]{1,0:T(8,128)S(1)} %get-tuple-element.77), channel_id=1, source_target_pairs={{0,96},{1,97},{2,98},{3,99},{4,100},{5,101},{6,102},{7,103},{8,104... | collective-permute-start | bytes 221192 | tf_op jit(solution)/shard_map/image_x/ppermute | solution.py:35
  62.1 1.2 collective-permute-start.13
  63.3 1.4 %collective-permute-done.11.r1 = f32[144,128]{1,0:T(8,128)S(1)} collective-permute-done((f32[144,128]{1,0:T(8,128)S(1)}, f32[144,128]{1,0:T(8,128)S(1)}, u32[]{:S(2)}, u32[]{:S(2)}) %collective-permute-start.11) | collective-permute-done | bytes 73760 | tf_op jit(solution)/shard_map/image_x/ppermute | solution.py:35
  64.7 2.2 %collective-permute-done.13.r2 = f32[144,128]{1,0:T(8,128)S(1)} collective-permute-done((f32[144,128]{1,0:T(8,128)S(1)}, f32[144,128]{1,0:T(8,128)S(1)}, u32[]{:S(2)}, u32[]{:S(2)}) %collective-permute-start.13) | collective-permute-done | bytes 73760 | tf_op jit(solution)/shard_map/image_x/ppermute | solution.py:35
  66.8 0.9 collective-permute-start.19
  67.7 2.0 %collective-permute-start.18 = (f32[144,128]{1,0:T(8,128)S(1)}, f32[144,128]{1,0:T(8,128)S(1)}, u32[]{:S(2)}, u32[]{:S(2)}) collective-permute-start(f32[144,128]{1,0:T(8,128)S(1)} %image_x.1.image), channel_id=1, source_target_pairs={{0,12},{1,13},{2,14},{3,15},{4,44},{5,45},{6,46},{7,47},{8,76},{9,... | collective-permute-start | bytes 221192 | tf_op jit(solution)/shard_map/image_planes/ppermute | solution.py:35
  69.7 1.7 %collective-permute-start.17 = (f32[144,128]{1,0:T(8,128)S(1)}, f32[144,128]{1,0:T(8,128)S(1)}, u32[]{:S(2)}, u32[]{:S(2)}) collective-permute-start(f32[144,128]{1,0:T(8,128)S(1)} %image_x.1.image), channel_id=1, source_target_pairs={{0,4},{1,5},{2,6},{3,7},{4,36},{5,37},{6,38},{7,39},{8,68},{9,69},... | collective-permute-start | bytes 221192 | tf_op jit(solution)/shard_map/image_planes/ppermute | solution.py:35
  71.5 0.7 collective-permute-start.16
  72.4 7.1 %collective-permute-done.17.p1 = f32[144,128]{1,0:T(8,128)S(1)} collective-permute-done((f32[144,128]{1,0:T(8,128)S(1)}, f32[144,128]{1,0:T(8,128)S(1)}, u32[]{:S(2)}, u32[]{:S(2)}) %collective-permute-start.17) | collective-permute-done | bytes 73760 | tf_op jit(solution)/shard_map/image_planes/ppermute | solution.py:35
  80.1 2.3 %collective-permute-start.20 = (f32[576,128]{1,0:T(8,128)S(1)}, f32[576,128]{1,0:T(8,128)S(1)}, u32[]{:S(2)}, u32[]{:S(2)}) collective-permute-start(f32[576,128]{1,0:T(8,128)S(1)} %image_planes.1.b0), channel_id=1, source_target_pairs={{0,1},{1,2},{2,3},{3,0},{4,5},{5,6},{6,7},{7,4},{8,9},{9,10},{10,1... | collective-permute-start | bytes 884744 | tf_op jit(solution)/shard_map/image_y/ppermute | solution.py:35
  83.0 4.7 %inverse.1 = f32[128,128]{1,0:T(8,128)S(1)} custom-call(f32[128,128]{1,0:T(8,128)S(1)} %get-tuple-element.88.source), custom_call_target="tpu_custom_call" | custom-call | flops 2000000000 | tf_op jit(solution)/shard_map/inverse/pallas_call | solution.py:383
  87.7 2.7 %collective-permute-start.22 = (f32[576,128]{1,0:T(8,128)S(1)}, f32[576,128]{1,0:T(8,128)S(1)}, u32[]{:S(2)}, u32[]{:S(2)}) collective-permute-start(f32[576,128]{1,0:T(8,128)S(1)} %collective-permute-done.20.b1), channel_id=1, source_target_pairs={{0,1},{1,2},{2,3},{3,0},{4,5},{5,6},{6,7},{7,4},{8,9},{9,10},{10,1... | collective-permute-start | bytes 884744 | tf_op jit(solution)/shard_map/image_far/ppermute | solution.py:35
  90.4 2.9 %collective-permute-start.26 = (f32[288,128]{1,0:T(8,128)S(1)}, f32[288,128]{1,0:T(8,128)S(1)}, u32[]{:S(2)}, u32[]{:S(2)}) collective-permute-start(f32[288,128]{1,0:T(8,128)S(1)} %image_columns.2.p0), channel_id=1, source_target_pairs={{0,64},{1,65},{2,66},{3,67},{4,68},{5,69},{6,70},{7,71},{8,72},{9,... | collective-permute-start | bytes 442376 | tf_op jit(solution)/shard_map/image_columns/ppermute | solution.py:35
  93.4 2.3 %collective-permute-start.25 = (f32[288,128]{1,0:T(8,128)S(1)}, f32[288,128]{1,0:T(8,128)S(1)}, u32[]{:S(2)}, u32[]{:S(2)}) collective-permute-start(f32[288,128]{1,0:T(8,128)S(1)} %image_columns.2.p0), channel_id=1, source_target_pairs={{0,96},{1,97},{2,98},{3,99},{4,100},{5,101},{6,102},{7,103},{8,104... | collective-permute-start | bytes 442376 | tf_op jit(solution)/shard_map/image_columns/ppermute | solution.py:35
  95.7 0.6 collective-permute-start.24
  96.3 0.6 pick.1
  96.9 4.8 %collective-permute-start.23 = (f32[1152,128]{1,0:T(8,128)S(1)}, f32[1152,128]{1,0:T(8,128)S(1)}, u32[]{:S(2)}, u32[]{:S(2)}) collective-permute-start(f32[1152,128]{1,0:T(8,128)S(1)} %pick.1), channel_id=1, source_target_pairs={{0,16},{1,17},{2,18},{3,19},{4,20},{5,21},{6,22},{7,23},{8,24},{9,... | collective-permute-start | bytes 1769480 | tf_op jit(solution)/shard_map/image_swap/ppermute | solution.py:35
  101.7 0.6 image_columns.3.own
  102.3 3.2 %collective-permute-start.27 = (f32[1152,128]{1,0:T(8,128)S(1)}, f32[1152,128]{1,0:T(8,128)S(1)}, u32[]{:S(2)}, u32[]{:S(2)}) collective-permute-start(f32[1152,128]{1,0:T(8,128)S(1)} %image_columns.3.own), channel_id=1, source_target_pairs={{0,16},{1,17},{2,18},{3,19},{4,20},{5,21},{6,22},{7,23},{8,24},{9,... | collective-permute-start | bytes 1769480 | tf_op jit(solution)/shard_map/image_columns/ppermute | solution.py:35
  105.6 1.5 %gather.1 = (f32[2304,128]{1,0:T(8,128)S(1)}, f32[2304,128]{1,0:T(8,128)S(1)}, f32[128,128]{1,0:T(8,128)S(1)}) custom-call(s32[4]{0:T(128)S(1)} %pad_add_fusion.place, f32[576,128]{1,0:T(8,128)S(1)} %panel_y.1.after.own.p0, f32[576,128]{1,0:T(8,128)S(1)} %collective-permute-done.3.front.below.p1, f32[576,128]{1,0:T(8,128)S(1)} %collective-permute-done.4.back.above.p3, ...), custom_call_target="tpu_custom_call" | custom-call | tf_op jit(solution)/shard_map/gather/pallas_call | solution.py:383
  107.1 1.2 collective-permute-done.28
  108.4 1.5 %collective-permute-start.31 = (f32[128,128]{1,0:T(8,128)S(1)}, f32[128,128]{1,0:T(8,128)S(1)}, u32[]{:S(2)}, u32[]{:S(2)}) collective-permute-start(f32[128,128]{1,0:T(8,128)S(1)} %add.18.k0), channel_id=1, source_target_pairs={{0,64},{1,65},{2,66},{3,67},{4,68},{5,69},{6,70},{7,71},{8,72},{9,... | collective-permute-start | bytes 196616 | tf_op jit(solution)/shard_map/inner/ppermute | solution.py:35
  109.9 1.6 %collective-permute-start.30 = (f32[128,128]{1,0:T(8,128)S(1)}, f32[128,128]{1,0:T(8,128)S(1)}, u32[]{:S(2)}, u32[]{:S(2)}) collective-permute-start(f32[128,128]{1,0:T(8,128)S(1)} %add.18.k0), channel_id=1, source_target_pairs={{0,96},{1,97},{2,98},{3,99},{4,100},{5,101},{6,102},{7,103},{8,104... | collective-permute-start | bytes 196616 | tf_op jit(solution)/shard_map/inner/ppermute | solution.py:35
  112.0 6.4 %first_update.1 = (f32[2304,1152]{1,0:T(8,128)S(1)}, f32[128,1152]{1,0:T(8,128)S(1)}) custom-call(s32[4]{0:T(128)S(1)} %pad_add_fusion.place, f32[2304,1152]{1,0:T(8,128)S(1)} %get-tuple-element.53.whole, f32[2304,128]{1,0:T(8,128)S(1)} %get-tuple-element.90.shifted_rows, f32[2304,128]{1,0:T(8,128)S(1)} %get-tuple-element.91.image_rows, ...), custom_call_target="tpu_custom_call" | custom-call | flops 4076863488 | tf_op jit(solution)/shard_map/first_update/pallas_call | solution.py:383
  118.5 5.2 %last_update.1 = f32[2304,1152]{1,0:T(8,128)} custom-call(f32[2304,1152]{1,0:T(8,128)S(1)} %get-tuple-element.99.base, f32[2304,128]{1,0:T(8,128)S(1)} %get-tuple-element.90.shifted_rows, f32[128,1152]{1,0:T(8,128)S(1)} %get-tuple-element.100.turned, f32[128,128]{1,0:T(8,128)S(1)} %inverse.1, f32[128,128]{1,0:T(8,128)S(1)} %add.18.k0, ...), custom_call_target="tpu_custom_call" | custom-call | flops 2717908992 | bytes 10616832 | tf_op jit(solution)/shard_map/last_update/pallas_call | solution.py:509
  (38 shorter events, 4.2 us)
Async XLA Ops:
  0.6 5.4 %collective-permute-start.1 = (f32[144,128]{1,0:T(8,128)}, f32[144,128]{1,0:T(8,128)S(1)}, u32[]{:S(2)}, u32[]{:S(2)}) collective-permute-start(f32[144,128]{1,0:T(8,128)} %p0.1), channel_id=1, source_target_pairs={{0,3},{1,0},{2,1},{3,2},{4,7},{5,4},{6,5},{7,6},{8,11},{9,8},{10,9... | collective-permute-start | bytes 221192 | tf_op jit(solution)/shard_map/panel_y/ppermute | solution.py:35
  4.3 5.2 %collective-permute-start = (f32[144,128]{1,0:T(8,128)}, f32[144,128]{1,0:T(8,128)S(1)}, u32[]{:S(2)}, u32[]{:S(2)}) collective-permute-start(f32[144,128]{1,0:T(8,128)} %p0.1), channel_id=1, source_target_pairs={{0,1},{1,2},{2,3},{3,0},{4,5},{5,6},{6,7},{7,4},{8,9},{9,10},{10,1... | collective-permute-start | bytes 221192 | tf_op jit(solution)/shard_map/panel_y/ppermute | solution.py:35
  4.3 5.6 %collective-permute-start.2 = (f32[144,128]{1,0:T(8,128)}, f32[144,128]{1,0:T(8,128)S(1)}, u32[]{:S(2)}, u32[]{:S(2)}) collective-permute-start(f32[144,128]{1,0:T(8,128)} %p0.1), channel_id=1, source_target_pairs={{0,2},{1,3},{2,0},{3,1},{4,6},{5,7},{6,4},{7,5},{8,10},{9,11},{10,... | collective-permute-start | bytes 221192 | tf_op jit(solution)/shard_map/panel_y/ppermute | solution.py:35
  9.9 0.9 copy-start
  11.3 8.2 %collective-permute-start.4 = (f32[576,128]{1,0:T(8,128)S(1)}, f32[576,128]{1,0:T(8,128)S(1)}, u32[]{:S(2)}, u32[]{:S(2)}) collective-permute-start(f32[576,128]{1,0:T(8,128)S(1)} %panel_y.1.after.own.p0), channel_id=1, source_target_pairs={{0,12},{1,13},{2,14},{3,15},{4,0},{5,1},{6,2},{7,3},{8,4},{9,5},{1... | collective-permute-start | bytes 884744 | tf_op jit(solution)/shard_map/panel_z/ppermute | solution.py:35
  13.1 8.5 %collective-permute-start.3 = (f32[576,128]{1,0:T(8,128)S(1)}, f32[576,128]{1,0:T(8,128)S(1)}, u32[]{:S(2)}, u32[]{:S(2)}) collective-permute-start(f32[576,128]{1,0:T(8,128)S(1)} %panel_y.1.after.own.p0), channel_id=1, source_target_pairs={{0,4},{1,5},{2,6},{3,7},{4,8},{5,9},{6,10},{7,11},{8,12},{9,13},{1... | collective-permute-start | bytes 884744 | tf_op jit(solution)/shard_map/panel_z/ppermute | solution.py:35
  21.6 5.6 %collective-permute-start.5 = (f32[576,128]{1,0:T(8,128)S(1)}, f32[576,128]{1,0:T(8,128)S(1)}, u32[]{:S(2)}, u32[]{:S(2)}) collective-permute-start(f32[576,128]{1,0:T(8,128)S(1)} %collective-permute-done.3.front.below.p1), channel_id=1, source_target_pairs={{0,4},{1,5},{2,6},{3,7},{4,8},{5,9},{6,10},{7,11},{8,12},{9,13},{1... | collective-permute-start | bytes 884744 | tf_op jit(solution)/shard_map/panel_far/ppermute | solution.py:35
  28.2 7.3 %collective-permute-start.6 = (f32[256,128]{1,0:T(8,128)S(1)}, f32[256,128]{1,0:T(8,128)S(1)}, u32[]{:S(2)}, u32[]{:S(2)}) collective-permute-start(f32[256,128]{1,0:T(8,128)S(1)} %gram.1), channel_id=1, source_target_pairs={{0,16},{1,17},{2,18},{3,19},{4,20},{5,21},{6,22},{7,23},{8,24},{9,... | collective-permute-start | bytes 393224 | tf_op jit(solution)/shard_map/gram_sum/ppermute | solution.py:35
  35.5 6.3 %collective-permute-start.9 = (f32[256,128]{1,0:T(8,128)S(1)}, f32[256,128]{1,0:T(8,128)S(1)}, u32[]{:S(2)}, u32[]{:S(2)}) collective-permute-start(f32[256,128]{1,0:T(8,128)S(1)} %add.17.g0), channel_id=1, source_target_pairs={{0,64},{1,65},{2,66},{3,67},{4,68},{5,69},{6,70},{7,71},{8,72},{9,... | collective-permute-start | bytes 393224 | tf_op jit(solution)/shard_map/gram_sum/ppermute | solution.py:35
  38.4 6.4 %collective-permute-start.8 = (f32[256,128]{1,0:T(8,128)S(1)}, f32[256,128]{1,0:T(8,128)S(1)}, u32[]{:S(2)}, u32[]{:S(2)}) collective-permute-start(f32[256,128]{1,0:T(8,128)S(1)} %add.17.g0), channel_id=1, source_target_pairs={{0,96},{1,97},{2,98},{3,99},{4,100},{5,101},{6,102},{7,103},{8,104... | collective-permute-start | bytes 393224 | tf_op jit(solution)/shard_map/gram_sum/ppermute | solution.py:35
  39.2 5.6 %collective-permute-start.7 = (f32[256,128]{1,0:T(8,128)S(1)}, f32[256,128]{1,0:T(8,128)S(1)}, u32[]{:S(2)}, u32[]{:S(2)}) collective-permute-start(f32[256,128]{1,0:T(8,128)S(1)} %add.17.g0), channel_id=1, source_target_pairs={{0,32},{1,33},{2,34},{3,35},{4,36},{5,37},{6,38},{7,39},{8,40},{9,... | collective-permute-start | bytes 393224 | tf_op jit(solution)/shard_map/gram_sum/ppermute | solution.py:35
  44.8 7.6 %collective-permute-start.10 = (f32[1152,128]{1,0:T(8,128)S(1)}, f32[1152,128]{1,0:T(8,128)S(1)}, u32[]{:S(2)}, u32[]{:S(2)}) collective-permute-start(f32[1152,128]{1,0:T(8,128)S(1)} %get-tuple-element.74), channel_id=1, source_target_pairs={{0,16},{1,17},{2,18},{3,19},{4,20},{5,21},{6,22},{7,23},{8,24},{9,... | collective-permute-start | bytes 1769480 | tf_op jit(solution)/shard_map/image_core/ppermute | solution.py:35
  46.5 6.8 %collective-permute-start.14 = (f32[288,128]{1,0:T(8,128)S(1)}, f32[288,128]{1,0:T(8,128)S(1)}, u32[]{:S(2)}, u32[]{:S(2)}) collective-permute-start(f32[288,128]{1,0:T(8,128)S(1)} %get-tuple-element.80), channel_id=1, source_target_pairs={{0,0},{1,1},{2,2},{3,3},{4,32},{5,33},{6,34},{7,35},{8,64},{9,65},... | collective-permute-start | bytes 442376 | tf_op jit(solution)/shard_map/panel_across/ppermute | solution.py:35
  53.8 9.5 %collective-permute-start.15 = (f32[144,128]{1,0:T(8,128)S(1)}, f32[144,128]{1,0:T(8,128)S(1)}, u32[]{:S(2)}, u32[]{:S(2)}) collective-permute-start(f32[144,128]{1,0:T(8,128)S(1)} %panel_across.1), channel_id=1, source_target_pairs={{0,16},{1,17},{2,18},{3,19},{4,20},{5,21},{6,22},{7,23},{8,24},{9,... | collective-permute-start | bytes 221192 | tf_op jit(solution)/shard_map/panel_across/ppermute | solution.py:35
  53.9 10.7 %collective-permute-start.11 = (f32[144,128]{1,0:T(8,128)S(1)}, f32[144,128]{1,0:T(8,128)S(1)}, u32[]{:S(2)}, u32[]{:S(2)}) collective-permute-start(f32[144,128]{1,0:T(8,128)S(1)} %get-tuple-element.76), channel_id=1, source_target_pairs={{0,32},{1,33},{2,34},{3,35},{4,36},{5,37},{6,38},{7,39},{8,40},{9,... | collective-permute-start | bytes 221192 | tf_op jit(solution)/shard_map/image_x/ppermute | solution.py:35
  59.9 4.7 %collective-permute-start.12 = (f32[144,128]{1,0:T(8,128)S(1)}, f32[144,128]{1,0:T(8,128)S(1)}, u32[]{:S(2)}, u32[]{:S(2)}) collective-permute-start(f32[144,128]{1,0:T(8,128)S(1)} %get-tuple-element.77), channel_id=1, source_target_pairs={{0,96},{1,97},{2,98},{3,99},{4,100},{5,101},{6,102},{7,103},{8,104... | collective-permute-start | bytes 221192 | tf_op jit(solution)/shard_map/image_x/ppermute | solution.py:35
  62.1 4.7 %collective-permute-start.13 = (f32[144,128]{1,0:T(8,128)S(1)}, f32[144,128]{1,0:T(8,128)S(1)}, u32[]{:S(2)}, u32[]{:S(2)}) collective-permute-start(f32[144,128]{1,0:T(8,128)S(1)} %get-tuple-element.78), channel_id=1, source_target_pairs={{0,64},{1,65},{2,66},{3,67},{4,68},{5,69},{6,70},{7,71},{8,72},{9,... | collective-permute-start | bytes 221192 | tf_op jit(solution)/shard_map/image_x/ppermute | solution.py:35
  66.8 5.3 %collective-permute-start.19 = (f32[144,128]{1,0:T(8,128)S(1)}, f32[144,128]{1,0:T(8,128)S(1)}, u32[]{:S(2)}, u32[]{:S(2)}) collective-permute-start(f32[144,128]{1,0:T(8,128)S(1)} %image_x.1.image), channel_id=1, source_target_pairs={{0,8},{1,9},{2,10},{3,11},{4,40},{5,41},{6,42},{7,43},{8,72},{9,73... | collective-permute-start | bytes 221192 | tf_op jit(solution)/shard_map/image_planes/ppermute | solution.py:35
  67.7 4.7 %collective-permute-start.18 = (f32[144,128]{1,0:T(8,128)S(1)}, f32[144,128]{1,0:T(8,128)S(1)}, u32[]{:S(2)}, u32[]{:S(2)}) collective-permute-start(f32[144,128]{1,0:T(8,128)S(1)} %image_x.1.image), channel_id=1, source_target_pairs={{0,12},{1,13},{2,14},{3,15},{4,44},{5,45},{6,46},{7,47},{8,76},{9,... | collective-permute-start | bytes 221192 | tf_op jit(solution)/shard_map/image_planes/ppermute | solution.py:35
  69.7 9.8 %collective-permute-start.17 = (f32[144,128]{1,0:T(8,128)S(1)}, f32[144,128]{1,0:T(8,128)S(1)}, u32[]{:S(2)}, u32[]{:S(2)}) collective-permute-start(f32[144,128]{1,0:T(8,128)S(1)} %image_x.1.image), channel_id=1, source_target_pairs={{0,4},{1,5},{2,6},{3,7},{4,36},{5,37},{6,38},{7,39},{8,68},{9,69},... | collective-permute-start | bytes 221192 | tf_op jit(solution)/shard_map/image_planes/ppermute | solution.py:35
  71.5 8.1 %collective-permute-start.16 = (f32[144,128]{1,0:T(8,128)S(1)}, f32[144,128]{1,0:T(8,128)S(1)}, u32[]{:S(2)}, u32[]{:S(2)}) collective-permute-start(f32[144,128]{1,0:T(8,128)S(1)} %image_x.1.image), channel_id=1, source_target_pairs={{0,0},{1,1},{2,2},{3,3},{4,32},{5,33},{6,34},{7,35},{8,64},{9,65},... | collective-permute-start | bytes 221192 | tf_op jit(solution)/shard_map/image_planes/ppermute | solution.py:35
  80.1 7.6 %collective-permute-start.20 = (f32[576,128]{1,0:T(8,128)S(1)}, f32[576,128]{1,0:T(8,128)S(1)}, u32[]{:S(2)}, u32[]{:S(2)}) collective-permute-start(f32[576,128]{1,0:T(8,128)S(1)} %image_planes.1.b0), channel_id=1, source_target_pairs={{0,1},{1,2},{2,3},{3,0},{4,5},{5,6},{6,7},{7,4},{8,9},{9,10},{10,1... | collective-permute-start | bytes 884744 | tf_op jit(solution)/shard_map/image_y/ppermute | solution.py:35
  82.4 13.9 %collective-permute-start.21 = (f32[576,128]{1,0:T(8,128)S(1)}, f32[576,128]{1,0:T(8,128)S(1)}, u32[]{:S(2)}, u32[]{:S(2)}) collective-permute-start(f32[576,128]{1,0:T(8,128)S(1)} %image_planes.1.b0), channel_id=1, source_target_pairs={{0,3},{1,0},{2,1},{3,2},{4,7},{5,4},{6,5},{7,6},{8,11},{9,8},{10,9... | collective-permute-start | bytes 884744 | tf_op jit(solution)/shard_map/image_y/ppermute | solution.py:35
  87.7 8.6 %collective-permute-start.22 = (f32[576,128]{1,0:T(8,128)S(1)}, f32[576,128]{1,0:T(8,128)S(1)}, u32[]{:S(2)}, u32[]{:S(2)}) collective-permute-start(f32[576,128]{1,0:T(8,128)S(1)} %collective-permute-done.20.b1), channel_id=1, source_target_pairs={{0,1},{1,2},{2,3},{3,0},{4,5},{5,6},{6,7},{7,4},{8,9},{9,10},{10,1... | collective-permute-start | bytes 884744 | tf_op jit(solution)/shard_map/image_far/ppermute | solution.py:35
  90.4 11.3 %collective-permute-start.26 = (f32[288,128]{1,0:T(8,128)S(1)}, f32[288,128]{1,0:T(8,128)S(1)}, u32[]{:S(2)}, u32[]{:S(2)}) collective-permute-start(f32[288,128]{1,0:T(8,128)S(1)} %image_columns.2.p0), channel_id=1, source_target_pairs={{0,64},{1,65},{2,66},{3,67},{4,68},{5,69},{6,70},{7,71},{8,72},{9,... | collective-permute-start | bytes 442376 | tf_op jit(solution)/shard_map/image_columns/ppermute | solution.py:35
  93.4 8.3 %collective-permute-start.25 = (f32[288,128]{1,0:T(8,128)S(1)}, f32[288,128]{1,0:T(8,128)S(1)}, u32[]{:S(2)}, u32[]{:S(2)}) collective-permute-start(f32[288,128]{1,0:T(8,128)S(1)} %image_columns.2.p0), channel_id=1, source_target_pairs={{0,96},{1,97},{2,98},{3,99},{4,100},{5,101},{6,102},{7,103},{8,104... | collective-permute-start | bytes 442376 | tf_op jit(solution)/shard_map/image_columns/ppermute | solution.py:35
  95.7 6.0 %collective-permute-start.24 = (f32[288,128]{1,0:T(8,128)S(1)}, f32[288,128]{1,0:T(8,128)S(1)}, u32[]{:S(2)}, u32[]{:S(2)}) collective-permute-start(f32[288,128]{1,0:T(8,128)S(1)} %image_columns.2.p0), channel_id=1, source_target_pairs={{0,32},{1,33},{2,34},{3,35},{4,36},{5,37},{6,38},{7,39},{8,40},{9,... | collective-permute-start | bytes 442376 | tf_op jit(solution)/shard_map/image_columns/ppermute | solution.py:35
  96.9 8.6 %collective-permute-start.23 = (f32[1152,128]{1,0:T(8,128)S(1)}, f32[1152,128]{1,0:T(8,128)S(1)}, u32[]{:S(2)}, u32[]{:S(2)}) collective-permute-start(f32[1152,128]{1,0:T(8,128)S(1)} %pick.1), channel_id=1, source_target_pairs={{0,16},{1,17},{2,18},{3,19},{4,20},{5,21},{6,22},{7,23},{8,24},{9,... | collective-permute-start | bytes 1769480 | tf_op jit(solution)/shard_map/image_swap/ppermute | solution.py:35
  102.3 9.7 %collective-permute-start.27 = (f32[1152,128]{1,0:T(8,128)S(1)}, f32[1152,128]{1,0:T(8,128)S(1)}, u32[]{:S(2)}, u32[]{:S(2)}) collective-permute-start(f32[1152,128]{1,0:T(8,128)S(1)} %image_columns.3.own), channel_id=1, source_target_pairs={{0,16},{1,17},{2,18},{3,19},{4,20},{5,21},{6,22},{7,23},{8,24},{9,... | collective-permute-start | bytes 1769480 | tf_op jit(solution)/shard_map/image_columns/ppermute | solution.py:35
  107.0 1.3 %collective-permute-start.28 = (f32[128,128]{1,0:T(8,128)S(1)}, f32[128,128]{1,0:T(8,128)S(1)}, u32[]{:S(2)}, u32[]{:S(2)}) collective-permute-start(f32[128,128]{1,0:T(8,128)S(1)} %get-tuple-element.97), channel_id=1, source_target_pairs={{0,16},{1,17},{2,18},{3,19},{4,20},{5,21},{6,22},{7,23},{8,24},{9,... | collective-permute-start | bytes 196616 | tf_op jit(solution)/shard_map/inner/ppermute | solution.py:35
  108.4 10.1 %collective-permute-start.31 = (f32[128,128]{1,0:T(8,128)S(1)}, f32[128,128]{1,0:T(8,128)S(1)}, u32[]{:S(2)}, u32[]{:S(2)}) collective-permute-start(f32[128,128]{1,0:T(8,128)S(1)} %add.18.k0), channel_id=1, source_target_pairs={{0,64},{1,65},{2,66},{3,67},{4,68},{5,69},{6,70},{7,71},{8,72},{9,... | collective-permute-start | bytes 196616 | tf_op jit(solution)/shard_map/inner/ppermute | solution.py:35
  109.9 8.5 %collective-permute-start.30 = (f32[128,128]{1,0:T(8,128)S(1)}, f32[128,128]{1,0:T(8,128)S(1)}, u32[]{:S(2)}, u32[]{:S(2)}) collective-permute-start(f32[128,128]{1,0:T(8,128)S(1)} %add.18.k0), channel_id=1, source_target_pairs={{0,96},{1,97},{2,98},{3,99},{4,100},{5,101},{6,102},{7,103},{8,104... | collective-permute-start | bytes 196616 | tf_op jit(solution)/shard_map/inner/ppermute | solution.py:35
  111.5 6.9 %collective-permute-start.29 = (f32[128,128]{1,0:T(8,128)S(1)}, f32[128,128]{1,0:T(8,128)S(1)}, u32[]{:S(2)}, u32[]{:S(2)}) collective-permute-start(f32[128,128]{1,0:T(8,128)S(1)} %add.18.k0), channel_id=1, source_target_pairs={{0,32},{1,33},{2,34},{3,35},{4,36},{5,37},{6,38},{7,39},{8,40},{9,... | collective-permute-start | bytes 196616 | tf_op jit(solution)/shard_map/inner/ppermute | solution.py:35

commit v3 on v2

--- a/solution.py
+++ b/solution.py
@@ -153,21 +153,22 @@
     gram_near[...] = full_dot(front[...], front[...], ((0,), (0,))) + full_dot(back[...], back[...], ((0,), (0,)))
 
 
-def far_gram_kernel(place, own, below, above, far, gram, gram_near, out):
-    x, core, z = place[0], place[1], place[2]
-    out[:WIDTH, :] = (gram[...] + full_dot(far[...], far[...], ((0,), (0,)))) + gram_near[...]
-    out[WIDTH:, :] = jnp.zeros((WIDTH, WIDTH), F32)
-    for k, block in zip(around(core), (own, below, above, far)):
-
-        @pl.when((x == 0) & (core == 0) & (z == k))
-        def _(block=block):
-            out[WIDTH:, :] = block[:WIDTH, :]
-
-
-def image_kernel(place, whole, high, low, near, own, front, back, far, sent, kept, across):
+def image_kernel(place, whole, high, low, near, gram, gram_near, own, front, back, far, sent, kept, across):
+    blocks = (own, front, back, far)
+    total = (gram[...] + full_dot(far[...], far[...], ((0,), (0,)))) + gram_near[...]
+    for out in (sent, kept):
+        out[8 * PIECE : 8 * PIECE + WIDTH, :] = total
+        out[8 * PIECE + WIDTH :, :] = jnp.zeros((WIDTH, WIDTH), F32)
+    for k, piece in zip(around(place[1]), blocks):
+
+        @pl.when((place[0] == 0) & (place[1] == 0) & (place[2] == k))
+        def _(piece=piece):
+            kept[8 * PIECE + WIDTH :, :] = piece[:WIDTH, :]
+            sent[8 * PIECE + WIDTH :, :] = piece[:WIDTH, :]
+
     image = (near[...] + turned_image(place, 2, far, high, low)).T
     block, half = 2 * (place[3] % 2) + place[2] // 2, place[2] % 2
-    for k, piece in zip(around(place[1]), (own, front, back, far)):
+    for k, piece in zip(around(place[1]), blocks):
 
         @pl.when((place[2] - k + 4) % 4 == block)
         def _(piece=piece):
@@ -185,25 +186,28 @@
                     out[(4 + x) * PIECE : (5 + x) * PIECE, :] = corner[index : index + PIECE, :]
 
 
-def factor_kernel(g0, g1, g3, g2, upper, upper_here, normal, work):
-    total = (g0[...] + g2[...]) + (g1[...] + g3[...])
-    work[...] = total[:WIDTH, :]
+def factor_kernel(own, r1, r3, r2, upper, upper_here, normal, work):
+    total = (own[...] + r2[...]) + (r1[...] + r3[...])
+    gram = total[:WIDTH, :]
+    work[...] = gram
     cholesky_rows(work, upper_here)
     factor = upper_here[...]
     upper[...] = factor
-    normal[...] = total[:WIDTH, :] + full_dot(total[WIDTH:, :], factor, ((0,), (0,)))
-
-
-def deal_kernel(place, kept, received, upper, m0, m1, m3, m2, image):
-    half = kept[...] + received[...]
-    image[...] = half[: 4 * PIECE, :] + split_dot(half[4 * PIECE :, :], upper[...], ((1,), (0,)))
+    normal[...] = gram + full_dot(total[WIDTH:, :], factor, ((0,), (0,)))
+
+
+def combine_kernel(own, r1, r3, r2, upper, image):
+    total = (own[...] + r2[...]) + (r1[...] + r3[...])
+    image[...] = total[:PIECE, :] + split_dot(total[PIECE:, :], upper[...], ((1,), (0,)))
+
+
+def deal_kernel(place, kept, received, small, m0, m1, m3, m2):
+    small[...] = kept[8 * PIECE :, :] + received[8 * PIECE :, :]
     for k, out in ((0, m0), (1, m1), (3, m3), (2, m2)):
-        start = pl.multiple_of(((place[0] + k) % 4) * PIECE, 16)
-        out[...] = image[pl.ds(start, PIECE), :]
-
-
-def sum_kernel(own, r1, r3, r2, image):
-    image[...] = (own[...] + r2[...]) + (r1[...] + r3[...])
+        for part in range(2):
+            start = pl.multiple_of((4 * part + (place[0] + k) % 4) * PIECE, 16)
+            rows = pl.ds(start, PIECE)
+            out[part * PIECE : (part + 1) * PIECE, :] = kept[rows, :] + received[rows, :]
 
 
 def untag_kernel(place, p0, p1, p3, p2, out):
@@ -430,50 +434,44 @@
     far = after(far, gram)
     in_z = [in_y, below, above, far]
 
-    with jax.named_scope("gram"):
-        gram = local(far_gram_kernel, shape(2 * WIDTH), 4)(place, *in_z, gram, gram_near)
-    with jax.named_scope("gram_sum"):
-        gram = gram + send(gram, other_core)
-        grams = [gram] + ring(gram, along_x)
     with jax.named_scope("image"):
         sent, kept, across = local(
-            image_kernel, [shape(8 * PIECE)] * 2 + [shape(2 * PIECE)], 24, flops=2 * ROWS * COLS * WIDTH
-        )(place, whole, high, low, near, *after(in_z, gram))
-    grams = after(grams, kept)
+            image_kernel, [shape(8 * PIECE + 2 * WIDTH)] * 2 + [shape(2 * PIECE)], 24, flops=2 * ROWS * COLS * WIDTH
+        )(place, whole, high, low, near, gram, gram_near, *in_z)
     with jax.named_scope("image_core"):
-        received = send(after(sent, grams), other_core)
+        received = send(sent, other_core)
+    with jax.named_scope("deal"):
+        gram, m0, m1, m3, m2 = local(deal_kernel, [shape(2 * WIDTH)] + [shape(2 * PIECE)] * 4, 8)(place, kept, received)
+    with jax.named_scope("gram_x"):
+        grams = [gram] + ring(gram, along_x)
+    with jax.named_scope("image_x"):
+        r1, r3, r2 = (send(m, along_x(k)) for m, k in ((m1, 1), (m3, 3), (m2, 2)))
     with jax.named_scope("panel_across"):
         across = send(after(across, grams), planes(0))
     with jax.named_scope("factor"):
         upper, upper_here, normal = local(factor_kernel, [tile] * 3, 4, [pltpu.VMEM((WIDTH, WIDTH), F32)], 2000000000)(
             *grams
         )
-    with jax.named_scope("deal"):
-        m0, m1, m3, m2 = local(deal_kernel, [shape(PIECE)] * 4, 8, [pltpu.VMEM((4 * PIECE, WIDTH), F32)])(
-            place, kept, received, upper_here
-        )
+    r1, r3, r2, across = after((r1, r3, r2, across), normal)
     with jax.named_scope("image_x"):
-        r1, r3, r2 = (send(m, along_x(k)) for m, k in ((m1, 1), (m3, 3), (m2, 2)))
-    with jax.named_scope("panel_across"):
-        handed = send(local(hand_kernel, shape(PIECE), 4)(place, after(across, m0)), other_core)
-    r1, r3, r2, handed = after((r1, r3, r2, handed))
-    with jax.named_scope("image_x"):
-        image = local(sum_kernel, shape(PIECE), 4)(m0, r1, r3, r2)
+        image = local(combine_kernel, shape(PIECE), 4)(m0, r1, r3, r2, upper_here)
 
     with jax.named_scope("image_planes"):
         planes_in = [send(image, planes(k)) for k in (0, 1, 3, 2)]
-        in_plane = local(join_z_kernel, shape(4 * PIECE), 4)(place, *planes_in)
+    with jax.named_scope("panel_across"):
+        handed = send(local(hand_kernel, shape(PIECE), 4)(place, after(across, planes_in[3])), other_core)
+    with jax.named_scope("image_planes"):
+        in_plane = local(join_z_kernel, shape(4 * PIECE), 4)(place, *after(planes_in, handed))
     with jax.named_scope("image_y"):
         below, above = send(in_plane, turn(along_y, 1)), send(in_plane, turn(along_y, 3))
     with jax.named_scope("image_columns"):
-        tagged = local(tag_kernel, shape(2 * PIECE), 4)(place, image, across, after(handed, in_plane))
+        tagged = local(tag_kernel, shape(2 * PIECE), 4)(place, image, across, handed)
+        sides = ring(tagged, along_x)
     with jax.named_scope("inverse"):
         inverse = local(inverse_kernel, tile, 4, flops=2000000000)(after(normal, in_plane))
-    below, tagged = after((below, tagged), inverse)
+    below = after(below, inverse, sides[0])
     with jax.named_scope("image_far"):
         opposite = send(below, turn(along_y, 1))
-    with jax.named_scope("image_columns"):
-        sides = ring(after(tagged, below), along_x)
     blocks = [in_plane, below, above, opposite]
     with jax.named_scope("pick"):
         chosen = local(pick_kernel, shape(8 * PIECE), 8)(place, *blocks)

time: 124 us -> 118 us (0.952)
  waiting for transfers between devices: 22.3 us -> 14.6 us
  starting transfers between devices: 61 us -> 62.9 us
    ppermute x32 -> x31, waiting for transfers between devices: 22.3 us -> 14.6 us  [send(): return lax.ppermute(value, AXES, pairs(where))]
    ppermute x32 -> x31, starting transfers between devices: 61 us -> 62.9 us  [send(): return lax.ppermute(value, AXES, pairs(where))]
    pallas_call x15 -> x14, Pallas kernels: 29.1 us -> 28.5 us  [run(): pl.pallas_call(kernel, in_specs=specs, out_specs=outs, out_shape=out_shap...]
  transfers between devices with their start and end apart: 32 -> 31, of which waited for: 13 -> 11; matrix products, arithmetic and copies ran while one was open for 0% -> 0% of each run, Pallas kernels for 25% -> 24%
where the time goes in v3:
time: 118 us
  starting transfers between devices  62.9 us (53%)
  Pallas kernels  38 us (32%)
  waiting for transfers between devices  14.6 us (12%)
    ppermute x31, starting transfers between devices, send(): return lax.ppermute(value, AXES, pairs(where))  62.9 us
    pallas_call x14, Pallas kernels, run(): pl.pallas_call(kernel, in_specs=specs, out_specs=outs, out_shape=out_shap...  28.5 us
    ppermute x31, waiting for transfers between devices, send(): return lax.ppermute(value, AXES, pairs(where))  14.6 us
    pallas_call x1, Pallas kernels, shards(): pl.pallas_call(last_update_kernel, in_specs=[VMEM] * 8, out_specs=anywher...  5.21 us
    pallas_call x1, Pallas kernels, shards(): pl.pallas_call(split_kernel, in_specs=[anywhere, VMEM], out_specs=[VMEM]...  4.3 us
  transfers between devices with their start and end apart: 31, of which 11 were waited for; matrix products, arithmetic and copies ran while one was open for 0% of the time, Pallas kernels for 24%

profile of v3, /device:TPU:1, one launch (start us, length us, event | category | flops | bytes accessed | tf_op | source)
XLA Modules:
  0.0 117.6 jit_solution(10991107414830514882)
XLA Ops:
  0.6 3.6 %collective-permute-start.1 = (f32[144,128]{1,0:T(8,128)}, f32[144,128]{1,0:T(8,128)S(1)}, u32[]{:S(2)}, u32[]{:S(2)}) collective-permute-start(f32[144,128]{1,0:T(8,128)} %p0.1), channel_id=1, source_target_pairs={{0,3},{1,0},{2,1},{3,2},{4,7},{5,4},{6,5},{7,6},{8,11},{9,8},{10,9... | collective-permute-start | bytes 221192 | tf_op jit(solution)/shard_map/panel_y/ppermute | solution.py:35
  4.3 1.6 %collective-permute-start.2 = (f32[144,128]{1,0:T(8,128)}, f32[144,128]{1,0:T(8,128)S(1)}, u32[]{:S(2)}, u32[]{:S(2)}) collective-permute-start(f32[144,128]{1,0:T(8,128)} %p0.1), channel_id=1, source_target_pairs={{0,2},{1,3},{2,0},{3,1},{4,6},{5,7},{6,4},{7,5},{8,10},{9,11},{10,... | collective-permute-start | bytes 221192 | tf_op jit(solution)/shard_map/panel_y/ppermute | solution.py:35
  6.0 3.5 %collective-permute-done.p1 = f32[144,128]{1,0:T(8,128)S(1)} collective-permute-done((f32[144,128]{1,0:T(8,128)}, f32[144,128]{1,0:T(8,128)S(1)}, u32[]{:S(2)}, u32[]{:S(2)}) %collective-permute-start) | collective-permute-done | bytes 73760 | tf_op jit(solution)/shard_map/panel_y/ppermute | solution.py:35
  9.5 0.4 collective-permute-done.2.p2
  9.9 0.9 copy-done
  10.8 0.6 panel_y.1.after.own.p0
  11.3 1.7 %collective-permute-start.4 = (f32[576,128]{1,0:T(8,128)S(1)}, f32[576,128]{1,0:T(8,128)S(1)}, u32[]{:S(2)}, u32[]{:S(2)}) collective-permute-start(f32[576,128]{1,0:T(8,128)S(1)} %panel_y.1.after.own.p0), channel_id=1, source_target_pairs={{0,12},{1,13},{2,14},{3,15},{4,0},{5,1},{6,2},{7,3},{8,4},{9,5},{1... | collective-permute-start | bytes 884744 | tf_op jit(solution)/shard_map/panel_z/ppermute | solution.py:35
  13.1 2.2 %collective-permute-start.3 = (f32[576,128]{1,0:T(8,128)S(1)}, f32[576,128]{1,0:T(8,128)S(1)}, u32[]{:S(2)}, u32[]{:S(2)}) collective-permute-start(f32[576,128]{1,0:T(8,128)S(1)} %panel_y.1.after.own.p0), channel_id=1, source_target_pairs={{0,4},{1,5},{2,6},{3,7},{4,8},{5,9},{6,10},{7,11},{8,12},{9,13},{1... | collective-permute-start | bytes 884744 | tf_op jit(solution)/shard_map/panel_z/ppermute | solution.py:35
  15.3 4.3 %split.1 = (f32[2304,1152]{1,0:T(8,128)S(1)}, bf16[2304,1152]{1,0:T(8,128)(2,1)S(1)}, bf16[2304,1152]{1,0:T(8,128)(2,1)S(1)}) custom-call(f32[2304,1152]{1,0:T(8,128)} %trailing.1, f32[576,128]{1,0:T(8,128)S(1)} %panel_y.1.after.own.p0), custom_call_target="tpu_custom_call" | custom-call | bytes 10616832 | tf_op jit(solution)/shard_map/split/pallas_call | solution.py:418
  19.6 2.0 %collective-permute-done.3.front.p1 = f32[576,128]{1,0:T(8,128)S(1)} collective-permute-done((f32[576,128]{1,0:T(8,128)S(1)}, f32[576,128]{1,0:T(8,128)S(1)}, u32[]{:S(2)}, u32[]{:S(2)}) %collective-permute-start.3) | collective-permute-done | bytes 294944 | tf_op jit(solution)/shard_map/panel_z/ppermute | solution.py:35
  21.6 1.4 %collective-permute-start.5 = (f32[576,128]{1,0:T(8,128)S(1)}, f32[576,128]{1,0:T(8,128)S(1)}, u32[]{:S(2)}, u32[]{:S(2)}) collective-permute-start(f32[576,128]{1,0:T(8,128)S(1)} %collective-permute-done.3.front.p1), channel_id=1, source_target_pairs={{0,4},{1,5},{2,6},{3,7},{4,8},{5,9},{6,10},{7,11},{8,12},{9,13},{1... | collective-permute-start | bytes 884744 | tf_op jit(solution)/shard_map/panel_far/ppermute | solution.py:35
  23.0 3.9 %near.1 = (f32[128,1152]{1,0:T(8,128)S(1)}, f32[128,128]{1,0:T(8,128)S(1)}, f32[128,128]{1,0:T(8,128)S(1)}) custom-call(s32[4]{0:T(128)S(1)} %pad_add_fusion.place, bf16[2304,1152]{1,0:T(8,128)(2,1)S(1)} %get-tuple-element.47.high, bf16[2304,1152]{1,0:T(8,128)(2,1)S(1)} %get-tuple-element.48.low, f32[576,128]{1,0:T(8,128)S(1)} %panel_y.1.after.own.p0, ...), custom_call_target="tpu_custom_call" | custom-call | flops 1698693120 | tf_op jit(solution)/shard_map/near/pallas_call | solution.py:387
  27.1 2.5 %image.1 = (f32[1408,128]{1,0:T(8,128)S(1)}, f32[1408,128]{1,0:T(8,128)S(1)}, f32[288,128]{1,0:T(8,128)S(1)}) custom-call(s32[4]{0:T(128)S(1)} %pad_add_fusion.place, f32[2304,1152]{1,0:T(8,128)S(1)} %get-tuple-element.46.whole, bf16[2304,1152]{1,0:T(8,128)(2,1)S(1)} %get-tuple-element.47.high, bf16[2304,1152]{1,0:T(8,128)(2,1)S(1)} %get-tuple-element.48.low, ...), custom_call_target="tpu_custom_call" | custom-call | flops 679477248 | tf_op jit(solution)/shard_map/image/pallas_call | solution.py:387
  29.6 6.3 %collective-permute-start.6 = (f32[1408,128]{1,0:T(8,128)S(1)}, f32[1408,128]{1,0:T(8,128)S(1)}, u32[]{:S(2)}, u32[]{:S(2)}) collective-permute-start(f32[1408,128]{1,0:T(8,128)S(1)} %get-tuple-element.56), channel_id=1, source_target_pairs={{0,16},{1,17},{2,18},{3,19},{4,20},{5,21},{6,22},{7,23},{8,24},{9,... | collective-permute-start | bytes 2162696 | tf_op jit(solution)/shard_map/image_core/ppermute | solution.py:35
  36.0 1.8 %collective-permute-done.6.received = f32[1408,128]{1,0:T(8,128)S(1)} collective-permute-done((f32[1408,128]{1,0:T(8,128)S(1)}, f32[1408,128]{1,0:T(8,128)S(1)}, u32[]{:S(2)}, u32[]{:S(2)}) %collective-permute-start.6) | collective-permute-done | bytes 720928 | tf_op jit(solution)/shard_map/image_core/ppermute | solution.py:35
  37.8 0.6 deal.1
  38.4 2.8 %collective-permute-start.9 = (f32[256,128]{1,0:T(8,128)S(1)}, f32[256,128]{1,0:T(8,128)S(1)}, u32[]{:S(2)}, u32[]{:S(2)}) collective-permute-start(f32[256,128]{1,0:T(8,128)S(1)} %get-tuple-element.57.own), channel_id=1, source_target_pairs={{0,64},{1,65},{2,66},{3,67},{4,68},{5,69},{6,70},{7,71},{8,72},{9,... | collective-permute-start | bytes 393224 | tf_op jit(solution)/shard_map/gram_x/ppermute | solution.py:35
  41.2 0.9 collective-permute-start.8
  42.1 0.6 collective-permute-start.7
  43.0 2.4 %collective-permute-start.11 = (f32[288,128]{1,0:T(8,128)S(1)}, f32[288,128]{1,0:T(8,128)S(1)}, u32[]{:S(2)}, u32[]{:S(2)}) collective-permute-start(f32[288,128]{1,0:T(8,128)S(1)} %get-tuple-element.62), channel_id=1, source_target_pairs={{0,96},{1,97},{2,98},{3,99},{4,100},{5,101},{6,102},{7,103},{8,104... | collective-permute-start | bytes 442376 | tf_op jit(solution)/shard_map/image_x/ppermute | solution.py:35
  45.4 2.1 %collective-permute-start.12 = (f32[288,128]{1,0:T(8,128)S(1)}, f32[288,128]{1,0:T(8,128)S(1)}, u32[]{:S(2)}, u32[]{:S(2)}) collective-permute-start(f32[288,128]{1,0:T(8,128)S(1)} %get-tuple-element.63), channel_id=1, source_target_pairs={{0,64},{1,65},{2,66},{3,67},{4,68},{5,69},{6,70},{7,71},{8,72},{9,... | collective-permute-start | bytes 442376 | tf_op jit(solution)/shard_map/image_x/ppermute | solution.py:35
  47.7 0.7 collective-permute-start.13
  48.3 5.3 %factor.1 = (f32[128,128]{1,0:T(8,128)}, f32[128,128]{1,0:T(8,128)S(1)}, f32[128,128]{1,0:T(8,128)S(1)}) custom-call(f32[256,128]{1,0:T(8,128)S(1)} %get-tuple-element.57.own, f32[256,128]{1,0:T(8,128)S(1)} %collective-permute-done.7.r1, f32[256,128]{1,0:T(8,128)S(1)} %collective-permute-done.8.r3, f32[256,128]{1,0:T(8,128)S(1)} %collective-permute-done.9.r2), custom_call_target="tpu_custom_call" | custom-call | flops 2000000000 | tf_op jit(solution)/shard_map/factor/pallas_call | solution.py:387
  54.1 7.1 %collective-permute-start.17 = (f32[144,128]{1,0:T(8,128)S(1)}, f32[144,128]{1,0:T(8,128)S(1)}, u32[]{:S(2)}, u32[]{:S(2)}) collective-permute-start(f32[144,128]{1,0:T(8,128)S(1)} %image_x.1.image), channel_id=1, source_target_pairs={{0,8},{1,9},{2,10},{3,11},{4,40},{5,41},{6,42},{7,43},{8,72},{9,73... | collective-permute-start | bytes 221192 | tf_op jit(solution)/shard_map/image_planes/ppermute | solution.py:35
  61.1 2.9 %collective-permute-start.16 = (f32[144,128]{1,0:T(8,128)S(1)}, f32[144,128]{1,0:T(8,128)S(1)}, u32[]{:S(2)}, u32[]{:S(2)}) collective-permute-start(f32[144,128]{1,0:T(8,128)S(1)} %image_x.1.image), channel_id=1, source_target_pairs={{0,12},{1,13},{2,14},{3,15},{4,44},{5,45},{6,46},{7,47},{8,76},{9,... | collective-permute-start | bytes 221192 | tf_op jit(solution)/shard_map/image_planes/ppermute | solution.py:35
  64.0 0.7 collective-permute-start.14
  64.7 0.6 panel_across.1
  65.3 3.3 %collective-permute-start.18 = (f32[144,128]{1,0:T(8,128)S(1)}, f32[144,128]{1,0:T(8,128)S(1)}, u32[]{:S(2)}, u32[]{:S(2)}) collective-permute-start(f32[144,128]{1,0:T(8,128)S(1)} %panel_across.1), channel_id=1, source_target_pairs={{0,16},{1,17},{2,18},{3,19},{4,20},{5,21},{6,22},{7,23},{8,24},{9,... | collective-permute-start | bytes 221192 | tf_op jit(solution)/shard_map/panel_across/ppermute | solution.py:35
  68.6 4.7 %collective-permute-done.15.p1 = f32[144,128]{1,0:T(8,128)S(1)} collective-permute-done((f32[144,128]{1,0:T(8,128)S(1)}, f32[144,128]{1,0:T(8,128)S(1)}, u32[]{:S(2)}, u32[]{:S(2)}) %collective-permute-start.15) | collective-permute-done | bytes 73760 | tf_op jit(solution)/shard_map/image_planes/ppermute | solution.py:35
  73.2 0.6 image_planes.1.b0
  73.8 2.3 %collective-permute-start.19 = (f32[576,128]{1,0:T(8,128)S(1)}, f32[576,128]{1,0:T(8,128)S(1)}, u32[]{:S(2)}, u32[]{:S(2)}) collective-permute-start(f32[576,128]{1,0:T(8,128)S(1)} %image_planes.1.b0), channel_id=1, source_target_pairs={{0,1},{1,2},{2,3},{3,0},{4,5},{5,6},{6,7},{7,4},{8,9},{9,10},{10,1... | collective-permute-start | bytes 884744 | tf_op jit(solution)/shard_map/image_y/ppermute | solution.py:35
  76.2 0.6 image_columns.2.p0
  76.7 2.9 %collective-permute-start.20 = (f32[288,128]{1,0:T(8,128)S(1)}, f32[288,128]{1,0:T(8,128)S(1)}, u32[]{:S(2)}, u32[]{:S(2)}) collective-permute-start(f32[288,128]{1,0:T(8,128)S(1)} %image_columns.2.p0), channel_id=1, source_target_pairs={{0,32},{1,33},{2,34},{3,35},{4,36},{5,37},{6,38},{7,39},{8,40},{9,... | collective-permute-start | bytes 442376 | tf_op jit(solution)/shard_map/image_columns/ppermute | solution.py:35
  79.6 4.7 %inverse.1 = f32[128,128]{1,0:T(8,128)S(1)} custom-call(f32[128,128]{1,0:T(8,128)S(1)} %get-tuple-element.76.source), custom_call_target="tpu_custom_call" | custom-call | flops 2000000000 | tf_op jit(solution)/shard_map/inverse/pallas_call | solution.py:387
  84.3 2.8 %collective-permute-start.22 = (f32[576,128]{1,0:T(8,128)S(1)}, f32[576,128]{1,0:T(8,128)S(1)}, u32[]{:S(2)}, u32[]{:S(2)}) collective-permute-start(f32[576,128]{1,0:T(8,128)S(1)} %collective-permute-done.19.b1), channel_id=1, source_target_pairs={{0,1},{1,2},{2,3},{3,0},{4,5},{5,6},{6,7},{7,4},{8,9},{9,10},{10,1... | collective-permute-start | bytes 884744 | tf_op jit(solution)/shard_map/image_far/ppermute | solution.py:35
  87.1 3.3 %collective-permute-start.25 = (f32[288,128]{1,0:T(8,128)S(1)}, f32[288,128]{1,0:T(8,128)S(1)}, u32[]{:S(2)}, u32[]{:S(2)}) collective-permute-start(f32[288,128]{1,0:T(8,128)S(1)} %image_columns.2.p0), channel_id=1, source_target_pairs={{0,64},{1,65},{2,66},{3,67},{4,68},{5,69},{6,70},{7,71},{8,72},{9,... | collective-permute-start | bytes 442376 | tf_op jit(solution)/shard_map/image_columns/ppermute | solution.py:35
  90.4 1.1 collective-permute-start.24
  91.5 0.6 pick.1
  92.2 3.8 %collective-permute-start.23 = (f32[1152,128]{1,0:T(8,128)S(1)}, f32[1152,128]{1,0:T(8,128)S(1)}, u32[]{:S(2)}, u32[]{:S(2)}) collective-permute-start(f32[1152,128]{1,0:T(8,128)S(1)} %pick.1), channel_id=1, source_target_pairs={{0,16},{1,17},{2,18},{3,19},{4,20},{5,21},{6,22},{7,23},{8,24},{9,... | collective-permute-start | bytes 1769480 | tf_op jit(solution)/shard_map/image_swap/ppermute | solution.py:35
  96.2 0.6 image_columns.3.own
  96.8 1.2 %collective-permute-start.26 = (f32[1152,128]{1,0:T(8,128)S(1)}, f32[1152,128]{1,0:T(8,128)S(1)}, u32[]{:S(2)}, u32[]{:S(2)}) collective-permute-start(f32[1152,128]{1,0:T(8,128)S(1)} %image_columns.3.own), channel_id=1, source_target_pairs={{0,16},{1,17},{2,18},{3,19},{4,20},{5,21},{6,22},{7,23},{8,24},{9,... | collective-permute-start | bytes 1769480 | tf_op jit(solution)/shard_map/image_columns/ppermute | solution.py:35
  98.1 1.5 %gather.1 = (f32[2304,128]{1,0:T(8,128)S(1)}, f32[2304,128]{1,0:T(8,128)S(1)}, f32[128,128]{1,0:T(8,128)S(1)}) custom-call(s32[4]{0:T(128)S(1)} %pad_add_fusion.place, f32[576,128]{1,0:T(8,128)S(1)} %panel_y.1.after.own.p0, f32[576,128]{1,0:T(8,128)S(1)} %collective-permute-done.3.front.p1, f32[576,128]{1,0:T(8,128)S(1)} %collective-permute-done.4.back.p3, ...), custom_call_target="tpu_custom_call" | custom-call | tf_op jit(solution)/shard_map/gather/pallas_call | solution.py:387
  99.6 1.2 %collective-permute-done.27 = f32[128,128]{1,0:T(8,128)S(1)} collective-permute-done((f32[128,128]{1,0:T(8,128)S(1)}, f32[128,128]{1,0:T(8,128)S(1)}, u32[]{:S(2)}, u32[]{:S(2)}) %collective-permute-start.27) | collective-permute-done | bytes 65568 | tf_op jit(solution)/shard_map/inner/ppermute | solution.py:35
  100.9 3.4 %collective-permute-start.30 = (f32[128,128]{1,0:T(8,128)S(1)}, f32[128,128]{1,0:T(8,128)S(1)}, u32[]{:S(2)}, u32[]{:S(2)}) collective-permute-start(f32[128,128]{1,0:T(8,128)S(1)} %add.14.k0), channel_id=1, source_target_pairs={{0,64},{1,65},{2,66},{3,67},{4,68},{5,69},{6,70},{7,71},{8,72},{9,... | collective-permute-start | bytes 196616 | tf_op jit(solution)/shard_map/inner/ppermute | solution.py:35
  104.3 0.7 collective-permute-start.29
  105.0 0.8 collective-permute-start.28
  105.8 6.4 %first_update.1 = (f32[2304,1152]{1,0:T(8,128)S(1)}, f32[128,1152]{1,0:T(8,128)S(1)}) custom-call(s32[4]{0:T(128)S(1)} %pad_add_fusion.place, f32[2304,1152]{1,0:T(8,128)S(1)} %get-tuple-element.46.whole, f32[2304,128]{1,0:T(8,128)S(1)} %get-tuple-element.78.shifted_rows, f32[2304,128]{1,0:T(8,128)S(1)} %get-tuple-element.79.image_rows, ...), custom_call_target="tpu_custom_call" | custom-call | flops 4076863488 | tf_op jit(solution)/shard_map/first_update/pallas_call | solution.py:387
  112.2 5.2 %last_update.1 = f32[2304,1152]{1,0:T(8,128)} custom-call(f32[2304,1152]{1,0:T(8,128)S(1)} %get-tuple-element.85.base, f32[2304,128]{1,0:T(8,128)S(1)} %get-tuple-element.78.shifted_rows, f32[128,1152]{1,0:T(8,128)S(1)} %get-tuple-element.86.turned, f32[128,128]{1,0:T(8,128)S(1)} %inverse.1, f32[128,128]{1,0:T(8,128)S(1)} %add.14.k0, ...), custom_call_target="tpu_custom_call" | custom-call | flops 2717908992 | bytes 10616832 | tf_op jit(solution)/shard_map/last_update/pallas_call | solution.py:507
  (34 shorter events, 1.7 us)
Async XLA Ops:
  0.6 5.4 %collective-permute-start.1 = (f32[144,128]{1,0:T(8,128)}, f32[144,128]{1,0:T(8,128)S(1)}, u32[]{:S(2)}, u32[]{:S(2)}) collective-permute-start(f32[144,128]{1,0:T(8,128)} %p0.1), channel_id=1, source_target_pairs={{0,3},{1,0},{2,1},{3,2},{4,7},{5,4},{6,5},{7,6},{8,11},{9,8},{10,9... | collective-permute-start | bytes 221192 | tf_op jit(solution)/shard_map/panel_y/ppermute | solution.py:35
  4.3 5.2 %collective-permute-start = (f32[144,128]{1,0:T(8,128)}, f32[144,128]{1,0:T(8,128)S(1)}, u32[]{:S(2)}, u32[]{:S(2)}) collective-permute-start(f32[144,128]{1,0:T(8,128)} %p0.1), channel_id=1, source_target_pairs={{0,1},{1,2},{2,3},{3,0},{4,5},{5,6},{6,7},{7,4},{8,9},{9,10},{10,1... | collective-permute-start | bytes 221192 | tf_op jit(solution)/shard_map/panel_y/ppermute | solution.py:35
  4.3 5.6 %collective-permute-start.2 = (f32[144,128]{1,0:T(8,128)}, f32[144,128]{1,0:T(8,128)S(1)}, u32[]{:S(2)}, u32[]{:S(2)}) collective-permute-start(f32[144,128]{1,0:T(8,128)} %p0.1), channel_id=1, source_target_pairs={{0,2},{1,3},{2,0},{3,1},{4,6},{5,7},{6,4},{7,5},{8,10},{9,11},{10,... | collective-permute-start | bytes 221192 | tf_op jit(solution)/shard_map/panel_y/ppermute | solution.py:35
  9.9 0.9 copy-start
  11.3 8.2 %collective-permute-start.4 = (f32[576,128]{1,0:T(8,128)S(1)}, f32[576,128]{1,0:T(8,128)S(1)}, u32[]{:S(2)}, u32[]{:S(2)}) collective-permute-start(f32[576,128]{1,0:T(8,128)S(1)} %panel_y.1.after.own.p0), channel_id=1, source_target_pairs={{0,12},{1,13},{2,14},{3,15},{4,0},{5,1},{6,2},{7,3},{8,4},{9,5},{1... | collective-permute-start | bytes 884744 | tf_op jit(solution)/shard_map/panel_z/ppermute | solution.py:35
  13.1 8.5 %collective-permute-start.3 = (f32[576,128]{1,0:T(8,128)S(1)}, f32[576,128]{1,0:T(8,128)S(1)}, u32[]{:S(2)}, u32[]{:S(2)}) collective-permute-start(f32[576,128]{1,0:T(8,128)S(1)} %panel_y.1.after.own.p0), channel_id=1, source_target_pairs={{0,4},{1,5},{2,6},{3,7},{4,8},{5,9},{6,10},{7,11},{8,12},{9,13},{1... | collective-permute-start | bytes 884744 | tf_op jit(solution)/shard_map/panel_z/ppermute | solution.py:35
  21.6 5.6 %collective-permute-start.5 = (f32[576,128]{1,0:T(8,128)S(1)}, f32[576,128]{1,0:T(8,128)S(1)}, u32[]{:S(2)}, u32[]{:S(2)}) collective-permute-start(f32[576,128]{1,0:T(8,128)S(1)} %collective-permute-done.3.front.p1), channel_id=1, source_target_pairs={{0,4},{1,5},{2,6},{3,7},{4,8},{5,9},{6,10},{7,11},{8,12},{9,13},{1... | collective-permute-start | bytes 884744 | tf_op jit(solution)/shard_map/panel_far/ppermute | solution.py:35
  29.6 8.2 %collective-permute-start.6 = (f32[1408,128]{1,0:T(8,128)S(1)}, f32[1408,128]{1,0:T(8,128)S(1)}, u32[]{:S(2)}, u32[]{:S(2)}) collective-permute-start(f32[1408,128]{1,0:T(8,128)S(1)} %get-tuple-element.56), channel_id=1, source_target_pairs={{0,16},{1,17},{2,18},{3,19},{4,20},{5,21},{6,22},{7,23},{8,24},{9,... | collective-permute-start | bytes 2162696 | tf_op jit(solution)/shard_map/image_core/ppermute | solution.py:35
  38.4 7.0 %collective-permute-start.9 = (f32[256,128]{1,0:T(8,128)S(1)}, f32[256,128]{1,0:T(8,128)S(1)}, u32[]{:S(2)}, u32[]{:S(2)}) collective-permute-start(f32[256,128]{1,0:T(8,128)S(1)} %get-tuple-element.57.own), channel_id=1, source_target_pairs={{0,64},{1,65},{2,66},{3,67},{4,68},{5,69},{6,70},{7,71},{8,72},{9,... | collective-permute-start | bytes 393224 | tf_op jit(solution)/shard_map/gram_x/ppermute | solution.py:35
  41.2 6.4 %collective-permute-start.8 = (f32[256,128]{1,0:T(8,128)S(1)}, f32[256,128]{1,0:T(8,128)S(1)}, u32[]{:S(2)}, u32[]{:S(2)}) collective-permute-start(f32[256,128]{1,0:T(8,128)S(1)} %get-tuple-element.57.own), channel_id=1, source_target_pairs={{0,96},{1,97},{2,98},{3,99},{4,100},{5,101},{6,102},{7,103},{8,104... | collective-permute-start | bytes 393224 | tf_op jit(solution)/shard_map/gram_x/ppermute | solution.py:35
  42.1 5.6 %collective-permute-start.7 = (f32[256,128]{1,0:T(8,128)S(1)}, f32[256,128]{1,0:T(8,128)S(1)}, u32[]{:S(2)}, u32[]{:S(2)}) collective-permute-start(f32[256,128]{1,0:T(8,128)S(1)} %get-tuple-element.57.own), channel_id=1, source_target_pairs={{0,32},{1,33},{2,34},{3,35},{4,36},{5,37},{6,38},{7,39},{8,40},{9,... | collective-permute-start | bytes 393224 | tf_op jit(solution)/shard_map/gram_x/ppermute | solution.py:35
  42.7 10.9 %collective-permute-start.10 = (f32[288,128]{1,0:T(8,128)S(1)}, f32[288,128]{1,0:T(8,128)S(1)}, u32[]{:S(2)}, u32[]{:S(2)}) collective-permute-start(f32[288,128]{1,0:T(8,128)S(1)} %get-tuple-element.61), channel_id=1, source_target_pairs={{0,32},{1,33},{2,34},{3,35},{4,36},{5,37},{6,38},{7,39},{8,40},{9,... | collective-permute-start | bytes 442376 | tf_op jit(solution)/shard_map/image_x/ppermute | solution.py:35
  43.0 10.6 %collective-permute-start.11 = (f32[288,128]{1,0:T(8,128)S(1)}, f32[288,128]{1,0:T(8,128)S(1)}, u32[]{:S(2)}, u32[]{:S(2)}) collective-permute-start(f32[288,128]{1,0:T(8,128)S(1)} %get-tuple-element.62), channel_id=1, source_target_pairs={{0,96},{1,97},{2,98},{3,99},{4,100},{5,101},{6,102},{7,103},{8,104... | collective-permute-start | bytes 442376 | tf_op jit(solution)/shard_map/image_x/ppermute | solution.py:35
  45.4 8.5 %collective-permute-start.12 = (f32[288,128]{1,0:T(8,128)S(1)}, f32[288,128]{1,0:T(8,128)S(1)}, u32[]{:S(2)}, u32[]{:S(2)}) collective-permute-start(f32[288,128]{1,0:T(8,128)S(1)} %get-tuple-element.63), channel_id=1, source_target_pairs={{0,64},{1,65},{2,66},{3,67},{4,68},{5,69},{6,70},{7,71},{8,72},{9,... | collective-permute-start | bytes 442376 | tf_op jit(solution)/shard_map/image_x/ppermute | solution.py:35
  47.7 6.2 %collective-permute-start.13 = (f32[288,128]{1,0:T(8,128)S(1)}, f32[288,128]{1,0:T(8,128)S(1)}, u32[]{:S(2)}, u32[]{:S(2)}) collective-permute-start(f32[288,128]{1,0:T(8,128)S(1)} %get-tuple-element.65), channel_id=1, source_target_pairs={{0,0},{1,1},{2,2},{3,3},{4,32},{5,33},{6,34},{7,35},{8,64},{9,65},... | collective-permute-start | bytes 442376 | tf_op jit(solution)/shard_map/panel_across/ppermute | solution.py:35
  54.1 10.6 %collective-permute-start.17 = (f32[144,128]{1,0:T(8,128)S(1)}, f32[144,128]{1,0:T(8,128)S(1)}, u32[]{:S(2)}, u32[]{:S(2)}) collective-permute-start(f32[144,128]{1,0:T(8,128)S(1)} %image_x.1.image), channel_id=1, source_target_pairs={{0,8},{1,9},{2,10},{3,11},{4,40},{5,41},{6,42},{7,43},{8,72},{9,73... | collective-permute-start | bytes 221192 | tf_op jit(solution)/shard_map/image_planes/ppermute | solution.py:35
  61.1 7.4 %collective-permute-start.16 = (f32[144,128]{1,0:T(8,128)S(1)}, f32[144,128]{1,0:T(8,128)S(1)}, u32[]{:S(2)}, u32[]{:S(2)}) collective-permute-start(f32[144,128]{1,0:T(8,128)S(1)} %image_x.1.image), channel_id=1, source_target_pairs={{0,12},{1,13},{2,14},{3,15},{4,44},{5,45},{6,46},{7,47},{8,76},{9,... | collective-permute-start | bytes 221192 | tf_op jit(solution)/shard_map/image_planes/ppermute | solution.py:35
  64.0 9.2 %collective-permute-start.15 = (f32[144,128]{1,0:T(8,128)S(1)}, f32[144,128]{1,0:T(8,128)S(1)}, u32[]{:S(2)}, u32[]{:S(2)}) collective-permute-start(f32[144,128]{1,0:T(8,128)S(1)} %image_x.1.image), channel_id=1, source_target_pairs={{0,4},{1,5},{2,6},{3,7},{4,36},{5,37},{6,38},{7,39},{8,68},{9,69},... | collective-permute-start | bytes 221192 | tf_op jit(solution)/shard_map/image_planes/ppermute | solution.py:35
  64.0 9.2 %collective-permute-start.14 = (f32[144,128]{1,0:T(8,128)S(1)}, f32[144,128]{1,0:T(8,128)S(1)}, u32[]{:S(2)}, u32[]{:S(2)}) collective-permute-start(f32[144,128]{1,0:T(8,128)S(1)} %image_x.1.image), channel_id=1, source_target_pairs={{0,0},{1,1},{2,2},{3,3},{4,32},{5,33},{6,34},{7,35},{8,64},{9,65},... | collective-permute-start | bytes 221192 | tf_op jit(solution)/shard_map/image_planes/ppermute | solution.py:35
  65.3 8.0 %collective-permute-start.18 = (f32[144,128]{1,0:T(8,128)S(1)}, f32[144,128]{1,0:T(8,128)S(1)}, u32[]{:S(2)}, u32[]{:S(2)}) collective-permute-start(f32[144,128]{1,0:T(8,128)S(1)} %panel_across.1), channel_id=1, source_target_pairs={{0,16},{1,17},{2,18},{3,19},{4,20},{5,21},{6,22},{7,23},{8,24},{9,... | collective-permute-start | bytes 221192 | tf_op jit(solution)/shard_map/panel_across/ppermute | solution.py:35
  73.8 10.5 %collective-permute-start.19 = (f32[576,128]{1,0:T(8,128)S(1)}, f32[576,128]{1,0:T(8,128)S(1)}, u32[]{:S(2)}, u32[]{:S(2)}) collective-permute-start(f32[576,128]{1,0:T(8,128)S(1)} %image_planes.1.b0), channel_id=1, source_target_pairs={{0,1},{1,2},{2,3},{3,0},{4,5},{5,6},{6,7},{7,4},{8,9},{9,10},{10,1... | collective-permute-start | bytes 884744 | tf_op jit(solution)/shard_map/image_y/ppermute | solution.py:35
  76.2 15.4 %collective-permute-start.21 = (f32[576,128]{1,0:T(8,128)S(1)}, f32[576,128]{1,0:T(8,128)S(1)}, u32[]{:S(2)}, u32[]{:S(2)}) collective-permute-start(f32[576,128]{1,0:T(8,128)S(1)} %image_planes.1.b0), channel_id=1, source_target_pairs={{0,3},{1,0},{2,1},{3,2},{4,7},{5,4},{6,5},{7,6},{8,11},{9,8},{10,9... | collective-permute-start | bytes 884744 | tf_op jit(solution)/shard_map/image_y/ppermute | solution.py:35
  76.7 7.5 %collective-permute-start.20 = (f32[288,128]{1,0:T(8,128)S(1)}, f32[288,128]{1,0:T(8,128)S(1)}, u32[]{:S(2)}, u32[]{:S(2)}) collective-permute-start(f32[288,128]{1,0:T(8,128)S(1)} %image_columns.2.p0), channel_id=1, source_target_pairs={{0,32},{1,33},{2,34},{3,35},{4,36},{5,37},{6,38},{7,39},{8,40},{9,... | collective-permute-start | bytes 442376 | tf_op jit(solution)/shard_map/image_columns/ppermute | solution.py:35
  84.3 7.2 %collective-permute-start.22 = (f32[576,128]{1,0:T(8,128)S(1)}, f32[576,128]{1,0:T(8,128)S(1)}, u32[]{:S(2)}, u32[]{:S(2)}) collective-permute-start(f32[576,128]{1,0:T(8,128)S(1)} %collective-permute-done.19.b1), channel_id=1, source_target_pairs={{0,1},{1,2},{2,3},{3,0},{4,5},{5,6},{6,7},{7,4},{8,9},{9,10},{10,1... | collective-permute-start | bytes 884744 | tf_op jit(solution)/shard_map/image_far/ppermute | solution.py:35
  87.1 8.8 %collective-permute-start.25 = (f32[288,128]{1,0:T(8,128)S(1)}, f32[288,128]{1,0:T(8,128)S(1)}, u32[]{:S(2)}, u32[]{:S(2)}) collective-permute-start(f32[288,128]{1,0:T(8,128)S(1)} %image_columns.2.p0), channel_id=1, source_target_pairs={{0,64},{1,65},{2,66},{3,67},{4,68},{5,69},{6,70},{7,71},{8,72},{9,... | collective-permute-start | bytes 442376 | tf_op jit(solution)/shard_map/image_columns/ppermute | solution.py:35
  90.4 5.9 %collective-permute-start.24 = (f32[288,128]{1,0:T(8,128)S(1)}, f32[288,128]{1,0:T(8,128)S(1)}, u32[]{:S(2)}, u32[]{:S(2)}) collective-permute-start(f32[288,128]{1,0:T(8,128)S(1)} %image_columns.2.p0), channel_id=1, source_target_pairs={{0,96},{1,97},{2,98},{3,99},{4,100},{5,101},{6,102},{7,103},{8,104... | collective-permute-start | bytes 442376 | tf_op jit(solution)/shard_map/image_columns/ppermute | solution.py:35
  92.2 5.9 %collective-permute-start.23 = (f32[1152,128]{1,0:T(8,128)S(1)}, f32[1152,128]{1,0:T(8,128)S(1)}, u32[]{:S(2)}, u32[]{:S(2)}) collective-permute-start(f32[1152,128]{1,0:T(8,128)S(1)} %pick.1), channel_id=1, source_target_pairs={{0,16},{1,17},{2,18},{3,19},{4,20},{5,21},{6,22},{7,23},{8,24},{9,... | collective-permute-start | bytes 1769480 | tf_op jit(solution)/shard_map/image_swap/ppermute | solution.py:35
  96.8 8.9 %collective-permute-start.26 = (f32[1152,128]{1,0:T(8,128)S(1)}, f32[1152,128]{1,0:T(8,128)S(1)}, u32[]{:S(2)}, u32[]{:S(2)}) collective-permute-start(f32[1152,128]{1,0:T(8,128)S(1)} %image_columns.3.own), channel_id=1, source_target_pairs={{0,16},{1,17},{2,18},{3,19},{4,20},{5,21},{6,22},{7,23},{8,24},{9,... | collective-permute-start | bytes 1769480 | tf_op jit(solution)/shard_map/image_columns/ppermute | solution.py:35
  99.5 1.3 %collective-permute-start.27 = (f32[128,128]{1,0:T(8,128)S(1)}, f32[128,128]{1,0:T(8,128)S(1)}, u32[]{:S(2)}, u32[]{:S(2)}) collective-permute-start(f32[128,128]{1,0:T(8,128)S(1)} %get-tuple-element.83), channel_id=1, source_target_pairs={{0,16},{1,17},{2,18},{3,19},{4,20},{5,21},{6,22},{7,23},{8,24},{9,... | collective-permute-start | bytes 196616 | tf_op jit(solution)/shard_map/inner/ppermute | solution.py:35
  100.9 11.3 %collective-permute-start.30 = (f32[128,128]{1,0:T(8,128)S(1)}, f32[128,128]{1,0:T(8,128)S(1)}, u32[]{:S(2)}, u32[]{:S(2)}) collective-permute-start(f32[128,128]{1,0:T(8,128)S(1)} %add.14.k0), channel_id=1, source_target_pairs={{0,64},{1,65},{2,66},{3,67},{4,68},{5,69},{6,70},{7,71},{8,72},{9,... | collective-permute-start | bytes 196616 | tf_op jit(solution)/shard_map/inner/ppermute | solution.py:35
  104.3 7.9 %collective-permute-start.29 = (f32[128,128]{1,0:T(8,128)S(1)}, f32[128,128]{1,0:T(8,128)S(1)}, u32[]{:S(2)}, u32[]{:S(2)}) collective-permute-start(f32[128,128]{1,0:T(8,128)S(1)} %add.14.k0), channel_id=1, source_target_pairs={{0,96},{1,97},{2,98},{3,99},{4,100},{5,101},{6,102},{7,103},{8,104... | collective-permute-start | bytes 196616 | tf_op jit(solution)/shard_map/inner/ppermute | solution.py:35
  105.0 7.2 %collective-permute-start.28 = (f32[128,128]{1,0:T(8,128)S(1)}, f32[128,128]{1,0:T(8,128)S(1)}, u32[]{:S(2)}, u32[]{:S(2)}) collective-permute-start(f32[128,128]{1,0:T(8,128)S(1)} %add.14.k0), channel_id=1, source_target_pairs={{0,32},{1,33},{2,34},{3,35},{4,36},{5,37},{6,38},{7,39},{8,40},{9,... | collective-permute-start | bytes 196616 | tf_op jit(solution)/shard_map/inner/ppermute | solution.py:35

commit v4 on v3

--- a/solution.py
+++ b/solution.py
@@ -186,28 +186,29 @@
                     out[(4 + x) * PIECE : (5 + x) * PIECE, :] = corner[index : index + PIECE, :]
 
 
-def factor_kernel(own, r1, r3, r2, upper, upper_here, normal, work):
+def factor_kernel(own, r1, r3, r2, gram, upper, upper_here, work):
     total = (own[...] + r2[...]) + (r1[...] + r3[...])
-    gram = total[:WIDTH, :]
-    work[...] = gram
+    gram[...] = total
+    work[...] = total
     cholesky_rows(work, upper_here)
-    factor = upper_here[...]
-    upper[...] = factor
-    normal[...] = gram + full_dot(total[WIDTH:, :], factor, ((0,), (0,)))
-
-
-def combine_kernel(own, r1, r3, r2, upper, image):
+    upper[...] = upper_here[...]
+
+
+def combine_kernel(own, r1, r3, r2, gram, upper, image, normal):
     total = (own[...] + r2[...]) + (r1[...] + r3[...])
-    image[...] = total[:PIECE, :] + split_dot(total[PIECE:, :], upper[...], ((1,), (0,)))
+    image[...] = total[:PIECE, :] + split_dot(total[PIECE : 2 * PIECE, :], upper[...], ((1,), (0,)))
+    normal[...] = gram[...] + full_dot(total[2 * PIECE :, :], upper[...], ((0,), (0,)))
 
 
 def deal_kernel(place, kept, received, small, m0, m1, m3, m2):
-    small[...] = kept[8 * PIECE :, :] + received[8 * PIECE :, :]
+    small[...] = kept[8 * PIECE : 8 * PIECE + WIDTH, :] + received[8 * PIECE : 8 * PIECE + WIDTH, :]
+    top = kept[8 * PIECE + WIDTH :, :] + received[8 * PIECE + WIDTH :, :]
     for k, out in ((0, m0), (1, m1), (3, m3), (2, m2)):
         for part in range(2):
             start = pl.multiple_of((4 * part + (place[0] + k) % 4) * PIECE, 16)
             rows = pl.ds(start, PIECE)
             out[part * PIECE : (part + 1) * PIECE, :] = kept[rows, :] + received[rows, :]
+        out[2 * PIECE :, :] = top
 
 
 def untag_kernel(place, p0, p1, p3, p2, out):
@@ -441,7 +442,7 @@
     with jax.named_scope("image_core"):
         received = send(sent, other_core)
     with jax.named_scope("deal"):
-        gram, m0, m1, m3, m2 = local(deal_kernel, [shape(2 * WIDTH)] + [shape(2 * PIECE)] * 4, 8)(place, kept, received)
+        gram, m0, m1, m3, m2 = local(deal_kernel, [tile] + [shape(2 * PIECE + WIDTH)] * 4, 8)(place, kept, received)
     with jax.named_scope("gram_x"):
         grams = [gram] + ring(gram, along_x)
     with jax.named_scope("image_x"):
@@ -449,12 +450,12 @@
     with jax.named_scope("panel_across"):
         across = send(after(across, grams), planes(0))
     with jax.named_scope("factor"):
-        upper, upper_here, normal = local(factor_kernel, [tile] * 3, 4, [pltpu.VMEM((WIDTH, WIDTH), F32)], 2000000000)(
+        gram, upper, upper_here = local(factor_kernel, [tile] * 3, 4, [pltpu.VMEM((WIDTH, WIDTH), F32)], 2000000000)(
             *grams
         )
-    r1, r3, r2, across = after((r1, r3, r2, across), normal)
+    r1, r3, r2 = after((r1, r3, r2), upper_here)
     with jax.named_scope("image_x"):
-        image = local(combine_kernel, shape(PIECE), 4)(m0, r1, r3, r2, upper_here)
+        image, normal = local(combine_kernel, [shape(PIECE), tile], 4)(m0, r1, r3, r2, gram, upper_here)
 
     with jax.named_scope("image_planes"):
         planes_in = [send(image, planes(k)) for k in (0, 1, 3, 2)]

time: 118 us -> 115 us (0.975)
  starting transfers between devices: 62.9 us -> 58.2 us
  waiting for transfers between devices: 14.6 us -> 15.8 us
    ppermute x31, starting transfers between devices: 62.9 us -> 58.2 us  [send(): return lax.ppermute(value, AXES, pairs(where))]
  transfers between devices with their start and end apart: 31 -> 31, of which waited for: 11 -> 12; matrix products, arithmetic and copies ran while one was open for 0% -> 0% of each run, Pallas kernels for 24% -> 25%
where the time goes in v4:
time: 115 us; the launch traced here: 114 us
  starting transfers between devices  58.2 us (51%)
  Pallas kernels  38.1 us (33%)
  waiting for transfers between devices  15.8 us (14%)
    ppermute x31, starting transfers between devices, send(): return lax.ppermute(value, AXES, pairs(where))  58.2 us
    pallas_call x14, Pallas kernels, run(): pl.pallas_call(kernel, in_specs=specs, out_specs=outs, out_shape=out_shap...  28.6 us
    ppermute x31, waiting for transfers between devices, send(): return lax.ppermute(value, AXES, pairs(where))  15.8 us
    pallas_call x1, Pallas kernels, shards(): pl.pallas_call(last_update_kernel, in_specs=[VMEM] * 8, out_specs=anywher...  5.21 us
    pallas_call x1, Pallas kernels, shards(): pl.pallas_call(split_kernel, in_specs=[anywhere, VMEM], out_specs=[VMEM]...  4.3 us
  transfers between devices with their start and end apart: 31, of which 12 were waited for; matrix products, arithmetic and copies ran while one was open for 0% of the time, Pallas kernels for 25%

profile of v4, /device:TPU:1, one launch (start us, length us, event | category | flops | bytes accessed | tf_op | source)
XLA Modules:
  0.0 114.2 jit_solution(8663614974050251783)
XLA Ops:
  0.6 3.6 %collective-permute-start.1 = (f32[144,128]{1,0:T(8,128)}, f32[144,128]{1,0:T(8,128)S(1)}, u32[]{:S(2)}, u32[]{:S(2)}) collective-permute-start(f32[144,128]{1,0:T(8,128)} %p0.1), channel_id=1, source_target_pairs={{0,3},{1,0},{2,1},{3,2},{4,7},{5,4},{6,5},{7,6},{8,11},{9,8},{10,9... | collective-permute-start | bytes 221192 | tf_op jit(solution)/shard_map/panel_y/ppermute | solution.py:35
  4.3 1.6 %collective-permute-start.2 = (f32[144,128]{1,0:T(8,128)}, f32[144,128]{1,0:T(8,128)S(1)}, u32[]{:S(2)}, u32[]{:S(2)}) collective-permute-start(f32[144,128]{1,0:T(8,128)} %p0.1), channel_id=1, source_target_pairs={{0,2},{1,3},{2,0},{3,1},{4,6},{5,7},{6,4},{7,5},{8,10},{9,11},{10,... | collective-permute-start | bytes 221192 | tf_op jit(solution)/shard_map/panel_y/ppermute | solution.py:35
  6.0 3.5 %collective-permute-done.p1 = f32[144,128]{1,0:T(8,128)S(1)} collective-permute-done((f32[144,128]{1,0:T(8,128)}, f32[144,128]{1,0:T(8,128)S(1)}, u32[]{:S(2)}, u32[]{:S(2)}) %collective-permute-start) | collective-permute-done | bytes 73760 | tf_op jit(solution)/shard_map/panel_y/ppermute | solution.py:35
  9.9 0.9 copy-done
  10.8 0.6 panel_y.1.after.own.p0
  11.3 1.7 %collective-permute-start.4 = (f32[576,128]{1,0:T(8,128)S(1)}, f32[576,128]{1,0:T(8,128)S(1)}, u32[]{:S(2)}, u32[]{:S(2)}) collective-permute-start(f32[576,128]{1,0:T(8,128)S(1)} %panel_y.1.after.own.p0), channel_id=1, source_target_pairs={{0,12},{1,13},{2,14},{3,15},{4,0},{5,1},{6,2},{7,3},{8,4},{9,5},{1... | collective-permute-start | bytes 884744 | tf_op jit(solution)/shard_map/panel_z/ppermute | solution.py:35
  13.1 2.2 %collective-permute-start.3 = (f32[576,128]{1,0:T(8,128)S(1)}, f32[576,128]{1,0:T(8,128)S(1)}, u32[]{:S(2)}, u32[]{:S(2)}) collective-permute-start(f32[576,128]{1,0:T(8,128)S(1)} %panel_y.1.after.own.p0), channel_id=1, source_target_pairs={{0,4},{1,5},{2,6},{3,7},{4,8},{5,9},{6,10},{7,11},{8,12},{9,13},{1... | collective-permute-start | bytes 884744 | tf_op jit(solution)/shard_map/panel_z/ppermute | solution.py:35
  15.3 4.3 %split.1 = (f32[2304,1152]{1,0:T(8,128)S(1)}, bf16[2304,1152]{1,0:T(8,128)(2,1)S(1)}, bf16[2304,1152]{1,0:T(8,128)(2,1)S(1)}) custom-call(f32[2304,1152]{1,0:T(8,128)} %trailing.1, f32[576,128]{1,0:T(8,128)S(1)} %panel_y.1.after.own.p0), custom_call_target="tpu_custom_call" | custom-call | bytes 10616832 | tf_op jit(solution)/shard_map/split/pallas_call | solution.py:419
  19.6 2.0 %collective-permute-done.3.front.p1 = f32[576,128]{1,0:T(8,128)S(1)} collective-permute-done((f32[576,128]{1,0:T(8,128)S(1)}, f32[576,128]{1,0:T(8,128)S(1)}, u32[]{:S(2)}, u32[]{:S(2)}) %collective-permute-start.3) | collective-permute-done | bytes 294944 | tf_op jit(solution)/shard_map/panel_z/ppermute | solution.py:35
  21.6 1.4 %collective-permute-start.5 = (f32[576,128]{1,0:T(8,128)S(1)}, f32[576,128]{1,0:T(8,128)S(1)}, u32[]{:S(2)}, u32[]{:S(2)}) collective-permute-start(f32[576,128]{1,0:T(8,128)S(1)} %collective-permute-done.3.front.p1), channel_id=1, source_target_pairs={{0,4},{1,5},{2,6},{3,7},{4,8},{5,9},{6,10},{7,11},{8,12},{9,13},{1... | collective-permute-start | bytes 884744 | tf_op jit(solution)/shard_map/panel_far/ppermute | solution.py:35
  23.0 3.9 %near.1 = (f32[128,1152]{1,0:T(8,128)S(1)}, f32[128,128]{1,0:T(8,128)S(1)}, f32[128,128]{1,0:T(8,128)S(1)}) custom-call(s32[4]{0:T(128)S(1)} %pad_add_fusion.place, bf16[2304,1152]{1,0:T(8,128)(2,1)S(1)} %get-tuple-element.48.high, bf16[2304,1152]{1,0:T(8,128)(2,1)S(1)} %get-tuple-element.49.low, f32[576,128]{1,0:T(8,128)S(1)} %panel_y.1.after.own.p0, ...), custom_call_target="tpu_custom_call" | custom-call | flops 1698693120 | tf_op jit(solution)/shard_map/near/pallas_call | solution.py:388
  27.1 2.5 %image.1 = (f32[1408,128]{1,0:T(8,128)S(1)}, f32[1408,128]{1,0:T(8,128)S(1)}, f32[288,128]{1,0:T(8,128)S(1)}) custom-call(s32[4]{0:T(128)S(1)} %pad_add_fusion.place, f32[2304,1152]{1,0:T(8,128)S(1)} %get-tuple-element.47.whole, bf16[2304,1152]{1,0:T(8,128)(2,1)S(1)} %get-tuple-element.48.high, bf16[2304,1152]{1,0:T(8,128)(2,1)S(1)} %get-tuple-element.49.low, ...), custom_call_target="tpu_custom_call" | custom-call | flops 679477248 | tf_op jit(solution)/shard_map/image/pallas_call | solution.py:388
  29.6 6.3 %collective-permute-start.6 = (f32[1408,128]{1,0:T(8,128)S(1)}, f32[1408,128]{1,0:T(8,128)S(1)}, u32[]{:S(2)}, u32[]{:S(2)}) collective-permute-start(f32[1408,128]{1,0:T(8,128)S(1)} %get-tuple-element.57), channel_id=1, source_target_pairs={{0,16},{1,17},{2,18},{3,19},{4,20},{5,21},{6,22},{7,23},{8,24},{9,... | collective-permute-start | bytes 2162696 | tf_op jit(solution)/shard_map/image_core/ppermute | solution.py:35
  36.0 1.8 %collective-permute-done.6.received = f32[1408,128]{1,0:T(8,128)S(1)} collective-permute-done((f32[1408,128]{1,0:T(8,128)S(1)}, f32[1408,128]{1,0:T(8,128)S(1)}, u32[]{:S(2)}, u32[]{:S(2)}) %collective-permute-start.6) | collective-permute-done | bytes 720928 | tf_op jit(solution)/shard_map/image_core/ppermute | solution.py:35
  37.8 0.6 deal.1
  38.4 2.8 %collective-permute-start.9 = (f32[128,128]{1,0:T(8,128)S(1)}, f32[128,128]{1,0:T(8,128)S(1)}, u32[]{:S(2)}, u32[]{:S(2)}) collective-permute-start(f32[128,128]{1,0:T(8,128)S(1)} %get-tuple-element.58.own), channel_id=1, source_target_pairs={{0,64},{1,65},{2,66},{3,67},{4,68},{5,69},{6,70},{7,71},{8,72},{9,... | collective-permute-start | bytes 196616 | tf_op jit(solution)/shard_map/gram_x/ppermute | solution.py:35
  41.2 0.9 collective-permute-start.8
  42.1 0.6 collective-permute-start.7
  43.0 2.4 %collective-permute-start.11 = (f32[416,128]{1,0:T(8,128)S(1)}, f32[416,128]{1,0:T(8,128)S(1)}, u32[]{:S(2)}, u32[]{:S(2)}) collective-permute-start(f32[416,128]{1,0:T(8,128)S(1)} %get-tuple-element.63), channel_id=1, source_target_pairs={{0,96},{1,97},{2,98},{3,99},{4,100},{5,101},{6,102},{7,103},{8,104... | collective-permute-start | bytes 638984 | tf_op jit(solution)/shard_map/image_x/ppermute | solution.py:35
  45.4 0.6 collective-permute-start.12
  45.9 0.5 collective-permute-done.7.r1
  46.4 0.7 collective-permute-start.17
  47.1 5.3 %factor.1 = (f32[128,128]{1,0:T(8,128)S(1)}, f32[128,128]{1,0:T(8,128)}, f32[128,128]{1,0:T(8,128)S(1)}) custom-call(f32[128,128]{1,0:T(8,128)S(1)} %get-tuple-element.58.own, f32[128,128]{1,0:T(8,128)S(1)} %collective-permute-done.7.r1, f32[128,128]{1,0:T(8,128)S(1)} %collective-permute-done.8.r3, f32[128,128]{1,0:T(8,128)S(1)} %collective-permute-done.9.r2), custom_call_target="tpu_custom_call" | custom-call | flops 2000000000 | tf_op jit(solution)/shard_map/factor/pallas_call | solution.py:388
  52.4 2.3 %collective-permute-done.12.r2 = f32[416,128]{1,0:T(8,128)S(1)} collective-permute-done((f32[416,128]{1,0:T(8,128)S(1)}, f32[416,128]{1,0:T(8,128)S(1)}, u32[]{:S(2)}, u32[]{:S(2)}) %collective-permute-start.12) | collective-permute-done | bytes 213024 | tf_op jit(solution)/shard_map/image_x/ppermute | solution.py:35
  54.9 3.7 %collective-permute-start.16 = (f32[144,128]{1,0:T(8,128)S(1)}, f32[144,128]{1,0:T(8,128)S(1)}, u32[]{:S(2)}, u32[]{:S(2)}) collective-permute-start(f32[144,128]{1,0:T(8,128)S(1)} %get-tuple-element.69.image), channel_id=1, source_target_pairs={{0,8},{1,9},{2,10},{3,11},{4,40},{5,41},{6,42},{7,43},{8,72},{9,73... | collective-permute-start | bytes 221192 | tf_op jit(solution)/shard_map/image_planes/ppermute | solution.py:35
  58.6 0.7 collective-permute-start.13
  59.3 1.6 %collective-permute-done.16.p2 = f32[144,128]{1,0:T(8,128)S(1)} collective-permute-done((f32[144,128]{1,0:T(8,128)S(1)}, f32[144,128]{1,0:T(8,128)S(1)}, u32[]{:S(2)}, u32[]{:S(2)}) %collective-permute-start.16) | collective-permute-done | bytes 73760 | tf_op jit(solution)/shard_map/image_planes/ppermute | solution.py:35
  60.9 0.6 panel_across.1
  61.4 8.5 %collective-permute-start.18 = (f32[144,128]{1,0:T(8,128)S(1)}, f32[144,128]{1,0:T(8,128)S(1)}, u32[]{:S(2)}, u32[]{:S(2)}) collective-permute-start(f32[144,128]{1,0:T(8,128)S(1)} %panel_across.1), channel_id=1, source_target_pairs={{0,16},{1,17},{2,18},{3,19},{4,20},{5,21},{6,22},{7,23},{8,24},{9,... | collective-permute-start | bytes 221192 | tf_op jit(solution)/shard_map/panel_across/ppermute | solution.py:35
  69.9 1.6 %collective-permute-done.14.p1 = f32[144,128]{1,0:T(8,128)S(1)} collective-permute-done((f32[144,128]{1,0:T(8,128)S(1)}, f32[144,128]{1,0:T(8,128)S(1)}, u32[]{:S(2)}, u32[]{:S(2)}) %collective-permute-start.14) | collective-permute-done | bytes 73760 | tf_op jit(solution)/shard_map/image_planes/ppermute | solution.py:35
  71.5 0.6 image_planes.1.b0
  72.1 2.3 %collective-permute-start.19 = (f32[576,128]{1,0:T(8,128)S(1)}, f32[576,128]{1,0:T(8,128)S(1)}, u32[]{:S(2)}, u32[]{:S(2)}) collective-permute-start(f32[576,128]{1,0:T(8,128)S(1)} %image_planes.1.b0), channel_id=1, source_target_pairs={{0,1},{1,2},{2,3},{3,0},{4,5},{5,6},{6,7},{7,4},{8,9},{9,10},{10,1... | collective-permute-start | bytes 884744 | tf_op jit(solution)/shard_map/image_y/ppermute | solution.py:35
  74.4 0.6 image_columns.2.p0
  75.0 1.2 %collective-permute-start.20 = (f32[288,128]{1,0:T(8,128)S(1)}, f32[288,128]{1,0:T(8,128)S(1)}, u32[]{:S(2)}, u32[]{:S(2)}) collective-permute-start(f32[288,128]{1,0:T(8,128)S(1)} %image_columns.2.p0), channel_id=1, source_target_pairs={{0,32},{1,33},{2,34},{3,35},{4,36},{5,37},{6,38},{7,39},{8,40},{9,... | collective-permute-start | bytes 442376 | tf_op jit(solution)/shard_map/image_columns/ppermute | solution.py:35
  76.2 4.7 %inverse.1 = f32[128,128]{1,0:T(8,128)S(1)} custom-call(f32[128,128]{1,0:T(8,128)S(1)} %get-tuple-element.78.source), custom_call_target="tpu_custom_call" | custom-call | flops 2000000000 | tf_op jit(solution)/shard_map/inverse/pallas_call | solution.py:388
  80.9 2.7 %collective-permute-start.22 = (f32[576,128]{1,0:T(8,128)S(1)}, f32[576,128]{1,0:T(8,128)S(1)}, u32[]{:S(2)}, u32[]{:S(2)}) collective-permute-start(f32[576,128]{1,0:T(8,128)S(1)} %collective-permute-done.19.b1), channel_id=1, source_target_pairs={{0,1},{1,2},{2,3},{3,0},{4,5},{5,6},{6,7},{7,4},{8,9},{9,10},{10,1... | collective-permute-start | bytes 884744 | tf_op jit(solution)/shard_map/image_far/ppermute | solution.py:35
  83.6 2.8 %collective-permute-start.25 = (f32[288,128]{1,0:T(8,128)S(1)}, f32[288,128]{1,0:T(8,128)S(1)}, u32[]{:S(2)}, u32[]{:S(2)}) collective-permute-start(f32[288,128]{1,0:T(8,128)S(1)} %image_columns.2.p0), channel_id=1, source_target_pairs={{0,64},{1,65},{2,66},{3,67},{4,68},{5,69},{6,70},{7,71},{8,72},{9,... | collective-permute-start | bytes 442376 | tf_op jit(solution)/shard_map/image_columns/ppermute | solution.py:35
  86.5 0.7 collective-permute-start.24
  87.3 0.6 pick.1
  87.9 6.6 %collective-permute-start.23 = (f32[1152,128]{1,0:T(8,128)S(1)}, f32[1152,128]{1,0:T(8,128)S(1)}, u32[]{:S(2)}, u32[]{:S(2)}) collective-permute-start(f32[1152,128]{1,0:T(8,128)S(1)} %pick.1), channel_id=1, source_target_pairs={{0,16},{1,17},{2,18},{3,19},{4,20},{5,21},{6,22},{7,23},{8,24},{9,... | collective-permute-start | bytes 1769480 | tf_op jit(solution)/shard_map/image_swap/ppermute | solution.py:35
  94.5 0.6 image_columns.3.own
  95.2 0.9 collective-permute-done.23.swapped
  96.1 1.5 %gather.1 = (f32[2304,128]{1,0:T(8,128)S(1)}, f32[2304,128]{1,0:T(8,128)S(1)}, f32[128,128]{1,0:T(8,128)S(1)}) custom-call(s32[4]{0:T(128)S(1)} %pad_add_fusion.place, f32[576,128]{1,0:T(8,128)S(1)} %panel_y.1.after.own.p0, f32[576,128]{1,0:T(8,128)S(1)} %collective-permute-done.3.front.p1, f32[576,128]{1,0:T(8,128)S(1)} %collective-permute-done.4.back.p3, ...), custom_call_target="tpu_custom_call" | custom-call | tf_op jit(solution)/shard_map/gather/pallas_call | solution.py:388
  98.1 0.9 collective-permute-done.27
  99.0 1.9 %collective-permute-start.30 = (f32[128,128]{1,0:T(8,128)S(1)}, f32[128,128]{1,0:T(8,128)S(1)}, u32[]{:S(2)}, u32[]{:S(2)}) collective-permute-start(f32[128,128]{1,0:T(8,128)S(1)} %add.14.k0), channel_id=1, source_target_pairs={{0,64},{1,65},{2,66},{3,67},{4,68},{5,69},{6,70},{7,71},{8,72},{9,... | collective-permute-start | bytes 196616 | tf_op jit(solution)/shard_map/inner/ppermute | solution.py:35
  100.9 1.0 collective-permute-start.29
  102.3 6.4 %first_update.1 = (f32[2304,1152]{1,0:T(8,128)S(1)}, f32[128,1152]{1,0:T(8,128)S(1)}) custom-call(s32[4]{0:T(128)S(1)} %pad_add_fusion.place, f32[2304,1152]{1,0:T(8,128)S(1)} %get-tuple-element.47.whole, f32[2304,128]{1,0:T(8,128)S(1)} %get-tuple-element.80.shifted_rows, f32[2304,128]{1,0:T(8,128)S(1)} %get-tuple-element.81.image_rows, ...), custom_call_target="tpu_custom_call" | custom-call | flops 4076863488 | tf_op jit(solution)/shard_map/first_update/pallas_call | solution.py:388
  108.8 5.2 %last_update.1 = f32[2304,1152]{1,0:T(8,128)} custom-call(f32[2304,1152]{1,0:T(8,128)S(1)} %get-tuple-element.87.base, f32[2304,128]{1,0:T(8,128)S(1)} %get-tuple-element.80.shifted_rows, f32[128,1152]{1,0:T(8,128)S(1)} %get-tuple-element.88.turned, f32[128,128]{1,0:T(8,128)S(1)} %inverse.1, f32[128,128]{1,0:T(8,128)S(1)} %add.14.k0, ...), custom_call_target="tpu_custom_call" | custom-call | flops 2717908992 | bytes 10616832 | tf_op jit(solution)/shard_map/last_update/pallas_call | solution.py:508
  (34 shorter events, 2.5 us)
Async XLA Ops:
  0.6 5.4 %collective-permute-start.1 = (f32[144,128]{1,0:T(8,128)}, f32[144,128]{1,0:T(8,128)S(1)}, u32[]{:S(2)}, u32[]{:S(2)}) collective-permute-start(f32[144,128]{1,0:T(8,128)} %p0.1), channel_id=1, source_target_pairs={{0,3},{1,0},{2,1},{3,2},{4,7},{5,4},{6,5},{7,6},{8,11},{9,8},{10,9... | collective-permute-start | bytes 221192 | tf_op jit(solution)/shard_map/panel_y/ppermute | solution.py:35
  4.3 5.2 %collective-permute-start = (f32[144,128]{1,0:T(8,128)}, f32[144,128]{1,0:T(8,128)S(1)}, u32[]{:S(2)}, u32[]{:S(2)}) collective-permute-start(f32[144,128]{1,0:T(8,128)} %p0.1), channel_id=1, source_target_pairs={{0,1},{1,2},{2,3},{3,0},{4,5},{5,6},{6,7},{7,4},{8,9},{9,10},{10,1... | collective-permute-start | bytes 221192 | tf_op jit(solution)/shard_map/panel_y/ppermute | solution.py:35
  4.3 5.6 %collective-permute-start.2 = (f32[144,128]{1,0:T(8,128)}, f32[144,128]{1,0:T(8,128)S(1)}, u32[]{:S(2)}, u32[]{:S(2)}) collective-permute-start(f32[144,128]{1,0:T(8,128)} %p0.1), channel_id=1, source_target_pairs={{0,2},{1,3},{2,0},{3,1},{4,6},{5,7},{6,4},{7,5},{8,10},{9,11},{10,... | collective-permute-start | bytes 221192 | tf_op jit(solution)/shard_map/panel_y/ppermute | solution.py:35
  9.9 0.9 copy-start
  11.3 8.2 %collective-permute-start.4 = (f32[576,128]{1,0:T(8,128)S(1)}, f32[576,128]{1,0:T(8,128)S(1)}, u32[]{:S(2)}, u32[]{:S(2)}) collective-permute-start(f32[576,128]{1,0:T(8,128)S(1)} %panel_y.1.after.own.p0), channel_id=1, source_target_pairs={{0,12},{1,13},{2,14},{3,15},{4,0},{5,1},{6,2},{7,3},{8,4},{9,5},{1... | collective-permute-start | bytes 884744 | tf_op jit(solution)/shard_map/panel_z/ppermute | solution.py:35
  13.1 8.5 %collective-permute-start.3 = (f32[576,128]{1,0:T(8,128)S(1)}, f32[576,128]{1,0:T(8,128)S(1)}, u32[]{:S(2)}, u32[]{:S(2)}) collective-permute-start(f32[576,128]{1,0:T(8,128)S(1)} %panel_y.1.after.own.p0), channel_id=1, source_target_pairs={{0,4},{1,5},{2,6},{3,7},{4,8},{5,9},{6,10},{7,11},{8,12},{9,13},{1... | collective-permute-start | bytes 884744 | tf_op jit(solution)/shard_map/panel_z/ppermute | solution.py:35
  21.6 5.6 %collective-permute-start.5 = (f32[576,128]{1,0:T(8,128)S(1)}, f32[576,128]{1,0:T(8,128)S(1)}, u32[]{:S(2)}, u32[]{:S(2)}) collective-permute-start(f32[576,128]{1,0:T(8,128)S(1)} %collective-permute-done.3.front.p1), channel_id=1, source_target_pairs={{0,4},{1,5},{2,6},{3,7},{4,8},{5,9},{6,10},{7,11},{8,12},{9,13},{1... | collective-permute-start | bytes 884744 | tf_op jit(solution)/shard_map/panel_far/ppermute | solution.py:35
  29.6 8.2 %collective-permute-start.6 = (f32[1408,128]{1,0:T(8,128)S(1)}, f32[1408,128]{1,0:T(8,128)S(1)}, u32[]{:S(2)}, u32[]{:S(2)}) collective-permute-start(f32[1408,128]{1,0:T(8,128)S(1)} %get-tuple-element.57), channel_id=1, source_target_pairs={{0,16},{1,17},{2,18},{3,19},{4,20},{5,21},{6,22},{7,23},{8,24},{9,... | collective-permute-start | bytes 2162696 | tf_op jit(solution)/shard_map/image_core/ppermute | solution.py:35
  38.4 7.0 %collective-permute-start.9 = (f32[128,128]{1,0:T(8,128)S(1)}, f32[128,128]{1,0:T(8,128)S(1)}, u32[]{:S(2)}, u32[]{:S(2)}) collective-permute-start(f32[128,128]{1,0:T(8,128)S(1)} %get-tuple-element.58.own), channel_id=1, source_target_pairs={{0,64},{1,65},{2,66},{3,67},{4,68},{5,69},{6,70},{7,71},{8,72},{9,... | collective-permute-start | bytes 196616 | tf_op jit(solution)/shard_map/gram_x/ppermute | solution.py:35
  41.2 4.7 %collective-permute-start.8 = (f32[128,128]{1,0:T(8,128)S(1)}, f32[128,128]{1,0:T(8,128)S(1)}, u32[]{:S(2)}, u32[]{:S(2)}) collective-permute-start(f32[128,128]{1,0:T(8,128)S(1)} %get-tuple-element.58.own), channel_id=1, source_target_pairs={{0,96},{1,97},{2,98},{3,99},{4,100},{5,101},{6,102},{7,103},{8,104... | collective-permute-start | bytes 196616 | tf_op jit(solution)/shard_map/gram_x/ppermute | solution.py:35
  42.1 4.3 %collective-permute-start.7 = (f32[128,128]{1,0:T(8,128)S(1)}, f32[128,128]{1,0:T(8,128)S(1)}, u32[]{:S(2)}, u32[]{:S(2)}) collective-permute-start(f32[128,128]{1,0:T(8,128)S(1)} %get-tuple-element.58.own), channel_id=1, source_target_pairs={{0,32},{1,33},{2,34},{3,35},{4,36},{5,37},{6,38},{7,39},{8,40},{9,... | collective-permute-start | bytes 196616 | tf_op jit(solution)/shard_map/gram_x/ppermute | solution.py:35
  42.7 9.7 %collective-permute-start.10 = (f32[416,128]{1,0:T(8,128)S(1)}, f32[416,128]{1,0:T(8,128)S(1)}, u32[]{:S(2)}, u32[]{:S(2)}) collective-permute-start(f32[416,128]{1,0:T(8,128)S(1)} %get-tuple-element.62), channel_id=1, source_target_pairs={{0,32},{1,33},{2,34},{3,35},{4,36},{5,37},{6,38},{7,39},{8,40},{9,... | collective-permute-start | bytes 638984 | tf_op jit(solution)/shard_map/image_x/ppermute | solution.py:35
  43.0 9.4 %collective-permute-start.11 = (f32[416,128]{1,0:T(8,128)S(1)}, f32[416,128]{1,0:T(8,128)S(1)}, u32[]{:S(2)}, u32[]{:S(2)}) collective-permute-start(f32[416,128]{1,0:T(8,128)S(1)} %get-tuple-element.63), channel_id=1, source_target_pairs={{0,96},{1,97},{2,98},{3,99},{4,100},{5,101},{6,102},{7,103},{8,104... | collective-permute-start | bytes 638984 | tf_op jit(solution)/shard_map/image_x/ppermute | solution.py:35
  45.4 9.2 %collective-permute-start.12 = (f32[416,128]{1,0:T(8,128)S(1)}, f32[416,128]{1,0:T(8,128)S(1)}, u32[]{:S(2)}, u32[]{:S(2)}) collective-permute-start(f32[416,128]{1,0:T(8,128)S(1)} %get-tuple-element.64), channel_id=1, source_target_pairs={{0,64},{1,65},{2,66},{3,67},{4,68},{5,69},{6,70},{7,71},{8,72},{9,... | collective-permute-start | bytes 638984 | tf_op jit(solution)/shard_map/image_x/ppermute | solution.py:35
  46.4 12.9 %collective-permute-start.17 = (f32[288,128]{1,0:T(8,128)S(1)}, f32[288,128]{1,0:T(8,128)S(1)}, u32[]{:S(2)}, u32[]{:S(2)}) collective-permute-start(f32[288,128]{1,0:T(8,128)S(1)} %get-tuple-element.71), channel_id=1, source_target_pairs={{0,0},{1,1},{2,2},{3,3},{4,32},{5,33},{6,34},{7,35},{8,64},{9,65},... | collective-permute-start | bytes 442376 | tf_op jit(solution)/shard_map/panel_across/ppermute | solution.py:35
  54.9 5.9 %collective-permute-start.16 = (f32[144,128]{1,0:T(8,128)S(1)}, f32[144,128]{1,0:T(8,128)S(1)}, u32[]{:S(2)}, u32[]{:S(2)}) collective-permute-start(f32[144,128]{1,0:T(8,128)S(1)} %get-tuple-element.69.image), channel_id=1, source_target_pairs={{0,8},{1,9},{2,10},{3,11},{4,40},{5,41},{6,42},{7,43},{8,72},{9,73... | collective-permute-start | bytes 221192 | tf_op jit(solution)/shard_map/image_planes/ppermute | solution.py:35
  58.6 11.3 %collective-permute-start.15 = (f32[144,128]{1,0:T(8,128)S(1)}, f32[144,128]{1,0:T(8,128)S(1)}, u32[]{:S(2)}, u32[]{:S(2)}) collective-permute-start(f32[144,128]{1,0:T(8,128)S(1)} %get-tuple-element.69.image), channel_id=1, source_target_pairs={{0,12},{1,13},{2,14},{3,15},{4,44},{5,45},{6,46},{7,47},{8,76},{9,... | collective-permute-start | bytes 221192 | tf_op jit(solution)/shard_map/image_planes/ppermute | solution.py:35
  58.6 12.9 %collective-permute-start.14 = (f32[144,128]{1,0:T(8,128)S(1)}, f32[144,128]{1,0:T(8,128)S(1)}, u32[]{:S(2)}, u32[]{:S(2)}) collective-permute-start(f32[144,128]{1,0:T(8,128)S(1)} %get-tuple-element.69.image), channel_id=1, source_target_pairs={{0,4},{1,5},{2,6},{3,7},{4,36},{5,37},{6,38},{7,39},{8,68},{9,69},... | collective-permute-start | bytes 221192 | tf_op jit(solution)/shard_map/image_planes/ppermute | solution.py:35
  58.6 12.9 %collective-permute-start.13 = (f32[144,128]{1,0:T(8,128)S(1)}, f32[144,128]{1,0:T(8,128)S(1)}, u32[]{:S(2)}, u32[]{:S(2)}) collective-permute-start(f32[144,128]{1,0:T(8,128)S(1)} %get-tuple-element.69.image), channel_id=1, source_target_pairs={{0,0},{1,1},{2,2},{3,3},{4,32},{5,33},{6,34},{7,35},{8,64},{9,65},... | collective-permute-start | bytes 221192 | tf_op jit(solution)/shard_map/image_planes/ppermute | solution.py:35
  61.4 10.1 %collective-permute-start.18 = (f32[144,128]{1,0:T(8,128)S(1)}, f32[144,128]{1,0:T(8,128)S(1)}, u32[]{:S(2)}, u32[]{:S(2)}) collective-permute-start(f32[144,128]{1,0:T(8,128)S(1)} %panel_across.1), channel_id=1, source_target_pairs={{0,16},{1,17},{2,18},{3,19},{4,20},{5,21},{6,22},{7,23},{8,24},{9,... | collective-permute-start | bytes 221192 | tf_op jit(solution)/shard_map/panel_across/ppermute | solution.py:35
  72.1 8.8 %collective-permute-start.19 = (f32[576,128]{1,0:T(8,128)S(1)}, f32[576,128]{1,0:T(8,128)S(1)}, u32[]{:S(2)}, u32[]{:S(2)}) collective-permute-start(f32[576,128]{1,0:T(8,128)S(1)} %image_planes.1.b0), channel_id=1, source_target_pairs={{0,1},{1,2},{2,3},{3,0},{4,5},{5,6},{6,7},{7,4},{8,9},{9,10},{10,1... | collective-permute-start | bytes 884744 | tf_op jit(solution)/shard_map/image_y/ppermute | solution.py:35
  74.4 12.8 %collective-permute-start.21 = (f32[576,128]{1,0:T(8,128)S(1)}, f32[576,128]{1,0:T(8,128)S(1)}, u32[]{:S(2)}, u32[]{:S(2)}) collective-permute-start(f32[576,128]{1,0:T(8,128)S(1)} %image_planes.1.b0), channel_id=1, source_target_pairs={{0,3},{1,0},{2,1},{3,2},{4,7},{5,4},{6,5},{7,6},{8,11},{9,8},{10,9... | collective-permute-start | bytes 884744 | tf_op jit(solution)/shard_map/image_y/ppermute | solution.py:35
  75.0 5.8 %collective-permute-start.20 = (f32[288,128]{1,0:T(8,128)S(1)}, f32[288,128]{1,0:T(8,128)S(1)}, u32[]{:S(2)}, u32[]{:S(2)}) collective-permute-start(f32[288,128]{1,0:T(8,128)S(1)} %image_columns.2.p0), channel_id=1, source_target_pairs={{0,32},{1,33},{2,34},{3,35},{4,36},{5,37},{6,38},{7,39},{8,40},{9,... | collective-permute-start | bytes 442376 | tf_op jit(solution)/shard_map/image_columns/ppermute | solution.py:35
  80.9 6.4 %collective-permute-start.22 = (f32[576,128]{1,0:T(8,128)S(1)}, f32[576,128]{1,0:T(8,128)S(1)}, u32[]{:S(2)}, u32[]{:S(2)}) collective-permute-start(f32[576,128]{1,0:T(8,128)S(1)} %collective-permute-done.19.b1), channel_id=1, source_target_pairs={{0,1},{1,2},{2,3},{3,0},{4,5},{5,6},{6,7},{7,4},{8,9},{9,10},{10,1... | collective-permute-start | bytes 884744 | tf_op jit(solution)/shard_map/image_far/ppermute | solution.py:35
  83.6 10.9 %collective-permute-start.25 = (f32[288,128]{1,0:T(8,128)S(1)}, f32[288,128]{1,0:T(8,128)S(1)}, u32[]{:S(2)}, u32[]{:S(2)}) collective-permute-start(f32[288,128]{1,0:T(8,128)S(1)} %image_columns.2.p0), channel_id=1, source_target_pairs={{0,64},{1,65},{2,66},{3,67},{4,68},{5,69},{6,70},{7,71},{8,72},{9,... | collective-permute-start | bytes 442376 | tf_op jit(solution)/shard_map/image_columns/ppermute | solution.py:35
  86.5 8.0 %collective-permute-start.24 = (f32[288,128]{1,0:T(8,128)S(1)}, f32[288,128]{1,0:T(8,128)S(1)}, u32[]{:S(2)}, u32[]{:S(2)}) collective-permute-start(f32[288,128]{1,0:T(8,128)S(1)} %image_columns.2.p0), channel_id=1, source_target_pairs={{0,96},{1,97},{2,98},{3,99},{4,100},{5,101},{6,102},{7,103},{8,104... | collective-permute-start | bytes 442376 | tf_op jit(solution)/shard_map/image_columns/ppermute | solution.py:35
  87.9 8.2 %collective-permute-start.23 = (f32[1152,128]{1,0:T(8,128)S(1)}, f32[1152,128]{1,0:T(8,128)S(1)}, u32[]{:S(2)}, u32[]{:S(2)}) collective-permute-start(f32[1152,128]{1,0:T(8,128)S(1)} %pick.1), channel_id=1, source_target_pairs={{0,16},{1,17},{2,18},{3,19},{4,20},{5,21},{6,22},{7,23},{8,24},{9,... | collective-permute-start | bytes 1769480 | tf_op jit(solution)/shard_map/image_swap/ppermute | solution.py:35
  95.1 7.2 %collective-permute-start.26 = (f32[1152,128]{1,0:T(8,128)S(1)}, f32[1152,128]{1,0:T(8,128)S(1)}, u32[]{:S(2)}, u32[]{:S(2)}) collective-permute-start(f32[1152,128]{1,0:T(8,128)S(1)} %image_columns.3.own), channel_id=1, source_target_pairs={{0,16},{1,17},{2,18},{3,19},{4,20},{5,21},{6,22},{7,23},{8,24},{9,... | collective-permute-start | bytes 1769480 | tf_op jit(solution)/shard_map/image_columns/ppermute | solution.py:35
  97.6 1.4 %collective-permute-start.27 = (f32[128,128]{1,0:T(8,128)S(1)}, f32[128,128]{1,0:T(8,128)S(1)}, u32[]{:S(2)}, u32[]{:S(2)}) collective-permute-start(f32[128,128]{1,0:T(8,128)S(1)} %get-tuple-element.85), channel_id=1, source_target_pairs={{0,16},{1,17},{2,18},{3,19},{4,20},{5,21},{6,22},{7,23},{8,24},{9,... | collective-permute-start | bytes 196616 | tf_op jit(solution)/shard_map/inner/ppermute | solution.py:35
  99.0 9.8 %collective-permute-start.30 = (f32[128,128]{1,0:T(8,128)S(1)}, f32[128,128]{1,0:T(8,128)S(1)}, u32[]{:S(2)}, u32[]{:S(2)}) collective-permute-start(f32[128,128]{1,0:T(8,128)S(1)} %add.14.k0), channel_id=1, source_target_pairs={{0,64},{1,65},{2,66},{3,67},{4,68},{5,69},{6,70},{7,71},{8,72},{9,... | collective-permute-start | bytes 196616 | tf_op jit(solution)/shard_map/inner/ppermute | solution.py:35
  100.9 7.9 %collective-permute-start.29 = (f32[128,128]{1,0:T(8,128)S(1)}, f32[128,128]{1,0:T(8,128)S(1)}, u32[]{:S(2)}, u32[]{:S(2)}) collective-permute-start(f32[128,128]{1,0:T(8,128)S(1)} %add.14.k0), channel_id=1, source_target_pairs={{0,96},{1,97},{2,98},{3,99},{4,100},{5,101},{6,102},{7,103},{8,104... | collective-permute-start | bytes 196616 | tf_op jit(solution)/shard_map/inner/ppermute | solution.py:35
  101.9 6.9 %collective-permute-start.28 = (f32[128,128]{1,0:T(8,128)S(1)}, f32[128,128]{1,0:T(8,128)S(1)}, u32[]{:S(2)}, u32[]{:S(2)}) collective-permute-start(f32[128,128]{1,0:T(8,128)S(1)} %add.14.k0), channel_id=1, source_target_pairs={{0,32},{1,33},{2,34},{3,35},{4,36},{5,37},{6,38},{7,39},{8,40},{9,... | collective-permute-start | bytes 196616 | tf_op jit(solution)/shard_map/inner/ppermute | solution.py:35

commit v5 on v4

--- a/solution.py
+++ b/solution.py
@@ -18,12 +18,14 @@
 SMEM = pl.BlockSpec(memory_space=pltpu.SMEM)
 
 
-def pairs(where):
+def pairs(where, only=None):
     result = []
     for x in range(4):
         for core in range(2):
             for z in range(4):
                 for y in range(4):
+                    if only is not None and not only(x, core, z, y):
+                        continue
                     tx, tcore, tz, ty = where(x, core, z, y)
                     source = (2 * x + core) * 16 + 4 * z + y
                     target = (2 * tx + tcore) * 16 + 4 * tz + ty
@@ -31,8 +33,8 @@
     return result
 
 
-def send(value, where):
-    return lax.ppermute(value, AXES, pairs(where))
+def send(value, where, only=None):
+    return lax.ppermute(value, AXES, pairs(where, only))
 
 
 def along_x(k):
@@ -448,7 +450,7 @@
     with jax.named_scope("image_x"):
         r1, r3, r2 = (send(m, along_x(k)) for m, k in ((m1, 1), (m3, 3), (m2, 2)))
     with jax.named_scope("panel_across"):
-        across = send(after(across, grams), planes(0))
+        across = send(after(across, grams), planes(0), lambda x, core, z, y: core == y // 2)
     with jax.named_scope("factor"):
         gram, upper, upper_here = local(factor_kernel, [tile] * 3, 4, [pltpu.VMEM((WIDTH, WIDTH), F32)], 2000000000)(
             *grams

time: 115 us -> 113 us (0.983)
  starting transfers between devices: 58.2 us -> 49.1 us
  waiting for transfers between devices: 15.8 us -> 22.5 us
    ppermute x31, starting transfers between devices: 58.2 us -> 49.1 us  [send(): return lax.ppermute(value, AXES, pairs(where, only))]
    ppermute x31, waiting for transfers between devices: 15.8 us -> 22.5 us  [send(): return lax.ppermute(value, AXES, pairs(where, only))]
  transfers between devices with their start and end apart: 31 -> 31, of which waited for: 12 -> 13; matrix products, arithmetic and copies ran while one was open for 0% -> 0% of each run, Pallas kernels for 25% -> 26%
where the time goes in v5:
time: 113 us; the launch traced here: 112 us
  starting transfers between devices  49.1 us (43%)
  Pallas kernels  38.1 us (34%)
  waiting for transfers between devices  22.5 us (20%)
    ppermute x31, starting transfers between devices, send(): return lax.ppermute(value, AXES, pairs(where, only))  49.1 us
    pallas_call x14, Pallas kernels, run(): pl.pallas_call(kernel, in_specs=specs, out_specs=outs, out_shape=out_shap...  28.6 us
    ppermute x31, waiting for transfers between devices, send(): return lax.ppermute(value, AXES, pairs(where, only))  22.5 us
    pallas_call x1, Pallas kernels, shards(): pl.pallas_call(last_update_kernel, in_specs=[VMEM] * 8, out_specs=anywher...  5.21 us
    pallas_call x1, Pallas kernels, shards(): pl.pallas_call(split_kernel, in_specs=[anywhere, VMEM], out_specs=[VMEM]...  4.3 us
  transfers between devices with their start and end apart: 31, of which 13 were waited for; matrix products, arithmetic and copies ran while one was open for 0% of the time, Pallas kernels for 26%

profile of v5, /device:TPU:1, one launch (start us, length us, event | category | flops | bytes accessed | tf_op | source)
XLA Modules:
  0.0 111.7 jit_solution(13205187418948795542)
XLA Ops:
  0.6 3.6 %collective-permute-start.1 = (f32[144,128]{1,0:T(8,128)}, f32[144,128]{1,0:T(8,128)S(1)}, u32[]{:S(2)}, u32[]{:S(2)}) collective-permute-start(f32[144,128]{1,0:T(8,128)} %p0.1), channel_id=1, source_target_pairs={{0,3},{1,0},{2,1},{3,2},{4,7},{5,4},{6,5},{7,6},{8,11},{9,8},{10,9... | collective-permute-start | bytes 221192 | tf_op jit(solution)/shard_map/panel_y/ppermute | solution.py:37
  4.3 1.6 %collective-permute-start.2 = (f32[144,128]{1,0:T(8,128)}, f32[144,128]{1,0:T(8,128)S(1)}, u32[]{:S(2)}, u32[]{:S(2)}) collective-permute-start(f32[144,128]{1,0:T(8,128)} %p0.1), channel_id=1, source_target_pairs={{0,2},{1,3},{2,0},{3,1},{4,6},{5,7},{6,4},{7,5},{8,10},{9,11},{10,... | collective-permute-start | bytes 221192 | tf_op jit(solution)/shard_map/panel_y/ppermute | solution.py:37
  6.0 3.5 %collective-permute-done.p1 = f32[144,128]{1,0:T(8,128)S(1)} collective-permute-done((f32[144,128]{1,0:T(8,128)}, f32[144,128]{1,0:T(8,128)S(1)}, u32[]{:S(2)}, u32[]{:S(2)}) %collective-permute-start) | collective-permute-done | bytes 73760 | tf_op jit(solution)/shard_map/panel_y/ppermute | solution.py:37
  9.9 0.9 copy-done
  10.8 0.6 panel_y.1.after.own.p0
  11.3 1.7 %collective-permute-start.4 = (f32[576,128]{1,0:T(8,128)S(1)}, f32[576,128]{1,0:T(8,128)S(1)}, u32[]{:S(2)}, u32[]{:S(2)}) collective-permute-start(f32[576,128]{1,0:T(8,128)S(1)} %panel_y.1.after.own.p0), channel_id=1, source_target_pairs={{0,12},{1,13},{2,14},{3,15},{4,0},{5,1},{6,2},{7,3},{8,4},{9,5},{1... | collective-permute-start | bytes 884744 | tf_op jit(solution)/shard_map/panel_z/ppermute | solution.py:37
  13.1 2.2 %collective-permute-start.3 = (f32[576,128]{1,0:T(8,128)S(1)}, f32[576,128]{1,0:T(8,128)S(1)}, u32[]{:S(2)}, u32[]{:S(2)}) collective-permute-start(f32[576,128]{1,0:T(8,128)S(1)} %panel_y.1.after.own.p0), channel_id=1, source_target_pairs={{0,4},{1,5},{2,6},{3,7},{4,8},{5,9},{6,10},{7,11},{8,12},{9,13},{1... | collective-permute-start | bytes 884744 | tf_op jit(solution)/shard_map/panel_z/ppermute | solution.py:37
  15.3 4.3 %split.1 = (f32[2304,1152]{1,0:T(8,128)S(1)}, bf16[2304,1152]{1,0:T(8,128)(2,1)S(1)}, bf16[2304,1152]{1,0:T(8,128)(2,1)S(1)}) custom-call(f32[2304,1152]{1,0:T(8,128)} %trailing.1, f32[576,128]{1,0:T(8,128)S(1)} %panel_y.1.after.own.p0), custom_call_target="tpu_custom_call" | custom-call | bytes 10616832 | tf_op jit(solution)/shard_map/split/pallas_call | solution.py:421
  19.6 2.0 %collective-permute-done.3.front.p1 = f32[576,128]{1,0:T(8,128)S(1)} collective-permute-done((f32[576,128]{1,0:T(8,128)S(1)}, f32[576,128]{1,0:T(8,128)S(1)}, u32[]{:S(2)}, u32[]{:S(2)}) %collective-permute-start.3) | collective-permute-done | bytes 294944 | tf_op jit(solution)/shard_map/panel_z/ppermute | solution.py:37
  21.6 1.4 %collective-permute-start.5 = (f32[576,128]{1,0:T(8,128)S(1)}, f32[576,128]{1,0:T(8,128)S(1)}, u32[]{:S(2)}, u32[]{:S(2)}) collective-permute-start(f32[576,128]{1,0:T(8,128)S(1)} %collective-permute-done.3.front.p1), channel_id=1, source_target_pairs={{0,4},{1,5},{2,6},{3,7},{4,8},{5,9},{6,10},{7,11},{8,12},{9,13},{1... | collective-permute-start | bytes 884744 | tf_op jit(solution)/shard_map/panel_far/ppermute | solution.py:37
  23.0 3.9 %near.1 = (f32[128,1152]{1,0:T(8,128)S(1)}, f32[128,128]{1,0:T(8,128)S(1)}, f32[128,128]{1,0:T(8,128)S(1)}) custom-call(s32[4]{0:T(128)S(1)} %pad_add_fusion.place, bf16[2304,1152]{1,0:T(8,128)(2,1)S(1)} %get-tuple-element.48.high, bf16[2304,1152]{1,0:T(8,128)(2,1)S(1)} %get-tuple-element.49.low, f32[576,128]{1,0:T(8,128)S(1)} %panel_y.1.after.own.p0, ...), custom_call_target="tpu_custom_call" | custom-call | flops 1698693120 | tf_op jit(solution)/shard_map/near/pallas_call | solution.py:390
  27.1 2.5 %image.1 = (f32[1408,128]{1,0:T(8,128)S(1)}, f32[1408,128]{1,0:T(8,128)S(1)}, f32[288,128]{1,0:T(8,128)S(1)}) custom-call(s32[4]{0:T(128)S(1)} %pad_add_fusion.place, f32[2304,1152]{1,0:T(8,128)S(1)} %get-tuple-element.47.whole, bf16[2304,1152]{1,0:T(8,128)(2,1)S(1)} %get-tuple-element.48.high, bf16[2304,1152]{1,0:T(8,128)(2,1)S(1)} %get-tuple-element.49.low, ...), custom_call_target="tpu_custom_call" | custom-call | flops 679477248 | tf_op jit(solution)/shard_map/image/pallas_call | solution.py:390
  29.6 6.3 %collective-permute-start.6 = (f32[1408,128]{1,0:T(8,128)S(1)}, f32[1408,128]{1,0:T(8,128)S(1)}, u32[]{:S(2)}, u32[]{:S(2)}) collective-permute-start(f32[1408,128]{1,0:T(8,128)S(1)} %get-tuple-element.57), channel_id=1, source_target_pairs={{0,16},{1,17},{2,18},{3,19},{4,20},{5,21},{6,22},{7,23},{8,24},{9,... | collective-permute-start | bytes 2162696 | tf_op jit(solution)/shard_map/image_core/ppermute | solution.py:37
  36.0 1.8 %collective-permute-done.6.received = f32[1408,128]{1,0:T(8,128)S(1)} collective-permute-done((f32[1408,128]{1,0:T(8,128)S(1)}, f32[1408,128]{1,0:T(8,128)S(1)}, u32[]{:S(2)}, u32[]{:S(2)}) %collective-permute-start.6) | collective-permute-done | bytes 720928 | tf_op jit(solution)/shard_map/image_core/ppermute | solution.py:37
  37.8 0.6 deal.1
  38.4 2.8 %collective-permute-start.9 = (f32[128,128]{1,0:T(8,128)S(1)}, f32[128,128]{1,0:T(8,128)S(1)}, u32[]{:S(2)}, u32[]{:S(2)}) collective-permute-start(f32[128,128]{1,0:T(8,128)S(1)} %get-tuple-element.58.own), channel_id=1, source_target_pairs={{0,64},{1,65},{2,66},{3,67},{4,68},{5,69},{6,70},{7,71},{8,72},{9,... | collective-permute-start | bytes 196616 | tf_op jit(solution)/shard_map/gram_x/ppermute | solution.py:37
  41.2 0.9 collective-permute-start.8
  42.1 0.6 collective-permute-start.7
  43.0 2.4 %collective-permute-start.11 = (f32[416,128]{1,0:T(8,128)S(1)}, f32[416,128]{1,0:T(8,128)S(1)}, u32[]{:S(2)}, u32[]{:S(2)}) collective-permute-start(f32[416,128]{1,0:T(8,128)S(1)} %get-tuple-element.63), channel_id=1, source_target_pairs={{0,96},{1,97},{2,98},{3,99},{4,100},{5,101},{6,102},{7,103},{8,104... | collective-permute-start | bytes 638984 | tf_op jit(solution)/shard_map/image_x/ppermute | solution.py:37
  45.4 0.6 collective-permute-start.12
  45.9 0.5 collective-permute-done.7.r1
  46.4 0.7 collective-permute-start.17
  47.1 5.3 %factor.1 = (f32[128,128]{1,0:T(8,128)S(1)}, f32[128,128]{1,0:T(8,128)}, f32[128,128]{1,0:T(8,128)S(1)}) custom-call(f32[128,128]{1,0:T(8,128)S(1)} %get-tuple-element.58.own, f32[128,128]{1,0:T(8,128)S(1)} %collective-permute-done.7.r1, f32[128,128]{1,0:T(8,128)S(1)} %collective-permute-done.8.r3, f32[128,128]{1,0:T(8,128)S(1)} %collective-permute-done.9.r2), custom_call_target="tpu_custom_call" | custom-call | flops 2000000000 | tf_op jit(solution)/shard_map/factor/pallas_call | solution.py:390
  52.4 2.3 %collective-permute-done.12.r2 = f32[416,128]{1,0:T(8,128)S(1)} collective-permute-done((f32[416,128]{1,0:T(8,128)S(1)}, f32[416,128]{1,0:T(8,128)S(1)}, u32[]{:S(2)}, u32[]{:S(2)}) %collective-permute-start.12) | collective-permute-done | bytes 213024 | tf_op jit(solution)/shard_map/image_x/ppermute | solution.py:37
  55.3 0.5 collective-permute-start.14
  55.8 0.7 collective-permute-start.13
  56.5 3.3 %collective-permute-done.16.p2 = f32[144,128]{1,0:T(8,128)S(1)} collective-permute-done((f32[144,128]{1,0:T(8,128)S(1)}, f32[144,128]{1,0:T(8,128)S(1)}, u32[]{:S(2)}, u32[]{:S(2)}) %collective-permute-start.16) | collective-permute-done | bytes 73760 | tf_op jit(solution)/shard_map/image_planes/ppermute | solution.py:37
  59.8 0.6 panel_across.1
  60.4 5.2 %collective-permute-start.18 = (f32[144,128]{1,0:T(8,128)S(1)}, f32[144,128]{1,0:T(8,128)S(1)}, u32[]{:S(2)}, u32[]{:S(2)}) collective-permute-start(f32[144,128]{1,0:T(8,128)S(1)} %panel_across.1), channel_id=1, source_target_pairs={{0,16},{1,17},{2,18},{3,19},{4,20},{5,21},{6,22},{7,23},{8,24},{9,... | collective-permute-start | bytes 221192 | tf_op jit(solution)/shard_map/panel_across/ppermute | solution.py:37
  65.6 2.5 %collective-permute-done.14.p1 = f32[144,128]{1,0:T(8,128)S(1)} collective-permute-done((f32[144,128]{1,0:T(8,128)S(1)}, f32[144,128]{1,0:T(8,128)S(1)}, u32[]{:S(2)}, u32[]{:S(2)}) %collective-permute-start.14) | collective-permute-done | bytes 73760 | tf_op jit(solution)/shard_map/image_planes/ppermute | solution.py:37
  68.0 0.6 image_planes.1.b0
  68.6 5.9 %collective-permute-start.19 = (f32[576,128]{1,0:T(8,128)S(1)}, f32[576,128]{1,0:T(8,128)S(1)}, u32[]{:S(2)}, u32[]{:S(2)}) collective-permute-start(f32[576,128]{1,0:T(8,128)S(1)} %image_planes.1.b0), channel_id=1, source_target_pairs={{0,1},{1,2},{2,3},{3,0},{4,5},{5,6},{6,7},{7,4},{8,9},{9,10},{10,1... | collective-permute-start | bytes 884744 | tf_op jit(solution)/shard_map/image_y/ppermute | solution.py:37
  74.5 0.6 image_columns.2.p0
  75.2 4.7 %inverse.1 = f32[128,128]{1,0:T(8,128)S(1)} custom-call(f32[128,128]{1,0:T(8,128)S(1)} %get-tuple-element.78.source), custom_call_target="tpu_custom_call" | custom-call | flops 2000000000 | tf_op jit(solution)/shard_map/inverse/pallas_call | solution.py:390
  79.8 0.8 collective-permute-done.20.p1
  80.7 4.0 %collective-permute-start.22 = (f32[576,128]{1,0:T(8,128)S(1)}, f32[576,128]{1,0:T(8,128)S(1)}, u32[]{:S(2)}, u32[]{:S(2)}) collective-permute-start(f32[576,128]{1,0:T(8,128)S(1)} %collective-permute-done.19.b1), channel_id=1, source_target_pairs={{0,1},{1,2},{2,3},{3,0},{4,5},{5,6},{6,7},{7,4},{8,9},{9,10},{10,1... | collective-permute-start | bytes 884744 | tf_op jit(solution)/shard_map/image_far/ppermute | solution.py:37
  84.7 0.6 collective-permute-start.24
  85.3 3.0 %collective-permute-done.22.b2 = f32[576,128]{1,0:T(8,128)S(1)} collective-permute-done((f32[576,128]{1,0:T(8,128)S(1)}, f32[576,128]{1,0:T(8,128)S(1)}, u32[]{:S(2)}, u32[]{:S(2)}) %collective-permute-start.22) | collective-permute-done | bytes 294944 | tf_op jit(solution)/shard_map/image_far/ppermute | solution.py:37
  88.3 0.6 pick.1
  89.0 2.5 %collective-permute-start.23 = (f32[1152,128]{1,0:T(8,128)S(1)}, f32[1152,128]{1,0:T(8,128)S(1)}, u32[]{:S(2)}, u32[]{:S(2)}) collective-permute-start(f32[1152,128]{1,0:T(8,128)S(1)} %pick.1), channel_id=1, source_target_pairs={{0,16},{1,17},{2,18},{3,19},{4,20},{5,21},{6,22},{7,23},{8,24},{9,... | collective-permute-start | bytes 1769480 | tf_op jit(solution)/shard_map/image_swap/ppermute | solution.py:37
  91.5 1.2 %collective-permute-done.24.p3 = f32[288,128]{1,0:T(8,128)S(1)} collective-permute-done((f32[288,128]{1,0:T(8,128)S(1)}, f32[288,128]{1,0:T(8,128)S(1)}, u32[]{:S(2)}, u32[]{:S(2)}) %collective-permute-start.24) | collective-permute-done | bytes 147488 | tf_op jit(solution)/shard_map/image_columns/ppermute | solution.py:37
  92.6 0.6 image_columns.3.own
  93.6 1.5 %gather.1 = (f32[2304,128]{1,0:T(8,128)S(1)}, f32[2304,128]{1,0:T(8,128)S(1)}, f32[128,128]{1,0:T(8,128)S(1)}) custom-call(s32[4]{0:T(128)S(1)} %pad_add_fusion.place, f32[576,128]{1,0:T(8,128)S(1)} %panel_y.1.after.own.p0, f32[576,128]{1,0:T(8,128)S(1)} %collective-permute-done.3.front.p1, f32[576,128]{1,0:T(8,128)S(1)} %collective-permute-done.4.back.p3, ...), custom_call_target="tpu_custom_call" | custom-call | tf_op jit(solution)/shard_map/gather/pallas_call | solution.py:390
  95.4 1.0 collective-permute-done.27
  96.4 2.0 %collective-permute-start.30 = (f32[128,128]{1,0:T(8,128)S(1)}, f32[128,128]{1,0:T(8,128)S(1)}, u32[]{:S(2)}, u32[]{:S(2)}) collective-permute-start(f32[128,128]{1,0:T(8,128)S(1)} %add.14.k0), channel_id=1, source_target_pairs={{0,64},{1,65},{2,66},{3,67},{4,68},{5,69},{6,70},{7,71},{8,72},{9,... | collective-permute-start | bytes 196616 | tf_op jit(solution)/shard_map/inner/ppermute | solution.py:37
  98.3 1.5 %collective-permute-start.29 = (f32[128,128]{1,0:T(8,128)S(1)}, f32[128,128]{1,0:T(8,128)S(1)}, u32[]{:S(2)}, u32[]{:S(2)}) collective-permute-start(f32[128,128]{1,0:T(8,128)S(1)} %add.14.k0), channel_id=1, source_target_pairs={{0,96},{1,97},{2,98},{3,99},{4,100},{5,101},{6,102},{7,103},{8,104... | collective-permute-start | bytes 196616 | tf_op jit(solution)/shard_map/inner/ppermute | solution.py:37
  99.9 6.4 %first_update.1 = (f32[2304,1152]{1,0:T(8,128)S(1)}, f32[128,1152]{1,0:T(8,128)S(1)}) custom-call(s32[4]{0:T(128)S(1)} %pad_add_fusion.place, f32[2304,1152]{1,0:T(8,128)S(1)} %get-tuple-element.47.whole, f32[2304,128]{1,0:T(8,128)S(1)} %get-tuple-element.80.shifted_rows, f32[2304,128]{1,0:T(8,128)S(1)} %get-tuple-element.81.image_rows, ...), custom_call_target="tpu_custom_call" | custom-call | flops 4076863488 | tf_op jit(solution)/shard_map/first_update/pallas_call | solution.py:390
  106.3 5.2 %last_update.1 = f32[2304,1152]{1,0:T(8,128)} custom-call(f32[2304,1152]{1,0:T(8,128)S(1)} %get-tuple-element.87.base, f32[2304,128]{1,0:T(8,128)S(1)} %get-tuple-element.80.shifted_rows, f32[128,1152]{1,0:T(8,128)S(1)} %get-tuple-element.88.turned, f32[128,128]{1,0:T(8,128)S(1)} %inverse.1, f32[128,128]{1,0:T(8,128)S(1)} %add.14.k0, ...), custom_call_target="tpu_custom_call" | custom-call | flops 2717908992 | bytes 10616832 | tf_op jit(solution)/shard_map/last_update/pallas_call | solution.py:510
  (34 shorter events, 2.5 us)
Async XLA Ops:
  0.6 5.4 %collective-permute-start.1 = (f32[144,128]{1,0:T(8,128)}, f32[144,128]{1,0:T(8,128)S(1)}, u32[]{:S(2)}, u32[]{:S(2)}) collective-permute-start(f32[144,128]{1,0:T(8,128)} %p0.1), channel_id=1, source_target_pairs={{0,3},{1,0},{2,1},{3,2},{4,7},{5,4},{6,5},{7,6},{8,11},{9,8},{10,9... | collective-permute-start | bytes 221192 | tf_op jit(solution)/shard_map/panel_y/ppermute | solution.py:37
  4.3 5.2 %collective-permute-start = (f32[144,128]{1,0:T(8,128)}, f32[144,128]{1,0:T(8,128)S(1)}, u32[]{:S(2)}, u32[]{:S(2)}) collective-permute-start(f32[144,128]{1,0:T(8,128)} %p0.1), channel_id=1, source_target_pairs={{0,1},{1,2},{2,3},{3,0},{4,5},{5,6},{6,7},{7,4},{8,9},{9,10},{10,1... | collective-permute-start | bytes 221192 | tf_op jit(solution)/shard_map/panel_y/ppermute | solution.py:37
  4.3 5.6 %collective-permute-start.2 = (f32[144,128]{1,0:T(8,128)}, f32[144,128]{1,0:T(8,128)S(1)}, u32[]{:S(2)}, u32[]{:S(2)}) collective-permute-start(f32[144,128]{1,0:T(8,128)} %p0.1), channel_id=1, source_target_pairs={{0,2},{1,3},{2,0},{3,1},{4,6},{5,7},{6,4},{7,5},{8,10},{9,11},{10,... | collective-permute-start | bytes 221192 | tf_op jit(solution)/shard_map/panel_y/ppermute | solution.py:37
  9.9 0.9 copy-start
  11.3 8.2 %collective-permute-start.4 = (f32[576,128]{1,0:T(8,128)S(1)}, f32[576,128]{1,0:T(8,128)S(1)}, u32[]{:S(2)}, u32[]{:S(2)}) collective-permute-start(f32[576,128]{1,0:T(8,128)S(1)} %panel_y.1.after.own.p0), channel_id=1, source_target_pairs={{0,12},{1,13},{2,14},{3,15},{4,0},{5,1},{6,2},{7,3},{8,4},{9,5},{1... | collective-permute-start | bytes 884744 | tf_op jit(solution)/shard_map/panel_z/ppermute | solution.py:37
  13.1 8.5 %collective-permute-start.3 = (f32[576,128]{1,0:T(8,128)S(1)}, f32[576,128]{1,0:T(8,128)S(1)}, u32[]{:S(2)}, u32[]{:S(2)}) collective-permute-start(f32[576,128]{1,0:T(8,128)S(1)} %panel_y.1.after.own.p0), channel_id=1, source_target_pairs={{0,4},{1,5},{2,6},{3,7},{4,8},{5,9},{6,10},{7,11},{8,12},{9,13},{1... | collective-permute-start | bytes 884744 | tf_op jit(solution)/shard_map/panel_z/ppermute | solution.py:37
  21.6 5.6 %collective-permute-start.5 = (f32[576,128]{1,0:T(8,128)S(1)}, f32[576,128]{1,0:T(8,128)S(1)}, u32[]{:S(2)}, u32[]{:S(2)}) collective-permute-start(f32[576,128]{1,0:T(8,128)S(1)} %collective-permute-done.3.front.p1), channel_id=1, source_target_pairs={{0,4},{1,5},{2,6},{3,7},{4,8},{5,9},{6,10},{7,11},{8,12},{9,13},{1... | collective-permute-start | bytes 884744 | tf_op jit(solution)/shard_map/panel_far/ppermute | solution.py:37
  29.6 8.2 %collective-permute-start.6 = (f32[1408,128]{1,0:T(8,128)S(1)}, f32[1408,128]{1,0:T(8,128)S(1)}, u32[]{:S(2)}, u32[]{:S(2)}) collective-permute-start(f32[1408,128]{1,0:T(8,128)S(1)} %get-tuple-element.57), channel_id=1, source_target_pairs={{0,16},{1,17},{2,18},{3,19},{4,20},{5,21},{6,22},{7,23},{8,24},{9,... | collective-permute-start | bytes 2162696 | tf_op jit(solution)/shard_map/image_core/ppermute | solution.py:37
  38.4 7.0 %collective-permute-start.9 = (f32[128,128]{1,0:T(8,128)S(1)}, f32[128,128]{1,0:T(8,128)S(1)}, u32[]{:S(2)}, u32[]{:S(2)}) collective-permute-start(f32[128,128]{1,0:T(8,128)S(1)} %get-tuple-element.58.own), channel_id=1, source_target_pairs={{0,64},{1,65},{2,66},{3,67},{4,68},{5,69},{6,70},{7,71},{8,72},{9,... | collective-permute-start | bytes 196616 | tf_op jit(solution)/shard_map/gram_x/ppermute | solution.py:37
  41.2 4.7 %collective-permute-start.8 = (f32[128,128]{1,0:T(8,128)S(1)}, f32[128,128]{1,0:T(8,128)S(1)}, u32[]{:S(2)}, u32[]{:S(2)}) collective-permute-start(f32[128,128]{1,0:T(8,128)S(1)} %get-tuple-element.58.own), channel_id=1, source_target_pairs={{0,96},{1,97},{2,98},{3,99},{4,100},{5,101},{6,102},{7,103},{8,104... | collective-permute-start | bytes 196616 | tf_op jit(solution)/shard_map/gram_x/ppermute | solution.py:37
  42.1 4.3 %collective-permute-start.7 = (f32[128,128]{1,0:T(8,128)S(1)}, f32[128,128]{1,0:T(8,128)S(1)}, u32[]{:S(2)}, u32[]{:S(2)}) collective-permute-start(f32[128,128]{1,0:T(8,128)S(1)} %get-tuple-element.58.own), channel_id=1, source_target_pairs={{0,32},{1,33},{2,34},{3,35},{4,36},{5,37},{6,38},{7,39},{8,40},{9,... | collective-permute-start | bytes 196616 | tf_op jit(solution)/shard_map/gram_x/ppermute | solution.py:37
  42.7 9.7 %collective-permute-start.10 = (f32[416,128]{1,0:T(8,128)S(1)}, f32[416,128]{1,0:T(8,128)S(1)}, u32[]{:S(2)}, u32[]{:S(2)}) collective-permute-start(f32[416,128]{1,0:T(8,128)S(1)} %get-tuple-element.62), channel_id=1, source_target_pairs={{0,32},{1,33},{2,34},{3,35},{4,36},{5,37},{6,38},{7,39},{8,40},{9,... | collective-permute-start | bytes 638984 | tf_op jit(solution)/shard_map/image_x/ppermute | solution.py:37
  43.0 9.4 %collective-permute-start.11 = (f32[416,128]{1,0:T(8,128)S(1)}, f32[416,128]{1,0:T(8,128)S(1)}, u32[]{:S(2)}, u32[]{:S(2)}) collective-permute-start(f32[416,128]{1,0:T(8,128)S(1)} %get-tuple-element.63), channel_id=1, source_target_pairs={{0,96},{1,97},{2,98},{3,99},{4,100},{5,101},{6,102},{7,103},{8,104... | collective-permute-start | bytes 638984 | tf_op jit(solution)/shard_map/image_x/ppermute | solution.py:37
  45.4 9.2 %collective-permute-start.12 = (f32[416,128]{1,0:T(8,128)S(1)}, f32[416,128]{1,0:T(8,128)S(1)}, u32[]{:S(2)}, u32[]{:S(2)}) collective-permute-start(f32[416,128]{1,0:T(8,128)S(1)} %get-tuple-element.64), channel_id=1, source_target_pairs={{0,64},{1,65},{2,66},{3,67},{4,68},{5,69},{6,70},{7,71},{8,72},{9,... | collective-permute-start | bytes 638984 | tf_op jit(solution)/shard_map/image_x/ppermute | solution.py:37
  46.4 10.1 %collective-permute-start.17 = (f32[288,128]{1,0:T(8,128)S(1)}, f32[288,128]{1,0:T(8,128)S(1)}, u32[]{:S(2)}, u32[]{:S(2)}) collective-permute-start(f32[288,128]{1,0:T(8,128)S(1)} %get-tuple-element.71), channel_id=1, source_target_pairs={{0,0},{1,1},{4,32},{5,33},{8,64},{9,65},{12,96},{13,97},{18,18},{1... | collective-permute-start | bytes 442376 | tf_op jit(solution)/shard_map/panel_across/ppermute | solution.py:37
  54.9 4.9 %collective-permute-start.16 = (f32[144,128]{1,0:T(8,128)S(1)}, f32[144,128]{1,0:T(8,128)S(1)}, u32[]{:S(2)}, u32[]{:S(2)}) collective-permute-start(f32[144,128]{1,0:T(8,128)S(1)} %get-tuple-element.69.image), channel_id=1, source_target_pairs={{0,8},{1,9},{2,10},{3,11},{4,40},{5,41},{6,42},{7,43},{8,72},{9,73... | collective-permute-start | bytes 221192 | tf_op jit(solution)/shard_map/image_planes/ppermute | solution.py:37
  55.0 10.5 %collective-permute-start.15 = (f32[144,128]{1,0:T(8,128)S(1)}, f32[144,128]{1,0:T(8,128)S(1)}, u32[]{:S(2)}, u32[]{:S(2)}) collective-permute-start(f32[144,128]{1,0:T(8,128)S(1)} %get-tuple-element.69.image), channel_id=1, source_target_pairs={{0,12},{1,13},{2,14},{3,15},{4,44},{5,45},{6,46},{7,47},{8,76},{9,... | collective-permute-start | bytes 221192 | tf_op jit(solution)/shard_map/image_planes/ppermute | solution.py:37
  55.3 12.7 %collective-permute-start.14 = (f32[144,128]{1,0:T(8,128)S(1)}, f32[144,128]{1,0:T(8,128)S(1)}, u32[]{:S(2)}, u32[]{:S(2)}) collective-permute-start(f32[144,128]{1,0:T(8,128)S(1)} %get-tuple-element.69.image), channel_id=1, source_target_pairs={{0,4},{1,5},{2,6},{3,7},{4,36},{5,37},{6,38},{7,39},{8,68},{9,69},... | collective-permute-start | bytes 221192 | tf_op jit(solution)/shard_map/image_planes/ppermute | solution.py:37
  55.8 12.2 %collective-permute-start.13 = (f32[144,128]{1,0:T(8,128)S(1)}, f32[144,128]{1,0:T(8,128)S(1)}, u32[]{:S(2)}, u32[]{:S(2)}) collective-permute-start(f32[144,128]{1,0:T(8,128)S(1)} %get-tuple-element.69.image), channel_id=1, source_target_pairs={{0,0},{1,1},{2,2},{3,3},{4,32},{5,33},{6,34},{7,35},{8,64},{9,65},... | collective-permute-start | bytes 221192 | tf_op jit(solution)/shard_map/image_planes/ppermute | solution.py:37
  60.4 7.7 %collective-permute-start.18 = (f32[144,128]{1,0:T(8,128)S(1)}, f32[144,128]{1,0:T(8,128)S(1)}, u32[]{:S(2)}, u32[]{:S(2)}) collective-permute-start(f32[144,128]{1,0:T(8,128)S(1)} %panel_across.1), channel_id=1, source_target_pairs={{0,16},{1,17},{2,18},{3,19},{4,20},{5,21},{6,22},{7,23},{8,24},{9,... | collective-permute-start | bytes 221192 | tf_op jit(solution)/shard_map/panel_across/ppermute | solution.py:37
  68.6 12.0 %collective-permute-start.19 = (f32[576,128]{1,0:T(8,128)S(1)}, f32[576,128]{1,0:T(8,128)S(1)}, u32[]{:S(2)}, u32[]{:S(2)}) collective-permute-start(f32[576,128]{1,0:T(8,128)S(1)} %image_planes.1.b0), channel_id=1, source_target_pairs={{0,1},{1,2},{2,3},{3,0},{4,5},{5,6},{6,7},{7,4},{8,9},{9,10},{10,1... | collective-permute-start | bytes 884744 | tf_op jit(solution)/shard_map/image_y/ppermute | solution.py:37
  74.5 10.8 %collective-permute-start.21 = (f32[576,128]{1,0:T(8,128)S(1)}, f32[576,128]{1,0:T(8,128)S(1)}, u32[]{:S(2)}, u32[]{:S(2)}) collective-permute-start(f32[576,128]{1,0:T(8,128)S(1)} %image_planes.1.b0), channel_id=1, source_target_pairs={{0,3},{1,0},{2,1},{3,2},{4,7},{5,4},{6,5},{7,6},{8,11},{9,8},{10,9... | collective-permute-start | bytes 884744 | tf_op jit(solution)/shard_map/image_y/ppermute | solution.py:37
  75.1 5.6 %collective-permute-start.20 = (f32[288,128]{1,0:T(8,128)S(1)}, f32[288,128]{1,0:T(8,128)S(1)}, u32[]{:S(2)}, u32[]{:S(2)}) collective-permute-start(f32[288,128]{1,0:T(8,128)S(1)} %image_columns.2.p0), channel_id=1, source_target_pairs={{0,32},{1,33},{2,34},{3,35},{4,36},{5,37},{6,38},{7,39},{8,40},{9,... | collective-permute-start | bytes 442376 | tf_op jit(solution)/shard_map/image_columns/ppermute | solution.py:37
  80.7 7.7 %collective-permute-start.22 = (f32[576,128]{1,0:T(8,128)S(1)}, f32[576,128]{1,0:T(8,128)S(1)}, u32[]{:S(2)}, u32[]{:S(2)}) collective-permute-start(f32[576,128]{1,0:T(8,128)S(1)} %collective-permute-done.19.b1), channel_id=1, source_target_pairs={{0,1},{1,2},{2,3},{3,0},{4,5},{5,6},{6,7},{7,4},{8,9},{9,10},{10,1... | collective-permute-start | bytes 884744 | tf_op jit(solution)/shard_map/image_far/ppermute | solution.py:37
  84.7 6.8 %collective-permute-start.25 = (f32[288,128]{1,0:T(8,128)S(1)}, f32[288,128]{1,0:T(8,128)S(1)}, u32[]{:S(2)}, u32[]{:S(2)}) collective-permute-start(f32[288,128]{1,0:T(8,128)S(1)} %image_columns.2.p0), channel_id=1, source_target_pairs={{0,64},{1,65},{2,66},{3,67},{4,68},{5,69},{6,70},{7,71},{8,72},{9,... | collective-permute-start | bytes 442376 | tf_op jit(solution)/shard_map/image_columns/ppermute | solution.py:37
  84.7 8.0 %collective-permute-start.24 = (f32[288,128]{1,0:T(8,128)S(1)}, f32[288,128]{1,0:T(8,128)S(1)}, u32[]{:S(2)}, u32[]{:S(2)}) collective-permute-start(f32[288,128]{1,0:T(8,128)S(1)} %image_columns.2.p0), channel_id=1, source_target_pairs={{0,96},{1,97},{2,98},{3,99},{4,100},{5,101},{6,102},{7,103},{8,104... | collective-permute-start | bytes 442376 | tf_op jit(solution)/shard_map/image_columns/ppermute | solution.py:37
  89.0 4.6 %collective-permute-start.23 = (f32[1152,128]{1,0:T(8,128)S(1)}, f32[1152,128]{1,0:T(8,128)S(1)}, u32[]{:S(2)}, u32[]{:S(2)}) collective-permute-start(f32[1152,128]{1,0:T(8,128)S(1)} %pick.1), channel_id=1, source_target_pairs={{0,16},{1,17},{2,18},{3,19},{4,20},{5,21},{6,22},{7,23},{8,24},{9,... | collective-permute-start | bytes 1769480 | tf_op jit(solution)/shard_map/image_swap/ppermute | solution.py:37
  93.2 6.6 %collective-permute-start.26 = (f32[1152,128]{1,0:T(8,128)S(1)}, f32[1152,128]{1,0:T(8,128)S(1)}, u32[]{:S(2)}, u32[]{:S(2)}) collective-permute-start(f32[1152,128]{1,0:T(8,128)S(1)} %image_columns.3.own), channel_id=1, source_target_pairs={{0,16},{1,17},{2,18},{3,19},{4,20},{5,21},{6,22},{7,23},{8,24},{9,... | collective-permute-start | bytes 1769480 | tf_op jit(solution)/shard_map/image_columns/ppermute | solution.py:37
  95.0 1.3 %collective-permute-start.27 = (f32[128,128]{1,0:T(8,128)S(1)}, f32[128,128]{1,0:T(8,128)S(1)}, u32[]{:S(2)}, u32[]{:S(2)}) collective-permute-start(f32[128,128]{1,0:T(8,128)S(1)} %get-tuple-element.85), channel_id=1, source_target_pairs={{0,16},{1,17},{2,18},{3,19},{4,20},{5,21},{6,22},{7,23},{8,24},{9,... | collective-permute-start | bytes 196616 | tf_op jit(solution)/shard_map/inner/ppermute | solution.py:37
  96.4 9.9 %collective-permute-start.30 = (f32[128,128]{1,0:T(8,128)S(1)}, f32[128,128]{1,0:T(8,128)S(1)}, u32[]{:S(2)}, u32[]{:S(2)}) collective-permute-start(f32[128,128]{1,0:T(8,128)S(1)} %add.14.k0), channel_id=1, source_target_pairs={{0,64},{1,65},{2,66},{3,67},{4,68},{5,69},{6,70},{7,71},{8,72},{9,... | collective-permute-start | bytes 196616 | tf_op jit(solution)/shard_map/inner/ppermute | solution.py:37
  98.3 7.9 %collective-permute-start.29 = (f32[128,128]{1,0:T(8,128)S(1)}, f32[128,128]{1,0:T(8,128)S(1)}, u32[]{:S(2)}, u32[]{:S(2)}) collective-permute-start(f32[128,128]{1,0:T(8,128)S(1)} %add.14.k0), channel_id=1, source_target_pairs={{0,96},{1,97},{2,98},{3,99},{4,100},{5,101},{6,102},{7,103},{8,104... | collective-permute-start | bytes 196616 | tf_op jit(solution)/shard_map/inner/ppermute | solution.py:37
  99.8 6.5 %collective-permute-start.28 = (f32[128,128]{1,0:T(8,128)S(1)}, f32[128,128]{1,0:T(8,128)S(1)}, u32[]{:S(2)}, u32[]{:S(2)}) collective-permute-start(f32[128,128]{1,0:T(8,128)S(1)} %add.14.k0), channel_id=1, source_target_pairs={{0,32},{1,33},{2,34},{3,35},{4,36},{5,37},{6,38},{7,39},{8,40},{9,... | collective-permute-start | bytes 196616 | tf_op jit(solution)/shard_map/inner/ppermute | solution.py:37

commit v6 on v5

--- a/solution.py
+++ b/solution.py
@@ -55,6 +55,10 @@
 
 def planes(k):
     return lambda x, core, z, y: (z, core, (x + k) % 4, y)
+
+
+def read_across(x, core, z, y):
+    return core == y // 2
 
 
 def ring(value, direction):
@@ -450,7 +454,7 @@
     with jax.named_scope("image_x"):
         r1, r3, r2 = (send(m, along_x(k)) for m, k in ((m1, 1), (m3, 3), (m2, 2)))
     with jax.named_scope("panel_across"):
-        across = send(after(across, grams), planes(0), lambda x, core, z, y: core == y // 2)
+        across = send(after(across, grams), planes(0), read_across)
     with jax.named_scope("factor"):
         gram, upper, upper_here = local(factor_kernel, [tile] * 3, 4, [pltpu.VMEM((WIDTH, WIDTH), F32)], 2000000000)(
             *grams
@@ -462,7 +466,7 @@
     with jax.named_scope("image_planes"):
         planes_in = [send(image, planes(k)) for k in (0, 1, 3, 2)]
     with jax.named_scope("panel_across"):
-        handed = send(local(hand_kernel, shape(PIECE), 4)(place, after(across, planes_in[3])), other_core)
+        handed = send(local(hand_kernel, shape(PIECE), 4)(place, after(across, planes_in[3])), other_core, read_across)
     with jax.named_scope("image_planes"):
         in_plane = local(join_z_kernel, shape(4 * PIECE), 4)(place, *after(planes_in, handed))
     with jax.named_scope("image_y"):

time: 113 us -> 114 us (level)
  waiting for transfers between devices: 22.5 us -> 25.9 us
  starting transfers between devices: 49.1 us -> 47.3 us
    ppermute x31, waiting for transfers between devices: 22.5 us -> 25.9 us  [send(): return lax.ppermute(value, AXES, pairs(where, only))]
    ppermute x31, starting transfers between devices: 49.1 us -> 47.3 us  [send(): return lax.ppermute(value, AXES, pairs(where, only))]
  transfers between devices with their start and end apart: 31 -> 31, of which waited for: 13 -> 14; matrix products, arithmetic and copies ran while one was open for 0% -> 0% of each run, Pallas kernels for 26% -> 25%
where the time goes in v6:
time: 114 us; the launch traced here: 113 us
  starting transfers between devices  47.3 us (41%)
  Pallas kernels  38.1 us (33%)
  waiting for transfers between devices  25.9 us (23%)
    ppermute x31, starting transfers between devices, send(): return lax.ppermute(value, AXES, pairs(where, only))  47.3 us
    pallas_call x14, Pallas kernels, run(): pl.pallas_call(kernel, in_specs=specs, out_specs=outs, out_shape=out_shap...  28.6 us
    ppermute x31, waiting for transfers between devices, send(): return lax.ppermute(value, AXES, pairs(where, only))  25.9 us
    pallas_call x1, Pallas kernels, shards(): pl.pallas_call(last_update_kernel, in_specs=[VMEM] * 8, out_specs=anywher...  5.21 us
    pallas_call x1, Pallas kernels, shards(): pl.pallas_call(split_kernel, in_specs=[anywhere, VMEM], out_specs=[VMEM]...  4.3 us
  transfers between devices with their start and end apart: 31, of which 14 were waited for; matrix products, arithmetic and copies ran while one was open for 0% of the time, Pallas kernels for 25%

profile of v6, /device:TPU:1, one launch (start us, length us, event | category | flops | bytes accessed | tf_op | source)
XLA Modules:
  0.0 113.5 jit_solution(6769025259019058550)
XLA Ops:
  0.6 3.6 %collective-permute-start.1 = (f32[144,128]{1,0:T(8,128)}, f32[144,128]{1,0:T(8,128)S(1)}, u32[]{:S(2)}, u32[]{:S(2)}) collective-permute-start(f32[144,128]{1,0:T(8,128)} %p0.1), channel_id=1, source_target_pairs={{0,3},{1,0},{2,1},{3,2},{4,7},{5,4},{6,5},{7,6},{8,11},{9,8},{10,9... | collective-permute-start | bytes 221192 | tf_op jit(solution)/shard_map/panel_y/ppermute | solution.py:37
  4.3 1.6 %collective-permute-start.2 = (f32[144,128]{1,0:T(8,128)}, f32[144,128]{1,0:T(8,128)S(1)}, u32[]{:S(2)}, u32[]{:S(2)}) collective-permute-start(f32[144,128]{1,0:T(8,128)} %p0.1), channel_id=1, source_target_pairs={{0,2},{1,3},{2,0},{3,1},{4,6},{5,7},{6,4},{7,5},{8,10},{9,11},{10,... | collective-permute-start | bytes 221192 | tf_op jit(solution)/shard_map/panel_y/ppermute | solution.py:37
  6.0 3.5 %collective-permute-done.p1 = f32[144,128]{1,0:T(8,128)S(1)} collective-permute-done((f32[144,128]{1,0:T(8,128)}, f32[144,128]{1,0:T(8,128)S(1)}, u32[]{:S(2)}, u32[]{:S(2)}) %collective-permute-start) | collective-permute-done | bytes 73760 | tf_op jit(solution)/shard_map/panel_y/ppermute | solution.py:37
  9.9 0.9 copy-done
  10.8 0.6 panel_y.1.after.own.p0
  11.3 1.7 %collective-permute-start.4 = (f32[576,128]{1,0:T(8,128)S(1)}, f32[576,128]{1,0:T(8,128)S(1)}, u32[]{:S(2)}, u32[]{:S(2)}) collective-permute-start(f32[576,128]{1,0:T(8,128)S(1)} %panel_y.1.after.own.p0), channel_id=1, source_target_pairs={{0,12},{1,13},{2,14},{3,15},{4,0},{5,1},{6,2},{7,3},{8,4},{9,5},{1... | collective-permute-start | bytes 884744 | tf_op jit(solution)/shard_map/panel_z/ppermute | solution.py:37
  13.1 2.2 %collective-permute-start.3 = (f32[576,128]{1,0:T(8,128)S(1)}, f32[576,128]{1,0:T(8,128)S(1)}, u32[]{:S(2)}, u32[]{:S(2)}) collective-permute-start(f32[576,128]{1,0:T(8,128)S(1)} %panel_y.1.after.own.p0), channel_id=1, source_target_pairs={{0,4},{1,5},{2,6},{3,7},{4,8},{5,9},{6,10},{7,11},{8,12},{9,13},{1... | collective-permute-start | bytes 884744 | tf_op jit(solution)/shard_map/panel_z/ppermute | solution.py:37
  15.3 4.3 %split.1 = (f32[2304,1152]{1,0:T(8,128)S(1)}, bf16[2304,1152]{1,0:T(8,128)(2,1)S(1)}, bf16[2304,1152]{1,0:T(8,128)(2,1)S(1)}) custom-call(f32[2304,1152]{1,0:T(8,128)} %trailing.1, f32[576,128]{1,0:T(8,128)S(1)} %panel_y.1.after.own.p0), custom_call_target="tpu_custom_call" | custom-call | bytes 10616832 | tf_op jit(solution)/shard_map/split/pallas_call | solution.py:425
  19.6 2.0 %collective-permute-done.3.front.p1 = f32[576,128]{1,0:T(8,128)S(1)} collective-permute-done((f32[576,128]{1,0:T(8,128)S(1)}, f32[576,128]{1,0:T(8,128)S(1)}, u32[]{:S(2)}, u32[]{:S(2)}) %collective-permute-start.3) | collective-permute-done | bytes 294944 | tf_op jit(solution)/shard_map/panel_z/ppermute | solution.py:37
  21.6 1.4 %collective-permute-start.5 = (f32[576,128]{1,0:T(8,128)S(1)}, f32[576,128]{1,0:T(8,128)S(1)}, u32[]{:S(2)}, u32[]{:S(2)}) collective-permute-start(f32[576,128]{1,0:T(8,128)S(1)} %collective-permute-done.3.front.p1), channel_id=1, source_target_pairs={{0,4},{1,5},{2,6},{3,7},{4,8},{5,9},{6,10},{7,11},{8,12},{9,13},{1... | collective-permute-start | bytes 884744 | tf_op jit(solution)/shard_map/panel_far/ppermute | solution.py:37
  23.0 3.9 %near.1 = (f32[128,1152]{1,0:T(8,128)S(1)}, f32[128,128]{1,0:T(8,128)S(1)}, f32[128,128]{1,0:T(8,128)S(1)}) custom-call(s32[4]{0:T(128)S(1)} %pad_add_fusion.place, bf16[2304,1152]{1,0:T(8,128)(2,1)S(1)} %get-tuple-element.48.high, bf16[2304,1152]{1,0:T(8,128)(2,1)S(1)} %get-tuple-element.49.low, f32[576,128]{1,0:T(8,128)S(1)} %panel_y.1.after.own.p0, ...), custom_call_target="tpu_custom_call" | custom-call | flops 1698693120 | tf_op jit(solution)/shard_map/near/pallas_call | solution.py:394
  27.1 2.5 %image.1 = (f32[1408,128]{1,0:T(8,128)S(1)}, f32[1408,128]{1,0:T(8,128)S(1)}, f32[288,128]{1,0:T(8,128)S(1)}) custom-call(s32[4]{0:T(128)S(1)} %pad_add_fusion.place, f32[2304,1152]{1,0:T(8,128)S(1)} %get-tuple-element.47.whole, bf16[2304,1152]{1,0:T(8,128)(2,1)S(1)} %get-tuple-element.48.high, bf16[2304,1152]{1,0:T(8,128)(2,1)S(1)} %get-tuple-element.49.low, ...), custom_call_target="tpu_custom_call" | custom-call | flops 679477248 | tf_op jit(solution)/shard_map/image/pallas_call | solution.py:394
  29.6 6.3 %collective-permute-start.6 = (f32[1408,128]{1,0:T(8,128)S(1)}, f32[1408,128]{1,0:T(8,128)S(1)}, u32[]{:S(2)}, u32[]{:S(2)}) collective-permute-start(f32[1408,128]{1,0:T(8,128)S(1)} %get-tuple-element.57), channel_id=1, source_target_pairs={{0,16},{1,17},{2,18},{3,19},{4,20},{5,21},{6,22},{7,23},{8,24},{9,... | collective-permute-start | bytes 2162696 | tf_op jit(solution)/shard_map/image_core/ppermute | solution.py:37
  36.0 1.8 %collective-permute-done.6.received = f32[1408,128]{1,0:T(8,128)S(1)} collective-permute-done((f32[1408,128]{1,0:T(8,128)S(1)}, f32[1408,128]{1,0:T(8,128)S(1)}, u32[]{:S(2)}, u32[]{:S(2)}) %collective-permute-start.6) | collective-permute-done | bytes 720928 | tf_op jit(solution)/shard_map/image_core/ppermute | solution.py:37
  37.8 0.6 deal.1
  38.4 2.8 %collective-permute-start.9 = (f32[128,128]{1,0:T(8,128)S(1)}, f32[128,128]{1,0:T(8,128)S(1)}, u32[]{:S(2)}, u32[]{:S(2)}) collective-permute-start(f32[128,128]{1,0:T(8,128)S(1)} %get-tuple-element.58.own), channel_id=1, source_target_pairs={{0,64},{1,65},{2,66},{3,67},{4,68},{5,69},{6,70},{7,71},{8,72},{9,... | collective-permute-start | bytes 196616 | tf_op jit(solution)/shard_map/gram_x/ppermute | solution.py:37
  41.2 0.9 collective-permute-start.8
  42.1 0.6 collective-permute-start.7
  43.0 2.4 %collective-permute-start.11 = (f32[416,128]{1,0:T(8,128)S(1)}, f32[416,128]{1,0:T(8,128)S(1)}, u32[]{:S(2)}, u32[]{:S(2)}) collective-permute-start(f32[416,128]{1,0:T(8,128)S(1)} %get-tuple-element.63), channel_id=1, source_target_pairs={{0,96},{1,97},{2,98},{3,99},{4,100},{5,101},{6,102},{7,103},{8,104... | collective-permute-start | bytes 638984 | tf_op jit(solution)/shard_map/image_x/ppermute | solution.py:37
  45.4 0.6 collective-permute-start.12
  45.9 0.5 collective-permute-done.7.r1
  46.4 0.7 collective-permute-start.17
  47.1 5.3 %factor.1 = (f32[128,128]{1,0:T(8,128)S(1)}, f32[128,128]{1,0:T(8,128)}, f32[128,128]{1,0:T(8,128)S(1)}) custom-call(f32[128,128]{1,0:T(8,128)S(1)} %get-tuple-element.58.own, f32[128,128]{1,0:T(8,128)S(1)} %collective-permute-done.7.r1, f32[128,128]{1,0:T(8,128)S(1)} %collective-permute-done.8.r3, f32[128,128]{1,0:T(8,128)S(1)} %collective-permute-done.9.r2), custom_call_target="tpu_custom_call" | custom-call | flops 2000000000 | tf_op jit(solution)/shard_map/factor/pallas_call | solution.py:394
  52.4 2.3 %collective-permute-done.12.r2 = f32[416,128]{1,0:T(8,128)S(1)} collective-permute-done((f32[416,128]{1,0:T(8,128)S(1)}, f32[416,128]{1,0:T(8,128)S(1)}, u32[]{:S(2)}, u32[]{:S(2)}) %collective-permute-start.12) | collective-permute-done | bytes 213024 | tf_op jit(solution)/shard_map/image_x/ppermute | solution.py:37
  55.3 0.5 collective-permute-start.14
  55.8 0.7 collective-permute-start.13
  56.5 3.3 %collective-permute-done.16.p2 = f32[144,128]{1,0:T(8,128)S(1)} collective-permute-done((f32[144,128]{1,0:T(8,128)S(1)}, f32[144,128]{1,0:T(8,128)S(1)}, u32[]{:S(2)}, u32[]{:S(2)}) %collective-permute-start.16) | collective-permute-done | bytes 73760 | tf_op jit(solution)/shard_map/image_planes/ppermute | solution.py:37
  59.8 0.6 panel_across.1
  60.4 1.3 %collective-permute-start.18 = (f32[144,128]{1,0:T(8,128)S(1)}, f32[144,128]{1,0:T(8,128)S(1)}, u32[]{:S(2)}, u32[]{:S(2)}) collective-permute-start(f32[144,128]{1,0:T(8,128)S(1)} %panel_across.1), channel_id=1, source_target_pairs={{0,16},{1,17},{4,20},{5,21},{8,24},{9,25},{12,28},{13,29},{18,2},{... | collective-permute-start | bytes 221192 | tf_op jit(solution)/shard_map/panel_across/ppermute | solution.py:37
  61.7 6.3 %collective-permute-done.14.p1 = f32[144,128]{1,0:T(8,128)S(1)} collective-permute-done((f32[144,128]{1,0:T(8,128)S(1)}, f32[144,128]{1,0:T(8,128)S(1)}, u32[]{:S(2)}, u32[]{:S(2)}) %collective-permute-start.14) | collective-permute-done | bytes 73760 | tf_op jit(solution)/shard_map/image_planes/ppermute | solution.py:37
  68.0 0.6 image_planes.1.b0
  68.6 7.7 %collective-permute-start.19 = (f32[576,128]{1,0:T(8,128)S(1)}, f32[576,128]{1,0:T(8,128)S(1)}, u32[]{:S(2)}, u32[]{:S(2)}) collective-permute-start(f32[576,128]{1,0:T(8,128)S(1)} %image_planes.1.b0), channel_id=1, source_target_pairs={{0,1},{1,2},{2,3},{3,0},{4,5},{5,6},{6,7},{7,4},{8,9},{9,10},{10,1... | collective-permute-start | bytes 884744 | tf_op jit(solution)/shard_map/image_y/ppermute | solution.py:37
  76.3 0.6 image_columns.2.p0
  77.0 4.7 %inverse.1 = f32[128,128]{1,0:T(8,128)S(1)} custom-call(f32[128,128]{1,0:T(8,128)S(1)} %get-tuple-element.78.source), custom_call_target="tpu_custom_call" | custom-call | flops 2000000000 | tf_op jit(solution)/shard_map/inverse/pallas_call | solution.py:394
  81.7 1.2 %collective-permute-done.20.p1 = f32[288,128]{1,0:T(8,128)S(1)} collective-permute-done((f32[288,128]{1,0:T(8,128)S(1)}, f32[288,128]{1,0:T(8,128)S(1)}, u32[]{:S(2)}, u32[]{:S(2)}) %collective-permute-start.20) | collective-permute-done | bytes 147488 | tf_op jit(solution)/shard_map/image_columns/ppermute | solution.py:37
  82.9 3.7 %collective-permute-start.22 = (f32[576,128]{1,0:T(8,128)S(1)}, f32[576,128]{1,0:T(8,128)S(1)}, u32[]{:S(2)}, u32[]{:S(2)}) collective-permute-start(f32[576,128]{1,0:T(8,128)S(1)} %collective-permute-done.19.b1), channel_id=1, source_target_pairs={{0,1},{1,2},{2,3},{3,0},{4,5},{5,6},{6,7},{7,4},{8,9},{9,10},{10,1... | collective-permute-start | bytes 884744 | tf_op jit(solution)/shard_map/image_far/ppermute | solution.py:37
  86.6 1.1 collective-permute-start.24
  87.7 2.6 %collective-permute-done.22.b2 = f32[576,128]{1,0:T(8,128)S(1)} collective-permute-done((f32[576,128]{1,0:T(8,128)S(1)}, f32[576,128]{1,0:T(8,128)S(1)}, u32[]{:S(2)}, u32[]{:S(2)}) %collective-permute-start.22) | collective-permute-done | bytes 294944 | tf_op jit(solution)/shard_map/image_far/ppermute | solution.py:37
  90.2 0.6 pick.1
  90.9 2.2 %collective-permute-start.23 = (f32[1152,128]{1,0:T(8,128)S(1)}, f32[1152,128]{1,0:T(8,128)S(1)}, u32[]{:S(2)}, u32[]{:S(2)}) collective-permute-start(f32[1152,128]{1,0:T(8,128)S(1)} %pick.1), channel_id=1, source_target_pairs={{0,16},{1,17},{2,18},{3,19},{4,20},{5,21},{6,22},{7,23},{8,24},{9,... | collective-permute-start | bytes 1769480 | tf_op jit(solution)/shard_map/image_swap/ppermute | solution.py:37
  93.1 0.7 collective-permute-done.24.p3
  93.8 0.6 image_columns.3.own
  94.7 1.5 %gather.1 = (f32[2304,128]{1,0:T(8,128)S(1)}, f32[2304,128]{1,0:T(8,128)S(1)}, f32[128,128]{1,0:T(8,128)S(1)}) custom-call(s32[4]{0:T(128)S(1)} %pad_add_fusion.place, f32[576,128]{1,0:T(8,128)S(1)} %panel_y.1.after.own.p0, f32[576,128]{1,0:T(8,128)S(1)} %collective-permute-done.3.front.p1, f32[576,128]{1,0:T(8,128)S(1)} %collective-permute-done.4.back.p3, ...), custom_call_target="tpu_custom_call" | custom-call | tf_op jit(solution)/shard_map/gather/pallas_call | solution.py:394
  96.6 0.9 collective-permute-done.27
  97.6 2.1 %collective-permute-start.30 = (f32[128,128]{1,0:T(8,128)S(1)}, f32[128,128]{1,0:T(8,128)S(1)}, u32[]{:S(2)}, u32[]{:S(2)}) collective-permute-start(f32[128,128]{1,0:T(8,128)S(1)} %add.14.k0), channel_id=1, source_target_pairs={{0,64},{1,65},{2,66},{3,67},{4,68},{5,69},{6,70},{7,71},{8,72},{9,... | collective-permute-start | bytes 196616 | tf_op jit(solution)/shard_map/inner/ppermute | solution.py:37
  99.7 1.9 %collective-permute-start.29 = (f32[128,128]{1,0:T(8,128)S(1)}, f32[128,128]{1,0:T(8,128)S(1)}, u32[]{:S(2)}, u32[]{:S(2)}) collective-permute-start(f32[128,128]{1,0:T(8,128)S(1)} %add.14.k0), channel_id=1, source_target_pairs={{0,96},{1,97},{2,98},{3,99},{4,100},{5,101},{6,102},{7,103},{8,104... | collective-permute-start | bytes 196616 | tf_op jit(solution)/shard_map/inner/ppermute | solution.py:37
  101.6 6.4 %first_update.1 = (f32[2304,1152]{1,0:T(8,128)S(1)}, f32[128,1152]{1,0:T(8,128)S(1)}) custom-call(s32[4]{0:T(128)S(1)} %pad_add_fusion.place, f32[2304,1152]{1,0:T(8,128)S(1)} %get-tuple-element.47.whole, f32[2304,128]{1,0:T(8,128)S(1)} %get-tuple-element.80.shifted_rows, f32[2304,128]{1,0:T(8,128)S(1)} %get-tuple-element.81.image_rows, ...), custom_call_target="tpu_custom_call" | custom-call | flops 4076863488 | tf_op jit(solution)/shard_map/first_update/pallas_call | solution.py:394
  108.1 5.2 %last_update.1 = f32[2304,1152]{1,0:T(8,128)} custom-call(f32[2304,1152]{1,0:T(8,128)S(1)} %get-tuple-element.87.base, f32[2304,128]{1,0:T(8,128)S(1)} %get-tuple-element.80.shifted_rows, f32[128,1152]{1,0:T(8,128)S(1)} %get-tuple-element.88.turned, f32[128,128]{1,0:T(8,128)S(1)} %inverse.1, f32[128,128]{1,0:T(8,128)S(1)} %add.14.k0, ...), custom_call_target="tpu_custom_call" | custom-call | flops 2717908992 | bytes 10616832 | tf_op jit(solution)/shard_map/last_update/pallas_call | solution.py:514
  (34 shorter events, 2.6 us)
Async XLA Ops:
  0.6 5.4 %collective-permute-start.1 = (f32[144,128]{1,0:T(8,128)}, f32[144,128]{1,0:T(8,128)S(1)}, u32[]{:S(2)}, u32[]{:S(2)}) collective-permute-start(f32[144,128]{1,0:T(8,128)} %p0.1), channel_id=1, source_target_pairs={{0,3},{1,0},{2,1},{3,2},{4,7},{5,4},{6,5},{7,6},{8,11},{9,8},{10,9... | collective-permute-start | bytes 221192 | tf_op jit(solution)/shard_map/panel_y/ppermute | solution.py:37
  4.3 5.2 %collective-permute-start = (f32[144,128]{1,0:T(8,128)}, f32[144,128]{1,0:T(8,128)S(1)}, u32[]{:S(2)}, u32[]{:S(2)}) collective-permute-start(f32[144,128]{1,0:T(8,128)} %p0.1), channel_id=1, source_target_pairs={{0,1},{1,2},{2,3},{3,0},{4,5},{5,6},{6,7},{7,4},{8,9},{9,10},{10,1... | collective-permute-start | bytes 221192 | tf_op jit(solution)/shard_map/panel_y/ppermute | solution.py:37
  4.3 5.6 %collective-permute-start.2 = (f32[144,128]{1,0:T(8,128)}, f32[144,128]{1,0:T(8,128)S(1)}, u32[]{:S(2)}, u32[]{:S(2)}) collective-permute-start(f32[144,128]{1,0:T(8,128)} %p0.1), channel_id=1, source_target_pairs={{0,2},{1,3},{2,0},{3,1},{4,6},{5,7},{6,4},{7,5},{8,10},{9,11},{10,... | collective-permute-start | bytes 221192 | tf_op jit(solution)/shard_map/panel_y/ppermute | solution.py:37
  9.9 0.9 copy-start
  11.3 8.2 %collective-permute-start.4 = (f32[576,128]{1,0:T(8,128)S(1)}, f32[576,128]{1,0:T(8,128)S(1)}, u32[]{:S(2)}, u32[]{:S(2)}) collective-permute-start(f32[576,128]{1,0:T(8,128)S(1)} %panel_y.1.after.own.p0), channel_id=1, source_target_pairs={{0,12},{1,13},{2,14},{3,15},{4,0},{5,1},{6,2},{7,3},{8,4},{9,5},{1... | collective-permute-start | bytes 884744 | tf_op jit(solution)/shard_map/panel_z/ppermute | solution.py:37
  13.1 8.5 %collective-permute-start.3 = (f32[576,128]{1,0:T(8,128)S(1)}, f32[576,128]{1,0:T(8,128)S(1)}, u32[]{:S(2)}, u32[]{:S(2)}) collective-permute-start(f32[576,128]{1,0:T(8,128)S(1)} %panel_y.1.after.own.p0), channel_id=1, source_target_pairs={{0,4},{1,5},{2,6},{3,7},{4,8},{5,9},{6,10},{7,11},{8,12},{9,13},{1... | collective-permute-start | bytes 884744 | tf_op jit(solution)/shard_map/panel_z/ppermute | solution.py:37
  21.6 5.6 %collective-permute-start.5 = (f32[576,128]{1,0:T(8,128)S(1)}, f32[576,128]{1,0:T(8,128)S(1)}, u32[]{:S(2)}, u32[]{:S(2)}) collective-permute-start(f32[576,128]{1,0:T(8,128)S(1)} %collective-permute-done.3.front.p1), channel_id=1, source_target_pairs={{0,4},{1,5},{2,6},{3,7},{4,8},{5,9},{6,10},{7,11},{8,12},{9,13},{1... | collective-permute-start | bytes 884744 | tf_op jit(solution)/shard_map/panel_far/ppermute | solution.py:37
  29.6 8.2 %collective-permute-start.6 = (f32[1408,128]{1,0:T(8,128)S(1)}, f32[1408,128]{1,0:T(8,128)S(1)}, u32[]{:S(2)}, u32[]{:S(2)}) collective-permute-start(f32[1408,128]{1,0:T(8,128)S(1)} %get-tuple-element.57), channel_id=1, source_target_pairs={{0,16},{1,17},{2,18},{3,19},{4,20},{5,21},{6,22},{7,23},{8,24},{9,... | collective-permute-start | bytes 2162696 | tf_op jit(solution)/shard_map/image_core/ppermute | solution.py:37
  38.4 7.0 %collective-permute-start.9 = (f32[128,128]{1,0:T(8,128)S(1)}, f32[128,128]{1,0:T(8,128)S(1)}, u32[]{:S(2)}, u32[]{:S(2)}) collective-permute-start(f32[128,128]{1,0:T(8,128)S(1)} %get-tuple-element.58.own), channel_id=1, source_target_pairs={{0,64},{1,65},{2,66},{3,67},{4,68},{5,69},{6,70},{7,71},{8,72},{9,... | collective-permute-start | bytes 196616 | tf_op jit(solution)/shard_map/gram_x/ppermute | solution.py:37
  41.2 4.7 %collective-permute-start.8 = (f32[128,128]{1,0:T(8,128)S(1)}, f32[128,128]{1,0:T(8,128)S(1)}, u32[]{:S(2)}, u32[]{:S(2)}) collective-permute-start(f32[128,128]{1,0:T(8,128)S(1)} %get-tuple-element.58.own), channel_id=1, source_target_pairs={{0,96},{1,97},{2,98},{3,99},{4,100},{5,101},{6,102},{7,103},{8,104... | collective-permute-start | bytes 196616 | tf_op jit(solution)/shard_map/gram_x/ppermute | solution.py:37
  42.1 4.3 %collective-permute-start.7 = (f32[128,128]{1,0:T(8,128)S(1)}, f32[128,128]{1,0:T(8,128)S(1)}, u32[]{:S(2)}, u32[]{:S(2)}) collective-permute-start(f32[128,128]{1,0:T(8,128)S(1)} %get-tuple-element.58.own), channel_id=1, source_target_pairs={{0,32},{1,33},{2,34},{3,35},{4,36},{5,37},{6,38},{7,39},{8,40},{9,... | collective-permute-start | bytes 196616 | tf_op jit(solution)/shard_map/gram_x/ppermute | solution.py:37
  42.7 9.7 %collective-permute-start.10 = (f32[416,128]{1,0:T(8,128)S(1)}, f32[416,128]{1,0:T(8,128)S(1)}, u32[]{:S(2)}, u32[]{:S(2)}) collective-permute-start(f32[416,128]{1,0:T(8,128)S(1)} %get-tuple-element.62), channel_id=1, source_target_pairs={{0,32},{1,33},{2,34},{3,35},{4,36},{5,37},{6,38},{7,39},{8,40},{9,... | collective-permute-start | bytes 638984 | tf_op jit(solution)/shard_map/image_x/ppermute | solution.py:37
  43.0 9.4 %collective-permute-start.11 = (f32[416,128]{1,0:T(8,128)S(1)}, f32[416,128]{1,0:T(8,128)S(1)}, u32[]{:S(2)}, u32[]{:S(2)}) collective-permute-start(f32[416,128]{1,0:T(8,128)S(1)} %get-tuple-element.63), channel_id=1, source_target_pairs={{0,96},{1,97},{2,98},{3,99},{4,100},{5,101},{6,102},{7,103},{8,104... | collective-permute-start | bytes 638984 | tf_op jit(solution)/shard_map/image_x/ppermute | solution.py:37
  45.4 9.2 %collective-permute-start.12 = (f32[416,128]{1,0:T(8,128)S(1)}, f32[416,128]{1,0:T(8,128)S(1)}, u32[]{:S(2)}, u32[]{:S(2)}) collective-permute-start(f32[416,128]{1,0:T(8,128)S(1)} %get-tuple-element.64), channel_id=1, source_target_pairs={{0,64},{1,65},{2,66},{3,67},{4,68},{5,69},{6,70},{7,71},{8,72},{9,... | collective-permute-start | bytes 638984 | tf_op jit(solution)/shard_map/image_x/ppermute | solution.py:37
  46.4 10.1 %collective-permute-start.17 = (f32[288,128]{1,0:T(8,128)S(1)}, f32[288,128]{1,0:T(8,128)S(1)}, u32[]{:S(2)}, u32[]{:S(2)}) collective-permute-start(f32[288,128]{1,0:T(8,128)S(1)} %get-tuple-element.71), channel_id=1, source_target_pairs={{0,0},{1,1},{4,32},{5,33},{8,64},{9,65},{12,96},{13,97},{18,18},{1... | collective-permute-start | bytes 442376 | tf_op jit(solution)/shard_map/panel_across/ppermute | solution.py:37
  54.9 4.9 %collective-permute-start.16 = (f32[144,128]{1,0:T(8,128)S(1)}, f32[144,128]{1,0:T(8,128)S(1)}, u32[]{:S(2)}, u32[]{:S(2)}) collective-permute-start(f32[144,128]{1,0:T(8,128)S(1)} %get-tuple-element.69.image), channel_id=1, source_target_pairs={{0,8},{1,9},{2,10},{3,11},{4,40},{5,41},{6,42},{7,43},{8,72},{9,73... | collective-permute-start | bytes 221192 | tf_op jit(solution)/shard_map/image_planes/ppermute | solution.py:37
  55.0 6.7 %collective-permute-start.15 = (f32[144,128]{1,0:T(8,128)S(1)}, f32[144,128]{1,0:T(8,128)S(1)}, u32[]{:S(2)}, u32[]{:S(2)}) collective-permute-start(f32[144,128]{1,0:T(8,128)S(1)} %get-tuple-element.69.image), channel_id=1, source_target_pairs={{0,12},{1,13},{2,14},{3,15},{4,44},{5,45},{6,46},{7,47},{8,76},{9,... | collective-permute-start | bytes 221192 | tf_op jit(solution)/shard_map/image_planes/ppermute | solution.py:37
  55.3 12.7 %collective-permute-start.14 = (f32[144,128]{1,0:T(8,128)S(1)}, f32[144,128]{1,0:T(8,128)S(1)}, u32[]{:S(2)}, u32[]{:S(2)}) collective-permute-start(f32[144,128]{1,0:T(8,128)S(1)} %get-tuple-element.69.image), channel_id=1, source_target_pairs={{0,4},{1,5},{2,6},{3,7},{4,36},{5,37},{6,38},{7,39},{8,68},{9,69},... | collective-permute-start | bytes 221192 | tf_op jit(solution)/shard_map/image_planes/ppermute | solution.py:37
  55.8 12.2 %collective-permute-start.13 = (f32[144,128]{1,0:T(8,128)S(1)}, f32[144,128]{1,0:T(8,128)S(1)}, u32[]{:S(2)}, u32[]{:S(2)}) collective-permute-start(f32[144,128]{1,0:T(8,128)S(1)} %get-tuple-element.69.image), channel_id=1, source_target_pairs={{0,0},{1,1},{2,2},{3,3},{4,32},{5,33},{6,34},{7,35},{8,64},{9,65},... | collective-permute-start | bytes 221192 | tf_op jit(solution)/shard_map/image_planes/ppermute | solution.py:37
  60.4 7.7 %collective-permute-start.18 = (f32[144,128]{1,0:T(8,128)S(1)}, f32[144,128]{1,0:T(8,128)S(1)}, u32[]{:S(2)}, u32[]{:S(2)}) collective-permute-start(f32[144,128]{1,0:T(8,128)S(1)} %panel_across.1), channel_id=1, source_target_pairs={{0,16},{1,17},{4,20},{5,21},{8,24},{9,25},{12,28},{13,29},{18,2},{... | collective-permute-start | bytes 221192 | tf_op jit(solution)/shard_map/panel_across/ppermute | solution.py:37
  68.6 14.2 %collective-permute-start.19 = (f32[576,128]{1,0:T(8,128)S(1)}, f32[576,128]{1,0:T(8,128)S(1)}, u32[]{:S(2)}, u32[]{:S(2)}) collective-permute-start(f32[576,128]{1,0:T(8,128)S(1)} %image_planes.1.b0), channel_id=1, source_target_pairs={{0,1},{1,2},{2,3},{3,0},{4,5},{5,6},{6,7},{7,4},{8,9},{9,10},{10,1... | collective-permute-start | bytes 884744 | tf_op jit(solution)/shard_map/image_y/ppermute | solution.py:37
  76.3 11.4 %collective-permute-start.21 = (f32[576,128]{1,0:T(8,128)S(1)}, f32[576,128]{1,0:T(8,128)S(1)}, u32[]{:S(2)}, u32[]{:S(2)}) collective-permute-start(f32[576,128]{1,0:T(8,128)S(1)} %image_planes.1.b0), channel_id=1, source_target_pairs={{0,3},{1,0},{2,1},{3,2},{4,7},{5,4},{6,5},{7,6},{8,11},{9,8},{10,9... | collective-permute-start | bytes 884744 | tf_op jit(solution)/shard_map/image_y/ppermute | solution.py:37
  76.9 5.9 %collective-permute-start.20 = (f32[288,128]{1,0:T(8,128)S(1)}, f32[288,128]{1,0:T(8,128)S(1)}, u32[]{:S(2)}, u32[]{:S(2)}) collective-permute-start(f32[288,128]{1,0:T(8,128)S(1)} %image_columns.2.p0), channel_id=1, source_target_pairs={{0,32},{1,33},{2,34},{3,35},{4,36},{5,37},{6,38},{7,39},{8,40},{9,... | collective-permute-start | bytes 442376 | tf_op jit(solution)/shard_map/image_columns/ppermute | solution.py:37
  82.9 7.4 %collective-permute-start.22 = (f32[576,128]{1,0:T(8,128)S(1)}, f32[576,128]{1,0:T(8,128)S(1)}, u32[]{:S(2)}, u32[]{:S(2)}) collective-permute-start(f32[576,128]{1,0:T(8,128)S(1)} %collective-permute-done.19.b1), channel_id=1, source_target_pairs={{0,1},{1,2},{2,3},{3,0},{4,5},{5,6},{6,7},{7,4},{8,9},{9,10},{10,1... | collective-permute-start | bytes 884744 | tf_op jit(solution)/shard_map/image_far/ppermute | solution.py:37
  86.6 6.5 %collective-permute-start.25 = (f32[288,128]{1,0:T(8,128)S(1)}, f32[288,128]{1,0:T(8,128)S(1)}, u32[]{:S(2)}, u32[]{:S(2)}) collective-permute-start(f32[288,128]{1,0:T(8,128)S(1)} %image_columns.2.p0), channel_id=1, source_target_pairs={{0,64},{1,65},{2,66},{3,67},{4,68},{5,69},{6,70},{7,71},{8,72},{9,... | collective-permute-start | bytes 442376 | tf_op jit(solution)/shard_map/image_columns/ppermute | solution.py:37
  86.6 7.2 %collective-permute-start.24 = (f32[288,128]{1,0:T(8,128)S(1)}, f32[288,128]{1,0:T(8,128)S(1)}, u32[]{:S(2)}, u32[]{:S(2)}) collective-permute-start(f32[288,128]{1,0:T(8,128)S(1)} %image_columns.2.p0), channel_id=1, source_target_pairs={{0,96},{1,97},{2,98},{3,99},{4,100},{5,101},{6,102},{7,103},{8,104... | collective-permute-start | bytes 442376 | tf_op jit(solution)/shard_map/image_columns/ppermute | solution.py:37
  90.9 3.9 %collective-permute-start.23 = (f32[1152,128]{1,0:T(8,128)S(1)}, f32[1152,128]{1,0:T(8,128)S(1)}, u32[]{:S(2)}, u32[]{:S(2)}) collective-permute-start(f32[1152,128]{1,0:T(8,128)S(1)} %pick.1), channel_id=1, source_target_pairs={{0,16},{1,17},{2,18},{3,19},{4,20},{5,21},{6,22},{7,23},{8,24},{9,... | collective-permute-start | bytes 1769480 | tf_op jit(solution)/shard_map/image_swap/ppermute | solution.py:37
  94.4 7.2 %collective-permute-start.26 = (f32[1152,128]{1,0:T(8,128)S(1)}, f32[1152,128]{1,0:T(8,128)S(1)}, u32[]{:S(2)}, u32[]{:S(2)}) collective-permute-start(f32[1152,128]{1,0:T(8,128)S(1)} %image_columns.3.own), channel_id=1, source_target_pairs={{0,16},{1,17},{2,18},{3,19},{4,20},{5,21},{6,22},{7,23},{8,24},{9,... | collective-permute-start | bytes 1769480 | tf_op jit(solution)/shard_map/image_columns/ppermute | solution.py:37
  96.2 1.4 %collective-permute-start.27 = (f32[128,128]{1,0:T(8,128)S(1)}, f32[128,128]{1,0:T(8,128)S(1)}, u32[]{:S(2)}, u32[]{:S(2)}) collective-permute-start(f32[128,128]{1,0:T(8,128)S(1)} %get-tuple-element.85), channel_id=1, source_target_pairs={{0,16},{1,17},{2,18},{3,19},{4,20},{5,21},{6,22},{7,23},{8,24},{9,... | collective-permute-start | bytes 196616 | tf_op jit(solution)/shard_map/inner/ppermute | solution.py:37
  97.6 10.5 %collective-permute-start.30 = (f32[128,128]{1,0:T(8,128)S(1)}, f32[128,128]{1,0:T(8,128)S(1)}, u32[]{:S(2)}, u32[]{:S(2)}) collective-permute-start(f32[128,128]{1,0:T(8,128)S(1)} %add.14.k0), channel_id=1, source_target_pairs={{0,64},{1,65},{2,66},{3,67},{4,68},{5,69},{6,70},{7,71},{8,72},{9,... | collective-permute-start | bytes 196616 | tf_op jit(solution)/shard_map/inner/ppermute | solution.py:37
  99.7 8.4 %collective-permute-start.29 = (f32[128,128]{1,0:T(8,128)S(1)}, f32[128,128]{1,0:T(8,128)S(1)}, u32[]{:S(2)}, u32[]{:S(2)}) collective-permute-start(f32[128,128]{1,0:T(8,128)S(1)} %add.14.k0), channel_id=1, source_target_pairs={{0,96},{1,97},{2,98},{3,99},{4,100},{5,101},{6,102},{7,103},{8,104... | collective-permute-start | bytes 196616 | tf_op jit(solution)/shard_map/inner/ppermute | solution.py:37
  101.6 6.4 %collective-permute-start.28 = (f32[128,128]{1,0:T(8,128)S(1)}, f32[128,128]{1,0:T(8,128)S(1)}, u32[]{:S(2)}, u32[]{:S(2)}) collective-permute-start(f32[128,128]{1,0:T(8,128)S(1)} %add.14.k0), channel_id=1, source_target_pairs={{0,32},{1,33},{2,34},{3,35},{4,36},{5,37},{6,38},{7,39},{8,40},{9,... | collective-permute-start | bytes 196616 | tf_op jit(solution)/shard_map/inner/ppermute | solution.py:37
